TPU v7x, 256 devices: a whole 4x4x8 slice. The times are simulated.
256 devices in a mesh: ctx: 32 (over y, x, core), tp: 8 (over z).
Axes of the slice: x: 4, y: 4, z: 8, core: 2. Of those that a mesh axis runs over, the one named last changes fastest.
Arguments:
- queries: bfloat16 [8192, 4096], P('ctx', 'tp'), may hold values from -120 to 120
- keys: bfloat16 [8192, 4096], P('ctx', 'tp'), may hold values from -7 to 7
- values: bfloat16 [8192, 4096], P('ctx', 'tp'), may hold values from -7 to 7
- out_weight: bfloat16 [4096, 4096], P(None, 'tp'), may hold values from -0.09375 to 0.09375
- out_grad: bfloat16 [8192, 4096], P('ctx', 'tp'), may hold values from -48 to 48
Outputs:
- mixed: bfloat16 [8192, 4096], P('ctx', 'tp')
- grad_queries: bfloat16 [8192, 4096], P('ctx', 'tp')
- grad_keys: bfloat16 [8192, 4096], P('ctx', 'tp')
- grad_values: bfloat16 [8192, 4096], P('ctx', 'tp')
- grad_weight: float32 [4096, 4096], P('ctx', 'tp')
All inputs are finite; a program needn't handle non-finite values.
Results may differ from a plain program's by a relative error of at most 0.02.
Values may be sent and summed in bfloat16 or wider, within the bound.
No kernel may reach another device: no remote copies, remote signals or barrier semaphores. Data moves between devices by JAX's collectives and lax.ppermute only.
A program may use at most 128 MiB of HBM per device.

v0:
```python
import jax
import jax.numpy as jnp
from jax import lax
from jax.sharding import PartitionSpec as P

HEAD_DIM = 128
BLOCK = 16


grad_scale = 0.015625


def from_partner(block, axis, stride):
    count = lax.axis_size(axis)
    route = []
    for low in range(count):
        high = low | 1 << stride
        if high != low and high < count:
            route += [(low, high), (high, low)]
    return lax.ppermute(block, axis, route)


def pair_mean(x, axis):
    shape = x.shape
    wide = x.astype(jnp.float32).reshape(shape[:axis] + (shape[axis] // 2, 2) + shape[axis + 1 :])
    return (0.5 * jnp.sum(wide, axis=axis + 1)).astype(jnp.bfloat16)


def spread_pairs(grad, axis):
    return 0.5 * jnp.repeat(grad, 2, axis=axis)


def swap_blocks(x, axis):
    shape = x.shape
    split = shape[:axis] + (shape[axis] // (2 * BLOCK), 2, BLOCK) + shape[axis + 1 :]
    return jnp.flip(x.reshape(split), axis + 1).reshape(shape)


def on_device(queries, keys, values, out_weight, out_grad):
    count_rows, local_width = queries.shape
    heads = local_width // HEAD_DIM
    scale = HEAD_DIM ** (-0.5)
    ctx_count = lax.axis_size("ctx")
    rank = lax.axis_index("ctx")
    depth = ctx_count.bit_length() - 1

    def grouped(x, count):
        return x.reshape((count, count_rows // count) + x.shape[1:])

    def blocked(x):
        return x.reshape(2, -1, BLOCK, heads, HEAD_DIM)

    stacked = jnp.stack([keys, values]).reshape(2, count_rows, heads, HEAD_DIM)
    local = [stacked]
    while local[-1].shape[1] > 2 * BLOCK:
        local.append(pair_mean(local[-1], 1))
    top_own = pair_mean(local[-1], 1)
    far = []
    own = top_own
    for level in range(depth):
        partner = from_partner(own, "ctx", level)
        far.append(partner)
        if level + 1 < depth:
            upper = (rank >> level) % 2 == 1
            first = jnp.where(upper, partner, own)
            second = jnp.where(upper, own, partner)
            own = pair_mean(jnp.concatenate([first, second], axis=1), 1)
    entries = (
        [blocked(local[0])]
        + [blocked(swap_blocks(layer, 1)) for layer in local]
        + [blocked(layer) for layer in far]
    )
    query_heads = queries.reshape(count_rows, heads, HEAD_DIM)
    pieces = [
        jnp.einsum(
            "gthe,gkhe->gthk",
            grouped(query_heads, e.shape[1]),
            e[0],
            preferred_element_type=jnp.float32,
        ).reshape(count_rows, heads, BLOCK)
        for e in entries
    ]
    scores = jnp.concatenate(pieces, axis=2) * scale
    top = jnp.max(scores, axis=2, keepdims=True)
    expo = jnp.exp(scores - top)
    prob = expo / jnp.sum(expo, axis=2, keepdims=True)
    weights = prob.astype(jnp.bfloat16)
    out = jnp.zeros((count_rows, heads, HEAD_DIM), jnp.float32)
    for index, e in enumerate(entries):
        part = grouped(weights[:, :, index * BLOCK : (index + 1) * BLOCK], e.shape[1])
        out = out + jnp.einsum(
            "gthk,gkhe->gthe", part, e[1], preferred_element_type=jnp.float32
        ).reshape(count_rows, heads, HEAD_DIM)
    attention = out.astype(jnp.bfloat16).reshape(count_rows, local_width)
    partial_out = jnp.einsum("th,dh->td", attention, out_weight, preferred_element_type=jnp.float32)
    mixed = lax.psum_scatter(
        partial_out.astype(jnp.bfloat16), "tp", scatter_dimension=1, tiled=True
    )
    full_grad = lax.all_gather(out_grad, "tp", axis=1, tiled=True)
    grad_attention = jnp.dot(full_grad, out_weight, preferred_element_type=jnp.float32).astype(
        jnp.bfloat16
    )
    grad_weight = lax.psum_scatter(
        (
            lax.dot_general(
                full_grad, attention, (((0,), (0,)), ((), ())), preferred_element_type=jnp.float32
            )
            * grad_scale
        ).astype(jnp.bfloat16),
        "ctx",
        scatter_dimension=0,
        tiled=True,
    ).astype(jnp.float32)
    grad_heads = grad_attention.reshape(count_rows, heads, HEAD_DIM)
    dprob = jnp.concatenate(
        [
            jnp.einsum(
                "gthe,gkhe->gthk",
                grouped(grad_heads, e.shape[1]),
                e[1],
                preferred_element_type=jnp.float32,
            ).reshape(count_rows, heads, BLOCK)
            for e in entries
        ],
        axis=2,
    )
    delta = jnp.sum(prob * dprob, axis=2, keepdims=True)
    dscore = (prob * (dprob - delta) * scale).astype(jnp.bfloat16)
    grad_query = jnp.zeros((count_rows, heads, HEAD_DIM), jnp.float32)
    direct = []
    for index, e in enumerate(entries):
        count = e.shape[1]
        window = slice(index * BLOCK, (index + 1) * BLOCK)
        dsc = grouped(dscore[:, :, window], count)
        wts = grouped(weights[:, :, window], count)
        grad_query = grad_query + jnp.einsum(
            "gthk,gkhe->gthe", dsc, e[0], preferred_element_type=jnp.float32
        ).reshape(count_rows, heads, HEAD_DIM)
        key_part = jnp.einsum(
            "gthk,gthe->gkhe", dsc, grouped(query_heads, count), preferred_element_type=jnp.float32
        )
        value_part = jnp.einsum(
            "gthk,gthe->gkhe", wts, grouped(grad_heads, count), preferred_element_type=jnp.float32
        )
        direct.append(jnp.stack([key_part, value_part]).reshape(2, count * BLOCK, heads, HEAD_DIM))
    local_count = len(local)
    local_direct = [swap_blocks(direct[1 + level], 1) for level in range(local_count)]
    local_direct[0] = direct[0] + local_direct[0]
    far_grad = [direct[1 + local_count + level] for level in range(depth)]
    carried = None
    for level in reversed(range(depth)):
        outgoing = far_grad[level]
        kept = None
        if carried is not None:
            upper = (rank >> level) % 2 == 1
            spread = spread_pairs(carried, 1)
            first = spread[:, :BLOCK]
            second = spread[:, BLOCK:]
            outgoing = outgoing + jnp.where(upper, first, second)
            kept = jnp.where(upper, second, first)
        back = from_partner(outgoing.astype(jnp.bfloat16), "ctx", level).astype(outgoing.dtype)
        carried = back if kept is None else kept + back
    total = local_direct[local_count - 1] + spread_pairs(carried, 1)
    for level in range(local_count - 1, 0, -1):
        total = local_direct[level - 1] + spread_pairs(total, 1)
    grad_keys = total[0].reshape(count_rows, local_width).astype(jnp.bfloat16)
    grad_values = total[1].reshape(count_rows, local_width).astype(jnp.bfloat16)
    grad_queries = grad_query.reshape(count_rows, local_width).astype(jnp.bfloat16)
    return (mixed, grad_queries, grad_keys, grad_values, grad_weight)


def solution(mesh):
    in_specs = (P("ctx", "tp"), P("ctx", "tp"), P("ctx", "tp"), P(None, "tp"), P("ctx", "tp"))
    out_specs = (P("ctx", "tp"), P("ctx", "tp"), P("ctx", "tp"), P("ctx", "tp"), P("ctx", "tp"))
    return jax.shard_map(
        on_device, mesh=mesh, in_specs=in_specs, out_specs=out_specs, check_vma=False
    )
```

profile of v0, /device:TPU:2, one launch (start us, length us, event | category | flops | bytes accessed | tf_op | source)
XLA Modules:
  0.0 233.0 jit_solution(18293421726966638189)
XLA Ops:
  23.5 2.4 %collective-permute-start.1 = (bf16[2,16,4,128]{3,1,2,0:T(8,128)(2,1)S(1)}, bf16[2,16,4,128]{3,1,2,0:T(8,128)(2,1)S(1)}, u32[]{:S(2)}, u32[]{:S(2)}) collective-permute-start(bf16[2,16,4,128]{3,1,2,0:T(8,128)(2,1)S(1)} %multiply_convert_fusion.7), channel_id=1, source_target_pairs={{0,16},{16,0},{8,24},{24,8},{32,48},{48,32},{40,56},{56,40},{64,80... | collective-permute-start | bytes 98312 | tf_op jit(solution)/shard_map/ppermute | solution.py:20
  30.1 3.6 %collective-permute-done.2 = bf16[2,16,4,128]{3,1,2,0:T(8,128)(2,1)S(1)} collective-permute-done((bf16[2,16,4,128]{3,1,2,0:T(8,128)(2,1)S(1)}, bf16[2,16,4,128]{3,1,2,0:T(8,128)(2,1)S(1)}, u32[]{:S(2)}, u32[]{:S(2)}) %collective-permute-start.2) | collective-permute-done | bytes 32800 | tf_op jit(solution)/shard_map/ppermute | solution.py:20
  35.3 2.6 %collective-permute-done.3 = bf16[2,16,4,128]{3,1,2,0:T(8,128)(2,1)S(1)} collective-permute-done((bf16[2,16,4,128]{3,1,2,0:T(8,128)(2,1)S(1)}, bf16[2,16,4,128]{3,1,2,0:T(8,128)(2,1)S(1)}, u32[]{:S(2)}, u32[]{:S(2)}) %collective-permute-start.3) | collective-permute-done | bytes 32800 | tf_op jit(solution)/shard_map/ppermute | solution.py:20
  38.1 3.0 %collective-permute-start.4 = (bf16[2,16,4,128]{3,1,2,0:T(8,128)(2,1)S(1)}, bf16[2,16,4,128]{3,1,2,0:T(8,128)(2,1)S(1)}, u32[]{:S(2)}, u32[]{:S(2)}) collective-permute-start(bf16[2,16,4,128]{3,1,2,0:T(8,128)(2,1)S(1)} %multiply_convert_fusion.4), channel_id=1, source_target_pairs={{0,128},{128,0},{8,136},{136,8},{16,144},{144,16},{24,152},{152,24... | collective-permute-start | bytes 98312 | tf_op jit(solution)/shard_map/ppermute | solution.py:20
  41.3 2.5 %collective-permute-done.4 = bf16[2,16,4,128]{3,1,2,0:T(8,128)(2,1)S(1)} collective-permute-done((bf16[2,16,4,128]{3,1,2,0:T(8,128)(2,1)S(1)}, bf16[2,16,4,128]{3,1,2,0:T(8,128)(2,1)S(1)}, u32[]{:S(2)}, u32[]{:S(2)}) %collective-permute-start.4) | collective-permute-done | bytes 32800 | tf_op jit(solution)/shard_map/ppermute | solution.py:20
  50.7 2.1 copy.750
  55.3 2.0 copy.748
  61.6 2.0 copy.751
  69.4 2.0 copy.752
  73.3 2.0 copy.753
  75.3 2.6 %fusion.38 = bf16[256,512]{1,0:T(8,128)(2,1)S(1)} fusion(f32[256,512]{1,0:T(8,128)} %copy.753, f32[256,512]{1,0:T(8,128)} %copy.752, f32[256,512]{1,0:T(8,128)} %copy.751, f32[256,512]{1,0:T(8,128)} %copy.750, f32[256,512]{1,0:T(8,128)} %copy.749, f32[32,8,4,128]{3,2,1,0:T(4,128)} %bitcast.639, f32[32,8,4,128]{3,2,1,0:T(4,128)} %bitcast.638, ...), kind=kLoop, calls=%fused_computation.92 | loop fusion | flops 1179648 | bytes 4980736 | tf_op jit(solution)/shard_map/convert_element_type | solution.py:94
  78.0 4.9 %fusion.2 = bf16[4096,512]{0,1:T(8,128)(2,1)} fusion(bf16[256,512]{1,0:T(8,128)(2,1)S(1)} %fusion.38, bf16[256,4096]{1,0:T(8,128)(2,1)} %all-gather.2.cloned.1.call-done), kind=kOutput, calls=%fused_computation.3 | convolution fusion | flops 1077936128 | bytes 6553600 | tf_op jit(solution)/shard_map/dot_general | solution.py:105
  82.9 6.5 %copy.843 = bf16[4096,512]{1,0:T(8,128)(2,1)} copy(bf16[4096,512]{0,1:T(8,128)(2,1)} %fusion.2) | data formatting | bytes 8388608
  89.6 4.9 %convolution_convert_fusion = bf16[256,4096]{1,0:T(8,128)(2,1)} fusion(bf16[256,512]{1,0:T(8,128)(2,1)S(1)} %fusion.38, bf16[4096,512]{1,0:T(8,128)(2,1)} %param.8), kind=kOutput, calls=%fused_computation.4 | convolution fusion | flops 1074790400 | bytes 6553600 | tf_op jit(solution)/shard_map/th,dh->td/dot_general | solution.py:95
  94.5 4.1 %convolution_convert_fusion.1 = bf16[256,512]{1,0:T(8,128)(2,1)S(1)} fusion(bf16[256,4096]{1,0:T(8,128)(2,1)} %all-gather.2.cloned.1.call-done, bf16[4096,512]{1,0:T(8,128)(2,1)} %param.8), kind=kOutput, calls=%fused_computation.27 | convolution fusion | flops 1073872896 | bytes 6553600 | tf_op jit(solution)/shard_map/dot_general | solution.py:100
  101.1 2.0 fusion.63
  110.2 2.1 copy.756
  114.3 2.1 copy.758
  149.9 2.2 copy.782
  165.0 3.2 %fusion.32 = bf16[256,512]{1,0:T(8,128)(2,1)} fusion(f32[256,512]{1,0:T(8,128)} %copy.790, f32[256,512]{1,0:T(8,128)} %copy.789, f32[256,512]{1,0:T(8,128)} %copy.788, f32[256,512]{1,0:T(8,128)S(1)} %copy.787, f32[256,512]{1,0:T(8,128)} %copy.786, f32[32,8,4,128]{3,2,1,0:T(4,128)} %bitcast.636, f32[32,8,4,128]{3,2,1,0:T(4,128)} %bitcast.634, ...), kind=kLoop, calls=%fused_computation.83 | loop fusion | flops 1179648 | bytes 4980736 | tf_op jit(solution)/shard_map/convert_element_type | solution.py:168
  168.9 2.8 %collective-permute-start.5 = (bf16[2,16,4,128]{3,1,2,0:T(8,128)(2,1)S(1)}, bf16[2,16,4,128]{3,1,2,0:T(8,128)(2,1)S(1)}, u32[]{:S(2)}, u32[]{:S(2)}) collective-permute-start(bf16[2,16,4,128]{3,1,2,0:T(8,128)(2,1)S(1)} %maximum_bitcast_fusion.4), channel_id=1, source_target_pairs={{0,128},{128,0},{8,136},{136,8},{16,144},{144,16},{24,152},{152,24... | collective-permute-start | bytes 98312 | tf_op jit(solution)/shard_map/ppermute | solution.py:20
  176.5 2.3 %collective-permute-done.6 = bf16[2,16,4,128]{3,1,2,0:T(8,128)(2,1)S(1)} collective-permute-done((bf16[2,16,4,128]{3,1,2,0:T(8,128)(2,1)S(1)}, bf16[2,16,4,128]{3,1,2,0:T(8,128)(2,1)S(1)}, u32[]{:S(2)}, u32[]{:S(2)}) %collective-permute-start.6) | collective-permute-done | bytes 32800 | tf_op jit(solution)/shard_map/ppermute | solution.py:20
  181.5 2.9 %collective-permute-done.7 = bf16[2,16,4,128]{3,1,2,0:T(8,128)(2,1)S(1)} collective-permute-done((bf16[2,16,4,128]{3,1,2,0:T(8,128)(2,1)S(1)}, bf16[2,16,4,128]{3,1,2,0:T(8,128)(2,1)S(1)}, u32[]{:S(2)}, u32[]{:S(2)}) %collective-permute-start.7) | collective-permute-done | bytes 32800 | tf_op jit(solution)/shard_map/ppermute | solution.py:20
  199.8 26.7 %reduce-scatter.5.cloned.1.call-done = bf16[256,512]{1,0:T(8,128)(2,1)} async-done(((bf16[256,4096]{1,0:T(8,128)(2,1)}), bf16[256,512]{1,0:T(8,128)(2,1)}) %reduce-scatter.5.cloned.1.call-update) | async-done | bytes 262160 | tf_op jit(solution)/shard_map/reduce_scatter | solution.py:96
  (326 shorter events, 124.4 us)
Async XLA Ops:
  7.2 70.8 %all-gather.2.cloned.1.call-start = ((), (), s32[]{:S(2)}) async-start(), calls=%async_computation.3 | async-start | bytes 2359296 | tf_op jit(solution)/shard_map/all_gather | solution.py:99
  10.8 12.4 %collective-permute-start = (bf16[2,16,4,128]{3,1,2,0:T(8,128)(2,1)}, bf16[2,16,4,128]{3,1,2,0:T(8,128)(2,1)S(1)}, u32[]{:S(2)}, u32[]{:S(2)}) collective-permute-start(bf16[2,16,4,128]{3,1,2,0:T(8,128)(2,1)} %fusion.119), channel_id=1, source_target_pairs={{0,8},{8,0},{16,24},{24,16},{32,40},{40,32},{48,56},{56,48},{64,72... | collective-permute-start | bytes 98312 | tf_op jit(solution)/shard_map/ppermute | solution.py:20
  10.9 187.0 %reduce-scatter.7.cloned.1.call-start = ((), (), s32[]{:S(2)}) async-start(), calls=%async_computation.4 | async-start | bytes 4325376
  23.2 29.6 %copy-start.21 = (bf16[1,2,2,16,4,128]{5,3,2,1,4,0:T(8,128)(2,1)}, bf16[1,2,2,16,4,128]{5,3,2,1,4,0:T(8,128)(2,1)S(1)}, u32[]{:S(2)}) copy-start(bf16[1,2,2,16,4,128]{5,3,2,1,4,0:T(8,128)(2,1)S(1)} %slice.260) | copy-start | bytes 196612
  23.3 20.5 %copy-start.30 = (bf16[2,16,4,128]{3,1,2,0:T(8,128)(2,1)}, bf16[2,16,4,128]{3,1,2,0:T(8,128)(2,1)S(1)}, u32[]{:S(2)}) copy-start(bf16[2,16,4,128]{3,1,2,0:T(8,128)(2,1)S(1)} %collective-permute-done) | copy-start | bytes 98308
  23.5 4.4 %collective-permute-start.1 = (bf16[2,16,4,128]{3,1,2,0:T(8,128)(2,1)S(1)}, bf16[2,16,4,128]{3,1,2,0:T(8,128)(2,1)S(1)}, u32[]{:S(2)}, u32[]{:S(2)}) collective-permute-start(bf16[2,16,4,128]{3,1,2,0:T(8,128)(2,1)S(1)} %multiply_convert_fusion.7), channel_id=1, source_target_pairs={{0,16},{16,0},{8,24},{24,8},{32,48},{48,32},{40,56},{56,40},{64,80... | collective-permute-start | bytes 98312 | tf_op jit(solution)/shard_map/ppermute | solution.py:20
  27.9 21.0 %copy-start.32 = (bf16[2,16,4,128]{3,1,2,0:T(8,128)(2,1)}, bf16[2,16,4,128]{3,1,2,0:T(8,128)(2,1)S(1)}, u32[]{:S(2)}) copy-start(bf16[2,16,4,128]{3,1,2,0:T(8,128)(2,1)S(1)} %collective-permute-done.1) | copy-start | bytes 98308
  28.2 5.5 %collective-permute-start.2 = (bf16[2,16,4,128]{3,1,2,0:T(8,128)(2,1)S(1)}, bf16[2,16,4,128]{3,1,2,0:T(8,128)(2,1)S(1)}, u32[]{:S(2)}, u32[]{:S(2)}) collective-permute-start(bf16[2,16,4,128]{3,1,2,0:T(8,128)(2,1)S(1)} %multiply_convert_fusion.6), channel_id=1, source_target_pairs={{0,32},{32,0},{8,40},{40,8},{16,48},{48,16},{24,56},{56,24},{64,96... | collective-permute-start | bytes 98312 | tf_op jit(solution)/shard_map/ppermute | solution.py:20
  33.9 4.0 %collective-permute-start.3 = (bf16[2,16,4,128]{3,1,2,0:T(8,128)(2,1)S(1)}, bf16[2,16,4,128]{3,1,2,0:T(8,128)(2,1)S(1)}, u32[]{:S(2)}, u32[]{:S(2)}) collective-permute-start(bf16[2,16,4,128]{3,1,2,0:T(8,128)(2,1)S(1)} %multiply_convert_fusion.5), channel_id=1, source_target_pairs={{0,64},{64,0},{8,72},{72,8},{16,80},{80,16},{24,88},{88,24},{32,96... | collective-permute-start | bytes 98312 | tf_op jit(solution)/shard_map/ppermute | solution.py:20
  38.1 5.7 %collective-permute-start.4 = (bf16[2,16,4,128]{3,1,2,0:T(8,128)(2,1)S(1)}, bf16[2,16,4,128]{3,1,2,0:T(8,128)(2,1)S(1)}, u32[]{:S(2)}, u32[]{:S(2)}) collective-permute-start(bf16[2,16,4,128]{3,1,2,0:T(8,128)(2,1)S(1)} %multiply_convert_fusion.4), channel_id=1, source_target_pairs={{0,128},{128,0},{8,136},{136,8},{16,144},{144,16},{24,152},{152,24... | collective-permute-start | bytes 98312 | tf_op jit(solution)/shard_map/ppermute | solution.py:20
  57.3 18.0 %copy-start.8 = (f32[16,16,4,128]{3,2,1,0:T(4,128)S(1)}, f32[16,16,4,128]{3,2,1,0:T(4,128)}, u32[]{:S(2)}) copy-start(f32[16,16,4,128]{3,2,1,0:T(4,128)} %copy.736) | copy-start | bytes 1572868
  89.3 137.1 %reduce-scatter.5.cloned.1.call-start = ((), (), s32[]{:S(2)}) async-start(), calls=%async_computation.2 | async-start | bytes 2359296 | tf_op jit(solution)/shard_map/reduce_scatter | solution.py:96
  164.9 15.8 %copy-start.16 = (f32[8,4,128,16]{2,3,1,0:T(8,128)S(1)}, f32[8,4,128,16]{2,3,1,0:T(8,128)}, u32[]{:S(2)}) copy-start(f32[8,4,128,16]{2,3,1,0:T(8,128)} %fusion.79) | copy-start | bytes 786436
  164.9 19.6 %copy-start.40 = (f32[1,1,16,4,128]{4,2,3,0,1:T(8,128)S(1)}, f32[1,1,16,4,128]{4,2,3,0,1:T(8,128)}, u32[]{:S(2)}) copy-start(f32[1,1,16,4,128]{4,2,3,0,1:T(8,128)} %convolution_bitcast_fusion.35) | copy-start | bytes 98308
  164.9 19.6 %copy-start.41 = (f32[1,1,16,4,128]{4,2,3,0,1:T(8,128)S(1)}, f32[1,1,16,4,128]{4,2,3,0,1:T(8,128)}, u32[]{:S(2)}) copy-start(f32[1,1,16,4,128]{4,2,3,0,1:T(8,128)} %convolution_bitcast_fusion.31) | copy-start | bytes 98308
  164.9 21.6 %copy-start.23 = (f32[4,4,128,16]{2,3,1,0:T(8,128)S(1)}, f32[4,4,128,16]{2,3,1,0:T(8,128)}, u32[]{:S(2)}) copy-start(f32[4,4,128,16]{2,3,1,0:T(8,128)} %fusion.76) | copy-start | bytes 393220
  164.9 21.6 %copy-start.24 = (f32[4,4,16,128]{3,2,1,0:T(8,128)S(1)}, f32[4,4,16,128]{3,2,1,0:T(8,128)}, u32[]{:S(2)}) copy-start(f32[4,4,16,128]{3,2,1,0:T(8,128)} %fusion.86) | copy-start | bytes 393220
  164.9 23.7 %copy-start.38 = (f32[1,1,16,4,128]{4,2,3,0,1:T(8,128)S(1)}, f32[1,1,16,4,128]{4,2,3,0,1:T(8,128)}, u32[]{:S(2)}) copy-start(f32[1,1,16,4,128]{4,2,3,0,1:T(8,128)} %convolution_bitcast_fusion.34) | copy-start | bytes 98308
  165.0 23.7 %copy-start.39 = (f32[1,1,16,4,128]{4,2,3,0,1:T(8,128)S(1)}, f32[1,1,16,4,128]{4,2,3,0,1:T(8,128)}, u32[]{:S(2)}) copy-start(f32[1,1,16,4,128]{4,2,3,0,1:T(8,128)} %convolution_bitcast_fusion.30) | copy-start | bytes 98308
  168.9 5.4 %collective-permute-start.5 = (bf16[2,16,4,128]{3,1,2,0:T(8,128)(2,1)S(1)}, bf16[2,16,4,128]{3,1,2,0:T(8,128)(2,1)S(1)}, u32[]{:S(2)}, u32[]{:S(2)}) collective-permute-start(bf16[2,16,4,128]{3,1,2,0:T(8,128)(2,1)S(1)} %maximum_bitcast_fusion.4), channel_id=1, source_target_pairs={{0,128},{128,0},{8,136},{136,8},{16,144},{144,16},{24,152},{152,24... | collective-permute-start | bytes 98312 | tf_op jit(solution)/shard_map/ppermute | solution.py:20
  174.4 4.3 %collective-permute-start.6 = (bf16[2,16,4,128]{3,1,2,0:T(8,128)(2,1)S(1)}, bf16[2,16,4,128]{3,1,2,0:T(8,128)(2,1)S(1)}, u32[]{:S(2)}, u32[]{:S(2)}) collective-permute-start(bf16[2,16,4,128]{3,1,2,0:T(8,128)(2,1)S(1)} %fusion.112), channel_id=1, source_target_pairs={{0,64},{64,0},{8,72},{72,8},{16,80},{80,16},{24,88},{88,24},{32,96... | collective-permute-start | bytes 98312 | tf_op jit(solution)/shard_map/ppermute | solution.py:20
  178.9 5.5 %collective-permute-start.7 = (bf16[2,16,4,128]{3,1,2,0:T(8,128)(2,1)S(1)}, bf16[2,16,4,128]{3,1,2,0:T(8,128)(2,1)S(1)}, u32[]{:S(2)}, u32[]{:S(2)}) collective-permute-start(bf16[2,16,4,128]{3,1,2,0:T(8,128)(2,1)S(1)} %fusion.114), channel_id=1, source_target_pairs={{0,32},{32,0},{8,40},{40,8},{16,48},{48,16},{24,56},{56,24},{64,96... | collective-permute-start | bytes 98312 | tf_op jit(solution)/shard_map/ppermute | solution.py:20
  184.5 4.0 %collective-permute-start.8 = (bf16[2,16,4,128]{3,1,2,0:T(8,128)(2,1)S(1)}, bf16[2,16,4,128]{3,1,2,0:T(8,128)(2,1)S(1)}, u32[]{:S(2)}, u32[]{:S(2)}) collective-permute-start(bf16[2,16,4,128]{3,1,2,0:T(8,128)(2,1)S(1)} %fusion.116), channel_id=1, source_target_pairs={{0,16},{16,0},{8,24},{24,8},{32,48},{48,32},{40,56},{56,40},{64,80... | collective-permute-start | bytes 98312 | tf_op jit(solution)/shard_map/ppermute | solution.py:20
  189.3 4.2 %collective-permute-start.9 = (bf16[2,16,4,128]{3,1,2,0:T(8,128)(2,1)}, bf16[2,16,4,128]{3,1,2,0:T(8,128)(2,1)}, u32[]{:S(2)}, u32[]{:S(2)}) collective-permute-start(bf16[2,16,4,128]{3,1,2,0:T(8,128)(2,1)} %fusion.118), channel_id=1, source_target_pairs={{0,8},{8,0},{16,24},{24,16},{32,40},{40,32},{48,56},{56,48},{64,72... | collective-permute-start | bytes 98312 | tf_op jit(solution)/shard_map/ppermute | solution.py:20
  (37 other events, 316.0 us)
Sparse Core Ops, SparseCore 0:
  11.0 43.9 all-gather.1
  89.5 91.6 reduce-scatter.6
  184.5 41.9 reduce-scatter.4
where the time goes:
time: 236 us; the launch traced here: 233 us
  matrix products  69.5 us (29%)
  local copies, waits for them, and re-layouts  69 us (29%)
  waiting for transfers between devices  46 us (19%)
  starting transfers between devices  17.1 us (7%)
  other arithmetic  16.4 us (7%)
  between operations  15.1 us (6%)
    reduce_scatter x1, waiting for transfers between devices, on_device(): lax.psum_scatter(partial_out.astype(jnp.bfloat16), 'tp', scatter_dimensio...  26.7 us
    ppermute x10, waiting for transfers between devices, from_partner(): return lax.ppermute(block, axis, route)  19.2 us
    ppermute x10, starting transfers between devices, from_partner(): return lax.ppermute(block, axis, route)  16.7 us
    unnamed x111, local copies, waits for them, and re-layouts  16.4 us
    dot_general x10, matrix products, on_device(): jnp.einsum('gthe,gkhe->gthk', grouped(grad_heads, e.shape[1]), e[1], pref...  14.5 us
    dot_general x10, matrix products, on_device(): jnp.einsum('gthk,gkhe->gthe', part, e[1], preferred_element_type=jnp.floa...  12.4 us
    dot_general x10, matrix products, on_device(): jnp.einsum('gthk,gthe->gkhe', wts, grouped(grad_heads, count), preferred_...  10.6 us
    reshape x5, local copies, waits for them, and re-layouts, on_device(): out = out + jnp.einsum('gthk,gkhe->gthe', part, e[1], preferred_element_t...  10.2 us
  transfers between devices with their start and end apart: 13, of which 9 were waited for; matrix products, arithmetic and copies ran while one was open for 59% of the time, Pallas kernels for 0%

commit v1 on v0

v1 whole, which is shorter than its diff:
```python
import functools

import jax
import jax.numpy as jnp
from jax import lax
from jax.experimental import pallas as pl
from jax.experimental.pallas import tpu as pltpu
from jax.sharding import PartitionSpec as P

HEAD_DIM = 128
BLOCK = 16
WIDTH = 512
HEADS = WIDTH // HEAD_DIM
ROWS = 256
HALF = 128
LOCAL_KEYS = 240
FAR = 96
KEYS = LOCAL_KEYS + FAR
GRAD_SCALE = 0.015625
BF = jnp.bfloat16
F32 = jnp.float32
SMALL = pltpu.CompilerParams(vmem_limit_bytes=16 << 20)
LARGE = pltpu.CompilerParams(vmem_limit_bytes=60 << 20)
ANY = pl.BlockSpec(memory_space=pl.ANY)


def dot(a, b, dims=((1,), (0,))):
    return lax.dot_general(a, b, (dims, ((), ())), preferred_element_type=F32)


def grid_of(shape):
    return lax.broadcasted_iota(jnp.int32, shape, 0), lax.broadcasted_iota(jnp.int32, shape, 1)


def matrix(cond, value=1.0):
    return jnp.where(cond, value, 0.0).astype(BF)


def whole(x):
    return pl.BlockSpec(x.shape, lambda i, rank=len(x.shape): (0,) * rank)


def cost(micros):
    return pl.CostEstimate(flops=0, bytes_accessed=int(micros * 3.7e6), transcendentals=0)


def call(kernel, outs, *args, params=SMALL, micros=0.3):
    return pl.pallas_call(
        kernel,
        grid=(1,),
        out_shape=outs,
        in_specs=[whole(a) for a in args],
        out_specs=jax.tree.map(whole, outs),
        compiler_params=params,
        cost_estimate=cost(micros),
    )(*args)


def shaped(shape, dtype=BF):
    return jax.ShapeDtypeStruct(shape, dtype)


def pool_kernel(inputs, low, pack, high):
    for side in range(2):
        cols = slice(side * WIDTH, (side + 1) * WIDTH)
        layer = inputs[:, (side + 1) * WIDTH : (side + 2) * WIDTH]
        at = 0
        rows = ROWS
        while rows > BLOCK:
            i, j = grid_of((rows // 2, rows))
            layer = dot(matrix(j >> 1 == i, 0.5), layer).astype(BF)
            rows //= 2
            if rows > BLOCK:
                low[at : at + rows, cols] = layer
                at += rows
        pack[0:BLOCK, cols] = layer
        i, j = grid_of((BLOCK, BLOCK))
        halve = matrix(j >> 1 == i, 0.5)
        total = jnp.zeros((BLOCK, WIDTH), F32)
        at, rows = 0, BLOCK
        while rows > 1:
            layer = dot(halve, layer).astype(BF)
            rows //= 2
            total += dot(matrix((i - at == j) & (j < rows)), layer)
            at += rows
        top = total.astype(BF)
        pack[BLOCK : 2 * BLOCK, cols] = top
        high[:, cols] = top


def relay_kernel(own, first, x1, x2, x3, out7, out8):
    x = jnp.concatenate([own[...], first[BLOCK:, :], x1[...], x2[...], x3[...]], axis=0)
    i, j = grid_of((BLOCK, 8 * BLOCK))
    out7[...] = dot(matrix(j == (i >> 1) * BLOCK + 12 + (i & 1)), x).astype(BF)
    out8[...] = dot(matrix((j == i * BLOCK + 14) & (i < 8)), x).astype(BF)


def key_columns(inputs, low, far, half, low_cols):
    return jnp.concatenate(
        [
            inputs[half * HALF : (half + 1) * HALF, WIDTH + low_cols.start : WIDTH + low_cols.stop],
            low[half * 64 : (half + 1) * 64, low_cols],
            low[128 + half * 32 : 128 + (half + 1) * 32, low_cols],
            low[192 + (1 - half) * 16 : 192 + (2 - half) * 16, low_cols],
            far[:, low_cols],
        ],
        axis=0,
    )


def visible():
    k, t = grid_of((KEYS, HALF))
    seen = (k < 128) & (k >> 5 == t >> 5)
    seen |= (k >= 128) & (k < 192) & ((k - 128) >> 4 == (t >> 5) ^ 1)
    seen |= (k >= 192) & (k < 224) & ((k - 192) >> 4 == (t >> 6) ^ 1)
    seen |= (k >= 224) & (k < LOCAL_KEYS + 64)
    seen |= (k >= LOCAL_KEYS + 64) & (((k - LOCAL_KEYS) & 15) < 8)
    return seen


def forward_kernel(
    weight, inputs, low, r1, x1, x2, x3, s1, s2, s3, attention, prob, far, shares, held, sems
):
    copies = []
    for n in range(8):
        rows = slice(n * WIDTH, (n + 1) * WIDTH)
        copies.append(pltpu.make_async_copy(weight.at[rows, :], held.at[n], sems.at[n]))
        copies[-1].start()
    x = jnp.concatenate([x1[...], x2[...], x3[...]], axis=0)
    i, j = grid_of((2 * BLOCK, 6 * BLOCK))
    five = (i < BLOCK) & (j == (i >> 3) * BLOCK + (i & 7))
    n = i - BLOCK
    six = (i >= BLOCK) & (j == 2 * BLOCK + (n >> 2) * BLOCK + 8 + (n & 3))
    far[0:16, :] = r1[0:16, :]
    far[16:48, :] = dot(matrix(five | six), x).astype(BF)
    far[48:64, :] = s1[...]
    far[64:80, :] = s2[...]
    far[80:96, :] = s3[...]
    seen = visible()
    scale = HEAD_DIM ** (-0.5)
    for head in range(HEADS):
        cols = slice(head * HEAD_DIM, (head + 1) * HEAD_DIM)
        vcols = slice(WIDTH + head * HEAD_DIM, WIDTH + (head + 1) * HEAD_DIM)
        for half in range(2):
            rows = slice(half * HALF, (half + 1) * HALF)
            kc = key_columns(inputs, low, far, half, cols)
            vc = key_columns(inputs, low, far, half, vcols)
            scores = dot(kc, inputs[rows, cols], ((1,), (1,))) * scale
            scores = jnp.where(seen, scores, -1e30)
            expo = jnp.exp(scores - jnp.max(scores, axis=0, keepdims=True))
            p = expo / jnp.sum(expo, axis=0, keepdims=True)
            prob[head * 2 + half] = p
            attention[rows, cols] = dot(p.astype(BF), vc, ((0,), (0,))).astype(BF)
    att = attention[...]
    for n in range(8):
        copies[n].wait()
        shares[n] = dot(att, held[n], ((1,), (1,))).astype(BF)


def backward_kernel(inputs, low, far, prob, grad, grad_queries, local, direct, m7, m8a, m8b):
    scale = HEAD_DIM ** (-0.5)
    t, j = grid_of((HALF, 112))
    fold = (
        matrix((j < 64) & (t >> 1 == j), 0.5)
        + matrix((j >= 64) & (j < 96) & (t >> 2 == j - 64), 0.25)
        + matrix((j >= 96) & (t >> 3 == j - 96), 0.125)
    )
    for head in range(HEADS):
        cols = slice(head * HEAD_DIM, (head + 1) * HEAD_DIM)
        vcols = slice(WIDTH + head * HEAD_DIM, WIDTH + (head + 1) * HEAD_DIM)
        parts = []
        for half in range(2):
            rows = slice(half * HALF, (half + 1) * HALF)
            kc = key_columns(inputs, low, far, half, cols)
            vc = key_columns(inputs, low, far, half, vcols)
            g = grad[rows, cols]
            p = prob[head * 2 + half]
            dprob = dot(vc, g, ((1,), (1,)))
            delta = jnp.sum(p * dprob, axis=0, keepdims=True)
            dscore = (p * (dprob - delta) * scale).astype(BF)
            grad_queries[rows, cols] = dot(dscore, kc, ((0,), (0,))).astype(BF)
            parts.append((dot(dscore, inputs[rows, cols]), dot(p.astype(BF), g)))
        for side, out_cols in enumerate((cols, vcols)):
            a, b = parts[0][side], parts[1][side]
            for half, (mine, other) in enumerate(((a, b), (b, a))):
                coarse = jnp.concatenate([mine[128:224], other[224:240]], axis=0).astype(BF)
                local[half * HALF : (half + 1) * HALF, out_cols] = mine[0:128] + dot(fold, coarse)
            remote = (a[LOCAL_KEYS:] + b[LOCAL_KEYS:]).astype(BF)
            direct[:, out_cols] = remote[0:48]
            m7[:, out_cols] = remote[48:64]
            m8a[:, out_cols] = remote[64:80]
            m8b[:, out_cols] = remote[80:96]


def relay_back_kernel(direct, t1, t2, t3, pair, u1, u2, u3):
    x = jnp.concatenate([direct[16:48, :], t1[...], t2[...], t3[...]], axis=0)
    n, j = grid_of((8 * BLOCK, 5 * BLOCK))
    m, i = n >> 4, n & 15
    pick = (i < 8) & (m >= 2) & (m < 4) & (j == (m - 2) * 8 + i)
    pick |= (i >= 8) & (i < 12) & (m >= 4) & (j == 16 + (m - 4) * 4 + (i - 8))
    pick |= (i >= 12) & (i < 14) & (j == 32 + 2 * m + (i - 12))
    pick |= (i == 14) & ((j == 48 + m) | (j == 64 + m))
    y = dot(matrix(pick), x).astype(BF)
    pair[...] = y[0:32]
    u1[...] = y[32:64]
    u2[...] = y[64:96]
    u3[...] = y[96:128]


def pair_kernel(direct, pair, v1, v2, v3, own, mate):
    total = pair[...].astype(F32)
    for v in (v1, v2, v3):
        total += v[...].astype(F32)
    own[...] = total[0:16].astype(BF)
    mate[0:16, :] = direct[0:16, :]
    mate[16:32, :] = total[16:32].astype(BF)


def finish_kernel(local, own, came, grad_keys, grad_values):
    x = jnp.concatenate([came[...], own[...]], axis=0)
    t, j = grid_of((ROWS, 3 * BLOCK))
    i = j & 15
    high = j >= BLOCK
    spread = (
        matrix((j < BLOCK) & (t >> 4 == j), 0.5**4)
        + matrix(high & (i < 8) & (t >> 5 == i), 0.5**5)
        + matrix(high & (i >= 8) & (i < 12) & (t >> 6 == i - 8), 0.5**6)
        + matrix(high & (i >= 12) & (i < 14) & (t >> 7 == i - 12), 0.5**7)
        + matrix(high & (i == 14), 0.5**8)
    )
    for side, out in enumerate((grad_keys, grad_values)):
        cols = slice(side * WIDTH, (side + 1) * WIDTH)
        out[...] = (local[:, cols] + dot(spread, x[:, cols])).astype(BF)


def chunk_of(step):
    z = lax.axis_index("tp")
    return lax.rem(z + (8 + step), 8)


def columns_of(step):
    return pl.ds(pl.multiple_of(chunk_of(step) * WIDTH, WIDTH), WIDTH)


OFFSETS = (0, -1, 1, -2, 2, -3, 3, 4)


def product_kernel(*refs):
    blocks, attention, weight = refs[:9], refs[9], refs[10]
    near, away, grad = refs[11:14]
    att_held, held, weight_held, near_held, away_held, sems = refs[14:]
    copies = [pltpu.make_async_copy(attention, att_held, sems.at[0])]
    for k in range(7):
        copies.append(pltpu.make_async_copy(blocks[k], held.at[k], sems.at[1 + k]))
    copies.append(pltpu.make_async_copy(blocks[7], held.at[7, 0:HALF], sems.at[8]))
    copies.append(pltpu.make_async_copy(blocks[8], held.at[7, HALF:ROWS], sems.at[9]))
    for k, offset in enumerate(OFFSETS):
        copies.append(
            pltpu.make_async_copy(weight.at[columns_of(offset), :], weight_held.at[k], sems.at[10 + k])
        )
    for c in copies:
        c.start()
    rank = lax.axis_index("ctx")
    core = rank & 1
    place = rank >> 1
    copies[0].wait()
    att = att_held[...]
    for k, offset in enumerate(OFFSETS):
        copies[1 + k].wait()
        if k == 7:
            copies[9].wait()
        z = chunk_of(offset)
        for side, out in enumerate((near_held, away_held)):
            for pair in range(2):
                at = pl.multiple_of((2 * pair + (core ^ side)) * 128, 128)
                term = (dot(held[k, :, pl.ds(at, 128)], att, ((0,), (0,))) * GRAD_SCALE).astype(BF)
                apart = (2 * z + pair) ^ place
                kx, ky = apart & 3, apart >> 2
                out[0, kx * 4 + ky] = term[:, :256]
                out[1, ky * 4 + kx] = term[:, 256:]
    stores = [
        pltpu.make_async_copy(away_held, away, sems.at[18]),
        pltpu.make_async_copy(near_held, near, sems.at[19]),
    ]
    for c in stores:
        c.start()
    total = jnp.zeros((ROWS, WIDTH), F32)
    for k in range(8):
        copies[10 + k].wait()
        total += dot(held[k], weight_held[k])
    grad[...] = total.astype(BF)
    for c in stores:
        c.wait()


def ctx_exchange(x, dy=0, dx=0, dc=0):
    pairs = []
    for rank in range(32):
        y, xx, c = rank >> 3, (rank >> 1) & 3, rank & 1
        pairs.append((rank, (((y ^ dy) << 2 | (xx ^ dx)) << 1) | (c ^ dc)))
    return lax.ppermute(x, "ctx", pairs)


def shift(x, step):
    return lax.ppermute(x, "tp", [(i, (i + step) % 8) for i in range(8)])


def gather_blocks(x):
    right = left = x
    blocks = [x]
    for _ in range(3):
        right, left = shift(right, 1), shift(left, -1)
        blocks += [right, left]
    return blocks + [shift(right[:HALF], 1), shift(left[HALF:], -1)]


def total_of(*terms):
    return functools.reduce(lambda a, b: a + b, [t.astype(F32) for t in terms])


def together(*xs):
    return lax.optimization_barrier(xs)


def send_blocks(held, count, last):
    moved = [[], []]
    for k in (2, 1, 3):
        for side in range(2):
            step = {"dx" if (side == 0) != last else "dy": k}
            moved[side].append(ctx_exchange(held[side][k * count : (k + 1) * count], **step))
    return moved


def on_device(queries, keys, values, out_weight, out_grad):
    tile = shaped((ROWS, WIDTH))
    half = shaped((HALF, WIDTH))
    pack16, pack32 = shaped((16, 2 * WIDTH)), shaped((32, 2 * WIDTH))

    r1, l1 = shift(out_grad, 1), shift(out_grad, -1)
    inputs = jnp.concatenate([queries, keys, values], axis=1)
    low, pack, high = call(
        pool_kernel, (shaped((224, 2 * WIDTH)), pack32, pack16), inputs, micros=2
    )
    first = ctx_exchange(pack, dc=1)

    both = jnp.concatenate([high, first[BLOCK:]], axis=0)
    r1, l1, both = together(r1, l1, both)
    r2, l2 = shift(r1, 1), shift(l1, -1)
    row = [ctx_exchange(both, dx=k) for k in (1, 2, 3)]

    out7, out8 = call(relay_kernel, (pack16,) * 2, high, first, *row)
    r2, l2, out7, out8 = together(r2, l2, out7, out8)
    r3, l3 = shift(r2, 1), shift(l2, -1)
    column = [ctx_exchange(out7, dy=1), ctx_exchange(out8, dy=2), ctx_exchange(out8, dy=3)]

    r3, l3, *column = together(r3, l3, *column)
    r4, l4 = shift(r3[:HALF], 1), shift(l3[HALF:], -1)
    operands = (inputs, low, first, *row, *column)
    outs = (tile, shaped((2 * HEADS, KEYS, HALF), F32), shaped((FAR, 2 * WIDTH)), shaped((8, ROWS, WIDTH)))
    attention, prob, far, shares = pl.pallas_call(
        forward_kernel,
        grid=(1,),
        out_shape=outs,
        in_specs=[ANY] + [whole(x) for x in operands],
        out_specs=tuple(whole(x) for x in outs),
        scratch_shapes=[pltpu.VMEM((8, WIDTH, WIDTH), BF), pltpu.SemaphoreType.DMA((8,))],
        compiler_params=LARGE,
        cost_estimate=cost(0),
    )(out_weight, *operands)
    mixed = lax.psum_scatter(shares.reshape(8 * ROWS, WIDTH), "tp", scatter_dimension=0, tiled=True)

    blocks = [out_grad, r1, l1, r2, l2, r3, l3, r4, l4]
    parts = shaped((2, 16, 128, 256))
    near, away, grad_attention = pl.pallas_call(
        product_kernel,
        grid=(1,),
        out_shape=(parts, parts, tile),
        in_specs=[ANY] * 11,
        out_specs=(ANY, ANY, whole(tile)),
        scratch_shapes=[
            pltpu.VMEM((ROWS, WIDTH), BF),
            pltpu.VMEM((8, ROWS, WIDTH), BF),
            pltpu.VMEM((8, WIDTH, WIDTH), BF),
            pltpu.VMEM((2, 16, 128, 256), BF),
            pltpu.VMEM((2, 16, 128, 256), BF),
            pltpu.SemaphoreType.DMA((20,)),
        ],
        compiler_params=LARGE,
        cost_estimate=cost(0),
    )(*blocks, attention, out_weight)

    back = ctx_exchange(away, dc=1)
    grad_queries, local, direct, m7, m8a, m8b = call(
        backward_kernel,
        (tile, shaped((ROWS, 2 * WIDTH), F32), shaped((48, 2 * WIDTH))) + (pack16,) * 3,
        inputs, low, far, prob, grad_attention, params=LARGE, micros=0,
    )

    held = [total_of(near[side], back[side]).astype(BF) for side in range(2)]
    direct, m7, m8a, m8b, *held = together(direct, m7, m8a, m8b, *held)
    moved = send_blocks(held, 4, False)
    column = [ctx_exchange(m7, dy=1), ctx_exchange(m8a, dy=2), ctx_exchange(m8b, dy=3)]

    held = [total_of(held[side][:4], *moved[side]).astype(BF) for side in range(2)]
    moved = send_blocks(held, 1, True)
    pair, *sent = call(relay_back_kernel, (pack32,) * 4, direct, *column)
    came = [ctx_exchange(sent[k - 1], dx=k) for k in (1, 2, 3)]

    own, mate = call(pair_kernel, (pack16, pack32), direct, pair, *came)
    came = ctx_exchange(mate, dc=1)
    held = [total_of(held[side][:1], *moved[side]) for side in range(2)]
    grad_weight = jnp.concatenate([h[0] for h in held], axis=1)

    grad_keys, grad_values = call(finish_kernel, (tile,) * 2, local, own, came)
    return mixed, grad_queries, grad_keys, grad_values, grad_weight


def solution(mesh):
    in_specs = (P("ctx", "tp"), P("ctx", "tp"), P("ctx", "tp"), P(None, "tp"), P("ctx", "tp"))
    out_specs = (P("ctx", "tp"),) * 5
    return jax.shard_map(
        on_device, mesh=mesh, in_specs=in_specs, out_specs=out_specs, check_vma=False
    )
```

time: 236 us -> 125 us (0.53)
  the two profiles are of different devices: /device:TPU:2 before, /device:TPU:1 now
where the time goes in v1:
time: 125 us
  starting transfers between devices  53.5 us (43%)
  Pallas kernels  25.4 us (20%)
  waiting for transfers between devices  23 us (18%)
  between operations  14.5 us (12%)
  local copies, waits for them, and re-layouts  4.68 us (4%)
  other arithmetic  3.54 us (3%)
    ppermute x27, starting transfers between devices, ctx_exchange(): return lax.ppermute(x, 'ctx', pairs)  39.9 us
    ppermute x27, waiting for transfers between devices, ctx_exchange(): return lax.ppermute(x, 'ctx', pairs)  22.9 us
    ppermute x8, starting transfers between devices, shift(): return lax.ppermute(x, 'tp', [(i, (i + step) % 8) for i in range(8)])  13.6 us
    pallas_call x6, Pallas kernels, call(): pl.pallas_call(kernel, grid=(1,), out_shape=outs, in_specs=[whole(a) for...  10.6 us
    pallas_call x1, Pallas kernels, on_device(): pl.pallas_call(forward_kernel, grid=(1,), out_shape=outs, in_specs=[ANY]...  8.22 us
    pallas_call x1, Pallas kernels, on_device(): pl.pallas_call(product_kernel, grid=(1,), out_shape=(parts, parts, tile),...  6.6 us
    unnamed x48, local copies, waits for them, and re-layouts  3.55 us
  transfers between devices with their start and end apart: 36, of which 13 were waited for; matrix products, arithmetic and copies ran while one was open for 5% of the time, Pallas kernels for 15%

profile of v1, /device:TPU:1, one launch (start us, length us, event | category | flops | bytes accessed | tf_op | source)
XLA Modules:
  0.0 124.5 jit_solution(5274729004374855401)
XLA Ops:
  7.2 2.5 %collective-permute-start.1 = (bf16[256,512]{1,0:T(8,128)(2,1)}, bf16[256,512]{1,0:T(8,128)(2,1)S(1)}, u32[]{:S(2)}, u32[]{:S(2)}) collective-permute-start(bf16[256,512]{1,0:T(8,128)(2,1)} %refs_0_.1), channel_id=1, source_target_pairs={{0,1},{1,2},{2,3},{3,4},{4,5},{5,6},{6,7},{7,0},{8,9},{9,10},{10,1... | collective-permute-start | bytes 786440 | tf_op jit(solution)/shard_map/ppermute | solution.py:305
  9.8 4.0 %collective-permute-start.2 = (bf16[256,512]{1,0:T(8,128)(2,1)}, bf16[256,512]{1,0:T(8,128)(2,1)S(1)}, u32[]{:S(2)}, u32[]{:S(2)}) collective-permute-start(bf16[256,512]{1,0:T(8,128)(2,1)} %refs_0_.1), channel_id=1, source_target_pairs={{0,7},{1,0},{2,1},{3,2},{4,3},{5,4},{6,5},{7,6},{8,15},{9,8},{10,9... | collective-permute-start | bytes 786440 | tf_op jit(solution)/shard_map/ppermute | solution.py:305
  16.7 2.2 %shard_map.92 = (bf16[224,1024]{1,0:T(8,128)(2,1)S(1)}, bf16[32,1024]{1,0:T(8,128)(2,1)S(1)}, bf16[16,1024]{1,0:T(8,128)(2,1)S(1)}) custom-call(bf16[256,1536]{1,0:T(8,128)(2,1)S(1)} %constant_dynamic-update-slice_fusion.inputs), custom_call_target="tpu_custom_call" | custom-call | bytes 7400000 | tf_op jit(solution)/shard_map/pallas_call | solution.py:48
  21.7 2.7 %collective-permute-start.7 = (bf16[256,512]{1,0:T(8,128)(2,1)S(1)}, bf16[256,512]{1,0:T(8,128)(2,1)S(1)}, u32[]{:S(2)}, u32[]{:S(2)}) collective-permute-start(bf16[256,512]{1,0:T(8,128)(2,1)S(1)} %collective-permute-done.2.refs_2_), channel_id=1, source_target_pairs={{0,7},{1,0},{2,1},{3,2},{4,3},{5,4},{6,5},{7,6},{8,15},{9,8},{10,9... | collective-permute-start | bytes 786440 | tf_op jit(solution)/shard_map/ppermute | solution.py:305
  24.4 2.5 %collective-permute-start.5 = (bf16[32,1024]{1,0:T(8,128)(2,1)S(1)}, bf16[32,1024]{1,0:T(8,128)(2,1)S(1)}, u32[]{:S(2)}, u32[]{:S(2)}) collective-permute-start(bf16[32,1024]{1,0:T(8,128)(2,1)S(1)} %pad_maximum_fusion.1), channel_id=1, source_target_pairs={{0,48},{8,56},{16,32},{24,40},{32,16},{40,24},{48,0},{56,8},{64,11... | collective-permute-start | bytes 196616 | tf_op jit(solution)/shard_map/ppermute | solution.py:301
  29.0 2.5 %collective-permute-done.4.x2 = bf16[32,1024]{1,0:T(8,128)(2,1)S(1)} collective-permute-done((bf16[32,1024]{1,0:T(8,128)(2,1)S(1)}, bf16[32,1024]{1,0:T(8,128)(2,1)S(1)}, u32[]{:S(2)}, u32[]{:S(2)}) %collective-permute-start.4) | collective-permute-done | bytes 65568 | tf_op jit(solution)/shard_map/ppermute | solution.py:301
  31.8 2.7 %collective-permute-start.9 = (bf16[256,512]{1,0:T(8,128)(2,1)S(1)}, bf16[256,512]{1,0:T(8,128)(2,1)S(1)}, u32[]{:S(2)}, u32[]{:S(2)}) collective-permute-start(bf16[256,512]{1,0:T(8,128)(2,1)S(1)} %collective-permute-done.7.refs_4_), channel_id=1, source_target_pairs={{0,7},{1,0},{2,1},{3,2},{4,3},{5,4},{6,5},{7,6},{8,15},{9,8},{10,9... | collective-permute-start | bytes 786440 | tf_op jit(solution)/shard_map/ppermute | solution.py:305
  35.8 1.9 %collective-permute-start.12 = (bf16[16,1024]{1,0:T(8,128)(2,1)S(1)}, bf16[16,1024]{1,0:T(8,128)(2,1)S(1)}, u32[]{:S(2)}, u32[]{:S(2)}) collective-permute-start(bf16[16,1024]{1,0:T(8,128)(2,1)S(1)} %get-tuple-element.60), channel_id=1, source_target_pairs={{0,192},{8,200},{16,208},{24,216},{32,224},{40,232},{48,240},{56,2... | collective-permute-start | bytes 98312 | tf_op jit(solution)/shard_map/ppermute | solution.py:301
  38.4 1.6 %collective-permute-done.12.s3 = bf16[16,1024]{1,0:T(8,128)(2,1)S(1)} collective-permute-done((bf16[16,1024]{1,0:T(8,128)(2,1)S(1)}, bf16[16,1024]{1,0:T(8,128)(2,1)S(1)}, u32[]{:S(2)}, u32[]{:S(2)}) %collective-permute-start.12) | collective-permute-done | bytes 32800 | tf_op jit(solution)/shard_map/ppermute | solution.py:301
  40.1 1.9 %collective-permute-done.11.s2 = bf16[16,1024]{1,0:T(8,128)(2,1)S(1)} collective-permute-done((bf16[16,1024]{1,0:T(8,128)(2,1)S(1)}, bf16[16,1024]{1,0:T(8,128)(2,1)S(1)}, u32[]{:S(2)}, u32[]{:S(2)}) %collective-permute-start.11) | collective-permute-done | bytes 32800 | tf_op jit(solution)/shard_map/ppermute | solution.py:301
  43.6 8.2 %shard_map.94 = (bf16[256,512]{1,0:T(8,128)(2,1)}, f32[8,336,128]{2,1,0:T(8,128)}, bf16[96,1024]{1,0:T(8,128)(2,1)}, bf16[8,256,512]{2,1,0:T(8,128)(2,1)}) custom-call(bf16[4096,512]{1,0:T(8,128)(2,1)} %refs_10_.1, bf16[256,1536]{1,0:T(8,128)(2,1)} %copy-done, bf16[224,1024]{1,0:T(8,128)(2,1)} %copy-done.1, bf16[32,1024]{1,0:T(8,128)(2,1)} %copy-done.3, ...), custom_call_target="tpu_custom_call" | custom-call | tf_op jit(solution)/shard_map/pallas_call | solution.py:360
  52.6 6.6 %shard_map.95 = (bf16[2,16,128,256]{3,2,1,0:T(8,128)(2,1)}, bf16[2,16,128,256]{3,2,1,0:T(8,128)(2,1)}, bf16[256,512]{1,0:T(8,128)(2,1)}) custom-call(bf16[256,512]{1,0:T(8,128)(2,1)} %refs_0_.1, bf16[256,512]{1,0:T(8,128)(2,1)} %copy-done.11, bf16[256,512]{1,0:T(8,128)(2,1)} %copy-done.12, bf16[256,512]{1,0:T(8,128)(2,1)} %copy-done.13, ...), custom_call_target="tpu_custom_call" | custom-call | tf_op jit(solution)/shard_map/pallas_call | solution.py:374
  59.2 5.3 %collective-permute-start.15 = (bf16[2,16,128,256]{3,2,1,0:T(8,128)(2,1)}, bf16[2,16,128,256]{3,2,1,0:T(8,128)(2,1)}, u32[]{:S(2)}, u32[]{:S(2)}) collective-permute-start(bf16[2,16,128,256]{3,2,1,0:T(8,128)(2,1)} %get-tuple-element.78), channel_id=1, source_target_pairs={{0,8},{8,0},{16,24},{24,16},{32,40},{40,32},{48,56},{56,48},{64,72... | collective-permute-start | bytes 6291464 | tf_op jit(solution)/shard_map/ppermute | solution.py:301
  64.5 6.9 %shard_map.96 = (bf16[256,512]{1,0:T(8,128)(2,1)}, f32[256,1024]{1,0:T(8,128)}, bf16[48,1024]{1,0:T(8,128)(2,1)}, bf16[16,1024]{1,0:T(8,128)(2,1)}, bf16[16,1024]{1,0:T(8,128)(2,1)}, /*index=5*/bf16[16,1024]{1,0:T(8,128)(2,1)}) custom-call(bf16[256,1536]{1,0:T(8,128)(2,1)} %copy-done, bf16[224,1024]{1,0:T(8,128)(2,1)} %copy-done.1, ...), custom_call_target="tpu_custom_call" | custom-call | tf_op jit(solution)/shard_map/pallas_call | solution.py:48
  71.5 2.5 %fusion.1 = (bf16[16,128,256]{2,1,0:T(8,128)(2,1)S(1)}, bf16[16,128,256]{2,1,0:T(8,128)(2,1)S(1)}) fusion(bf16[2,16,128,256]{3,2,1,0:T(8,128)(2,1)} %collective-permute-done.15, bf16[2,16,128,256]{3,2,1,0:T(8,128)(2,1)S(1)} %copy-done.8), kind=kLoop, calls=%fused_computation.3 | loop fusion | flops 4194304 | bytes 6291456 | tf_op jit(solution)/shard_map/convert_element_type | solution.py:399
  74.3 1.5 %collective-permute-start.17 = (bf16[16,1024]{1,0:T(8,128)(2,1)S(1)}, bf16[16,1024]{1,0:T(8,128)(2,1)S(1)}, u32[]{:S(2)}, u32[]{:S(2)}) collective-permute-start(bf16[16,1024]{1,0:T(8,128)(2,1)S(1)} %copy-done.21), channel_id=1, source_target_pairs={{0,128},{8,136},{16,144},{24,152},{32,160},{40,168},{48,176},{56,1... | collective-permute-start | bytes 98312 | tf_op jit(solution)/shard_map/ppermute | solution.py:301
  75.9 2.1 %collective-permute-start.18 = (bf16[16,1024]{1,0:T(8,128)(2,1)S(1)}, bf16[16,1024]{1,0:T(8,128)(2,1)S(1)}, u32[]{:S(2)}, u32[]{:S(2)}) collective-permute-start(bf16[16,1024]{1,0:T(8,128)(2,1)S(1)} %copy-done.20), channel_id=1, source_target_pairs={{0,192},{8,200},{16,208},{24,216},{32,224},{40,232},{48,240},{56,2... | collective-permute-start | bytes 98312 | tf_op jit(solution)/shard_map/ppermute | solution.py:301
  80.5 2.3 %collective-permute-start.20 = (bf16[32,1024]{1,0:T(8,128)(2,1)S(1)}, bf16[32,1024]{1,0:T(8,128)(2,1)S(1)}, u32[]{:S(2)}, u32[]{:S(2)}) collective-permute-start(bf16[32,1024]{1,0:T(8,128)(2,1)S(1)} %get-tuple-element.85), channel_id=1, source_target_pairs={{0,32},{8,40},{16,48},{24,56},{32,0},{40,8},{48,16},{56,24},{64,96... | collective-permute-start | bytes 196616 | tf_op jit(solution)/shard_map/ppermute | solution.py:301
  88.3 5.9 %collective-permute-start.22 = (bf16[32,1024]{1,0:T(8,128)(2,1)S(1)}, bf16[32,1024]{1,0:T(8,128)(2,1)S(1)}, u32[]{:S(2)}, u32[]{:S(2)}) collective-permute-start(bf16[32,1024]{1,0:T(8,128)(2,1)S(1)} %get-tuple-element.88), channel_id=1, source_target_pairs={{0,8},{8,0},{16,24},{24,16},{32,40},{40,32},{48,56},{56,48},{64,72... | collective-permute-start | bytes 196616 | tf_op jit(solution)/shard_map/ppermute | solution.py:301
  94.3 1.6 %collective-permute-start.29 = (bf16[4,128,256]{2,1,0:T(8,128)(2,1)S(1)}, bf16[4,128,256]{2,1,0:T(8,128)(2,1)S(1)}, u32[]{:S(2)}, u32[]{:S(2)}) collective-permute-start(bf16[4,128,256]{2,1,0:T(8,128)(2,1)S(1)} %get-tuple-element.98), channel_id=1, source_target_pairs={{0,128},{8,136},{16,144},{24,152},{32,160},{40,168},{48,176},{56,1... | collective-permute-start | bytes 786440 | tf_op jit(solution)/shard_map/ppermute | solution.py:301
  101.1 1.6 %collective-permute-start.28 = (bf16[1,128,256]{2,1,0:T(8,128)(2,1)S(1)}, bf16[1,128,256]{2,1,0:T(8,128)(2,1)S(1)}, u32[]{:S(2)}, u32[]{:S(2)}) collective-permute-start(bf16[1,128,256]{2,1,0:T(8,128)(2,1)S(1)} %get-tuple-element.102), channel_id=1, source_target_pairs={{0,192},{8,200},{16,208},{24,216},{32,224},{40,232},{48,240},{56,2... | collective-permute-start | bytes 196616 | tf_op jit(solution)/shard_map/ppermute | solution.py:301
  104.5 5.6 %collective-permute-done.31 = bf16[4,128,256]{2,1,0:T(8,128)(2,1)S(1)} collective-permute-done((bf16[4,128,256]{2,1,0:T(8,128)(2,1)S(1)}, bf16[4,128,256]{2,1,0:T(8,128)(2,1)S(1)}, u32[]{:S(2)}, u32[]{:S(2)}) %collective-permute-start.31) | collective-permute-done | bytes 262176 | tf_op jit(solution)/shard_map/ppermute | solution.py:301
  110.3 3.2 %collective-permute-start.34 = (bf16[1,128,256]{2,1,0:T(8,128)(2,1)S(1)}, bf16[1,128,256]{2,1,0:T(8,128)(2,1)S(1)}, u32[]{:S(2)}, u32[]{:S(2)}) collective-permute-start(bf16[1,128,256]{2,1,0:T(8,128)(2,1)S(1)} %get-tuple-element.105), channel_id=1, source_target_pairs={{0,48},{8,56},{16,32},{24,40},{32,16},{40,24},{48,0},{56,8},{64,11... | collective-permute-start | bytes 196616 | tf_op jit(solution)/shard_map/ppermute | solution.py:301
  115.0 1.9 %collective-permute-done.34 = bf16[1,128,256]{2,1,0:T(8,128)(2,1)S(1)} collective-permute-done((bf16[1,128,256]{2,1,0:T(8,128)(2,1)S(1)}, bf16[1,128,256]{2,1,0:T(8,128)(2,1)S(1)}, u32[]{:S(2)}, u32[]{:S(2)}) %collective-permute-start.34) | collective-permute-done | bytes 65568 | tf_op jit(solution)/shard_map/ppermute | solution.py:301
  (120 shorter events, 30.4 us)
Async XLA Ops:
  7.2 110.5 %reduce-scatter.2.cloned.1.call-start = ((), (), s32[]{:S(2)}) async-start(), calls=%async_computation.1 | async-start | bytes 2359296 | tf_op jit(solution)/shard_map/reduce_scatter | solution.py:370
  7.2 14.4 %collective-permute-start.1 = (bf16[256,512]{1,0:T(8,128)(2,1)}, bf16[256,512]{1,0:T(8,128)(2,1)S(1)}, u32[]{:S(2)}, u32[]{:S(2)}) collective-permute-start(bf16[256,512]{1,0:T(8,128)(2,1)} %refs_0_.1), channel_id=1, source_target_pairs={{0,1},{1,2},{2,3},{3,4},{4,5},{5,6},{6,7},{7,0},{8,9},{9,10},{10,1... | collective-permute-start | bytes 786440 | tf_op jit(solution)/shard_map/ppermute | solution.py:305
  9.8 11.9 %collective-permute-start.2 = (bf16[256,512]{1,0:T(8,128)(2,1)}, bf16[256,512]{1,0:T(8,128)(2,1)S(1)}, u32[]{:S(2)}, u32[]{:S(2)}) collective-permute-start(bf16[256,512]{1,0:T(8,128)(2,1)} %refs_0_.1), channel_id=1, source_target_pairs={{0,7},{1,0},{2,1},{3,2},{4,3},{5,4},{6,5},{7,6},{8,15},{9,8},{10,9... | collective-permute-start | bytes 786440 | tf_op jit(solution)/shard_map/ppermute | solution.py:305
  21.7 10.0 %collective-permute-start.6 = (bf16[256,512]{1,0:T(8,128)(2,1)S(1)}, bf16[256,512]{1,0:T(8,128)(2,1)S(1)}, u32[]{:S(2)}, u32[]{:S(2)}) collective-permute-start(bf16[256,512]{1,0:T(8,128)(2,1)S(1)} %collective-permute-done.1.refs_1_), channel_id=1, source_target_pairs={{0,1},{1,2},{2,3},{3,4},{4,5},{5,6},{6,7},{7,0},{8,9},{9,10},{10,1... | collective-permute-start | bytes 786440 | tf_op jit(solution)/shard_map/ppermute | solution.py:305
  21.7 10.0 %collective-permute-start.7 = (bf16[256,512]{1,0:T(8,128)(2,1)S(1)}, bf16[256,512]{1,0:T(8,128)(2,1)S(1)}, u32[]{:S(2)}, u32[]{:S(2)}) collective-permute-start(bf16[256,512]{1,0:T(8,128)(2,1)S(1)} %collective-permute-done.2.refs_2_), channel_id=1, source_target_pairs={{0,7},{1,0},{2,1},{3,2},{4,3},{5,4},{6,5},{7,6},{8,15},{9,8},{10,9... | collective-permute-start | bytes 786440 | tf_op jit(solution)/shard_map/ppermute | solution.py:305
  31.7 10.2 %collective-permute-start.8 = (bf16[256,512]{1,0:T(8,128)(2,1)S(1)}, bf16[256,512]{1,0:T(8,128)(2,1)S(1)}, u32[]{:S(2)}, u32[]{:S(2)}) collective-permute-start(bf16[256,512]{1,0:T(8,128)(2,1)S(1)} %collective-permute-done.6.refs_3_), channel_id=1, source_target_pairs={{0,1},{1,2},{2,3},{3,4},{4,5},{5,6},{6,7},{7,0},{8,9},{9,10},{10,1... | collective-permute-start | bytes 786440 | tf_op jit(solution)/shard_map/ppermute | solution.py:305
  31.8 10.1 %collective-permute-start.9 = (bf16[256,512]{1,0:T(8,128)(2,1)S(1)}, bf16[256,512]{1,0:T(8,128)(2,1)S(1)}, u32[]{:S(2)}, u32[]{:S(2)}) collective-permute-start(bf16[256,512]{1,0:T(8,128)(2,1)S(1)} %collective-permute-done.7.refs_4_), channel_id=1, source_target_pairs={{0,7},{1,0},{2,1},{3,2},{4,3},{5,4},{6,5},{7,6},{8,15},{9,8},{10,9... | collective-permute-start | bytes 786440 | tf_op jit(solution)/shard_map/ppermute | solution.py:305
  42.0 9.9 %collective-permute-start.14 = (bf16[128,512]{1,0:T(8,128)(2,1)S(1)}, bf16[128,512]{1,0:T(8,128)(2,1)S(1)}, u32[]{:S(2)}, u32[]{:S(2)}) collective-permute-start(bf16[128,512]{1,0:T(8,128)(2,1)S(1)} %slice.71), channel_id=1, source_target_pairs={{0,7},{1,0},{2,1},{3,2},{4,3},{5,4},{6,5},{7,6},{8,15},{9,8},{10,9... | collective-permute-start | bytes 393224 | tf_op jit(solution)/shard_map/ppermute | solution.py:305
  42.1 9.8 %collective-permute-start.13 = (bf16[128,512]{1,0:T(8,128)(2,1)S(1)}, bf16[128,512]{1,0:T(8,128)(2,1)S(1)}, u32[]{:S(2)}, u32[]{:S(2)}) collective-permute-start(bf16[128,512]{1,0:T(8,128)(2,1)S(1)} %slice.70), channel_id=1, source_target_pairs={{0,1},{1,2},{2,3},{3,4},{4,5},{5,6},{6,7},{7,0},{8,9},{9,10},{10,1... | collective-permute-start | bytes 393224 | tf_op jit(solution)/shard_map/ppermute | solution.py:305
  59.2 12.2 %collective-permute-start.15 = (bf16[2,16,128,256]{3,2,1,0:T(8,128)(2,1)}, bf16[2,16,128,256]{3,2,1,0:T(8,128)(2,1)}, u32[]{:S(2)}, u32[]{:S(2)}) collective-permute-start(bf16[2,16,128,256]{3,2,1,0:T(8,128)(2,1)} %get-tuple-element.78), channel_id=1, source_target_pairs={{0,8},{8,0},{16,24},{24,16},{32,40},{40,32},{48,56},{56,48},{64,72... | collective-permute-start | bytes 6291464 | tf_op jit(solution)/shard_map/ppermute | solution.py:301
  80.1 5.7 %collective-permute-start.19 = (bf16[32,1024]{1,0:T(8,128)(2,1)S(1)}, bf16[32,1024]{1,0:T(8,128)(2,1)S(1)}, u32[]{:S(2)}, u32[]{:S(2)}) collective-permute-start(bf16[32,1024]{1,0:T(8,128)(2,1)S(1)} %get-tuple-element.84), channel_id=1, source_target_pairs={{0,16},{8,24},{16,0},{24,8},{32,48},{40,56},{48,32},{56,40},{64,80... | collective-permute-start | bytes 196616 | tf_op jit(solution)/shard_map/ppermute | solution.py:301
  80.5 6.3 %collective-permute-start.20 = (bf16[32,1024]{1,0:T(8,128)(2,1)S(1)}, bf16[32,1024]{1,0:T(8,128)(2,1)S(1)}, u32[]{:S(2)}, u32[]{:S(2)}) collective-permute-start(bf16[32,1024]{1,0:T(8,128)(2,1)S(1)} %get-tuple-element.85), channel_id=1, source_target_pairs={{0,32},{8,40},{16,48},{24,56},{32,0},{40,8},{48,16},{56,24},{64,96... | collective-permute-start | bytes 196616 | tf_op jit(solution)/shard_map/ppermute | solution.py:301
  82.9 5.4 %collective-permute-start.21 = (bf16[32,1024]{1,0:T(8,128)(2,1)S(1)}, bf16[32,1024]{1,0:T(8,128)(2,1)S(1)}, u32[]{:S(2)}, u32[]{:S(2)}) collective-permute-start(bf16[32,1024]{1,0:T(8,128)(2,1)S(1)} %get-tuple-element.86), channel_id=1, source_target_pairs={{0,48},{8,56},{16,32},{24,40},{32,16},{40,24},{48,0},{56,8},{64,11... | collective-permute-start | bytes 196616 | tf_op jit(solution)/shard_map/ppermute | solution.py:301
  84.1 14.4 %collective-permute-start.23 = (bf16[4,128,256]{2,1,0:T(8,128)(2,1)S(1)}, bf16[4,128,256]{2,1,0:T(8,128)(2,1)S(1)}, u32[]{:S(2)}, u32[]{:S(2)}) collective-permute-start(bf16[4,128,256]{2,1,0:T(8,128)(2,1)S(1)} %get-tuple-element.95), channel_id=1, source_target_pairs={{0,32},{8,40},{16,48},{24,56},{32,0},{40,8},{48,16},{56,24},{64,96... | collective-permute-start | bytes 786440 | tf_op jit(solution)/shard_map/ppermute | solution.py:301
  85.1 14.5 %collective-permute-start.25 = (bf16[4,128,256]{2,1,0:T(8,128)(2,1)S(1)}, bf16[4,128,256]{2,1,0:T(8,128)(2,1)S(1)}, u32[]{:S(2)}, u32[]{:S(2)}) collective-permute-start(bf16[4,128,256]{2,1,0:T(8,128)(2,1)S(1)} %get-tuple-element.96), channel_id=1, source_target_pairs={{0,48},{8,56},{16,32},{24,40},{32,16},{40,24},{48,0},{56,8},{64,11... | collective-permute-start | bytes 786440 | tf_op jit(solution)/shard_map/ppermute | solution.py:301
  85.8 13.8 %collective-permute-start.24 = (bf16[4,128,256]{2,1,0:T(8,128)(2,1)S(1)}, bf16[4,128,256]{2,1,0:T(8,128)(2,1)S(1)}, u32[]{:S(2)}, u32[]{:S(2)}) collective-permute-start(bf16[4,128,256]{2,1,0:T(8,128)(2,1)S(1)} %get-tuple-element.97), channel_id=1, source_target_pairs={{0,16},{8,24},{16,0},{24,8},{32,48},{40,56},{48,32},{56,40},{64,80... | collective-permute-start | bytes 786440 | tf_op jit(solution)/shard_map/ppermute | solution.py:301
  88.3 7.6 %collective-permute-start.22 = (bf16[32,1024]{1,0:T(8,128)(2,1)S(1)}, bf16[32,1024]{1,0:T(8,128)(2,1)S(1)}, u32[]{:S(2)}, u32[]{:S(2)}) collective-permute-start(bf16[32,1024]{1,0:T(8,128)(2,1)S(1)} %get-tuple-element.88), channel_id=1, source_target_pairs={{0,8},{8,0},{16,24},{24,16},{32,40},{40,32},{48,56},{56,48},{64,72... | collective-permute-start | bytes 196616 | tf_op jit(solution)/shard_map/ppermute | solution.py:301
  94.3 9.6 %collective-permute-start.29 = (bf16[4,128,256]{2,1,0:T(8,128)(2,1)S(1)}, bf16[4,128,256]{2,1,0:T(8,128)(2,1)S(1)}, u32[]{:S(2)}, u32[]{:S(2)}) collective-permute-start(bf16[4,128,256]{2,1,0:T(8,128)(2,1)S(1)} %get-tuple-element.98), channel_id=1, source_target_pairs={{0,128},{8,136},{16,144},{24,152},{32,160},{40,168},{48,176},{56,1... | collective-permute-start | bytes 786440 | tf_op jit(solution)/shard_map/ppermute | solution.py:301
  95.9 14.1 %collective-permute-start.31 = (bf16[4,128,256]{2,1,0:T(8,128)(2,1)S(1)}, bf16[4,128,256]{2,1,0:T(8,128)(2,1)S(1)}, u32[]{:S(2)}, u32[]{:S(2)}) collective-permute-start(bf16[4,128,256]{2,1,0:T(8,128)(2,1)S(1)} %get-tuple-element.99), channel_id=1, source_target_pairs={{0,192},{8,200},{16,208},{24,216},{32,224},{40,232},{48,240},{56,2... | collective-permute-start | bytes 786440 | tf_op jit(solution)/shard_map/ppermute | solution.py:301
  98.5 11.6 %collective-permute-start.30 = (bf16[4,128,256]{2,1,0:T(8,128)(2,1)S(1)}, bf16[4,128,256]{2,1,0:T(8,128)(2,1)S(1)}, u32[]{:S(2)}, u32[]{:S(2)}) collective-permute-start(bf16[4,128,256]{2,1,0:T(8,128)(2,1)S(1)} %get-tuple-element.100), channel_id=1, source_target_pairs={{0,64},{8,72},{16,80},{24,88},{32,96},{40,104},{48,112},{56,120},{... | collective-permute-start | bytes 786440 | tf_op jit(solution)/shard_map/ppermute | solution.py:301
  99.8 13.7 %collective-permute-start.26 = (bf16[1,128,256]{2,1,0:T(8,128)(2,1)S(1)}, bf16[1,128,256]{2,1,0:T(8,128)(2,1)S(1)}, u32[]{:S(2)}, u32[]{:S(2)}) collective-permute-start(bf16[1,128,256]{2,1,0:T(8,128)(2,1)S(1)} %get-tuple-element.101), channel_id=1, source_target_pairs={{0,128},{8,136},{16,144},{24,152},{32,160},{40,168},{48,176},{56,1... | collective-permute-start | bytes 196616 | tf_op jit(solution)/shard_map/ppermute | solution.py:301
  101.1 12.4 %collective-permute-start.28 = (bf16[1,128,256]{2,1,0:T(8,128)(2,1)S(1)}, bf16[1,128,256]{2,1,0:T(8,128)(2,1)S(1)}, u32[]{:S(2)}, u32[]{:S(2)}) collective-permute-start(bf16[1,128,256]{2,1,0:T(8,128)(2,1)S(1)} %get-tuple-element.102), channel_id=1, source_target_pairs={{0,192},{8,200},{16,208},{24,216},{32,224},{40,232},{48,240},{56,2... | collective-permute-start | bytes 196616 | tf_op jit(solution)/shard_map/ppermute | solution.py:301
  103.9 9.6 %collective-permute-start.27 = (bf16[1,128,256]{2,1,0:T(8,128)(2,1)S(1)}, bf16[1,128,256]{2,1,0:T(8,128)(2,1)S(1)}, u32[]{:S(2)}, u32[]{:S(2)}) collective-permute-start(bf16[1,128,256]{2,1,0:T(8,128)(2,1)S(1)} %get-tuple-element.103), channel_id=1, source_target_pairs={{0,64},{8,72},{16,80},{24,88},{32,96},{40,104},{48,112},{56,120},{... | collective-permute-start | bytes 196616 | tf_op jit(solution)/shard_map/ppermute | solution.py:301
  110.3 6.6 %collective-permute-start.34 = (bf16[1,128,256]{2,1,0:T(8,128)(2,1)S(1)}, bf16[1,128,256]{2,1,0:T(8,128)(2,1)S(1)}, u32[]{:S(2)}, u32[]{:S(2)}) collective-permute-start(bf16[1,128,256]{2,1,0:T(8,128)(2,1)S(1)} %get-tuple-element.105), channel_id=1, source_target_pairs={{0,48},{8,56},{16,32},{24,40},{32,16},{40,24},{48,0},{56,8},{64,11... | collective-permute-start | bytes 196616 | tf_op jit(solution)/shard_map/ppermute | solution.py:301
  (35 other events, 317.3 us)
Sparse Core Ops, SparseCore 0:
  64.6 34.4 reduce-scatter.1

commit v2 on v1

--- a/solution.py
+++ b/solution.py
@@ -1,5 +1,3 @@
-import functools
-
 import jax
 import jax.numpy as jnp
 from jax import lax
@@ -60,10 +58,10 @@
     return jax.ShapeDtypeStruct(shape, dtype)
 
 
-def pool_kernel(inputs, low, pack, high):
-    for side in range(2):
+def pool_kernel(keys, values, low, pack, high):
+    for side, src in enumerate((keys, values)):
         cols = slice(side * WIDTH, (side + 1) * WIDTH)
-        layer = inputs[:, (side + 1) * WIDTH : (side + 2) * WIDTH]
+        layer = src[...]
         at = 0
         rows = ROWS
         while rows > BLOCK:
@@ -95,10 +93,10 @@
     out8[...] = dot(matrix((j == i * BLOCK + 14) & (i < 8)), x).astype(BF)
 
 
-def key_columns(inputs, low, far, half, low_cols):
+def key_columns(own, low, far, half, cols, low_cols):
     return jnp.concatenate(
         [
-            inputs[half * HALF : (half + 1) * HALF, WIDTH + low_cols.start : WIDTH + low_cols.stop],
+            own[half * HALF : (half + 1) * HALF, cols],
             low[half * 64 : (half + 1) * 64, low_cols],
             low[128 + half * 32 : 128 + (half + 1) * 32, low_cols],
             low[192 + (1 - half) * 16 : 192 + (2 - half) * 16, low_cols],
@@ -119,7 +117,8 @@
 
 
 def forward_kernel(
-    weight, inputs, low, r1, x1, x2, x3, s1, s2, s3, attention, prob, far, shares, held, sems
+    weight, queries, keys, values, low, r1, x1, x2, x3, s1, s2, s3,
+    attention, prob_out, far, shares_out, held, prob, shares, sems
 ):
     copies = []
     for n in range(8):
@@ -143,21 +142,30 @@
         vcols = slice(WIDTH + head * HEAD_DIM, WIDTH + (head + 1) * HEAD_DIM)
         for half in range(2):
             rows = slice(half * HALF, (half + 1) * HALF)
-            kc = key_columns(inputs, low, far, half, cols)
-            vc = key_columns(inputs, low, far, half, vcols)
-            scores = dot(kc, inputs[rows, cols], ((1,), (1,))) * scale
+            kc = key_columns(keys, low, far, half, cols, cols)
+            vc = key_columns(values, low, far, half, cols, vcols)
+            scores = dot(kc, queries[rows, cols], ((1,), (1,))) * scale
             scores = jnp.where(seen, scores, -1e30)
             expo = jnp.exp(scores - jnp.max(scores, axis=0, keepdims=True))
             p = expo / jnp.sum(expo, axis=0, keepdims=True)
             prob[head * 2 + half] = p
             attention[rows, cols] = dot(p.astype(BF), vc, ((0,), (0,))).astype(BF)
+    stores = [pltpu.make_async_copy(prob, prob_out, sems.at[8])]
+    stores[0].start()
     att = attention[...]
     for n in range(8):
         copies[n].wait()
         shares[n] = dot(att, held[n], ((1,), (1,))).astype(BF)
-
-
-def backward_kernel(inputs, low, far, prob, grad, grad_queries, local, direct, m7, m8a, m8b):
+        stores.append(pltpu.make_async_copy(shares.at[n], shares_out.at[n], sems.at[9 + n]))
+        stores[-1].start()
+    for c in stores:
+        c.wait()
+
+
+REMOTE_COLUMNS = [side * WIDTH + head * HEAD_DIM for head in range(HEADS) for side in range(2)]
+
+
+def backward_kernel(queries, keys, values, low, far, prob, grad, grad_queries, local, fine, top, first):
     scale = HEAD_DIM ** (-0.5)
     t, j = grid_of((HALF, 112))
     fold = (
@@ -165,59 +173,119 @@
         + matrix((j >= 64) & (j < 96) & (t >> 2 == j - 64), 0.25)
         + matrix((j >= 96) & (t >> 3 == j - 96), 0.125)
     )
+    remotes = []
     for head in range(HEADS):
         cols = slice(head * HEAD_DIM, (head + 1) * HEAD_DIM)
         vcols = slice(WIDTH + head * HEAD_DIM, WIDTH + (head + 1) * HEAD_DIM)
         parts = []
         for half in range(2):
             rows = slice(half * HALF, (half + 1) * HALF)
-            kc = key_columns(inputs, low, far, half, cols)
-            vc = key_columns(inputs, low, far, half, vcols)
+            kc = key_columns(keys, low, far, half, cols, cols)
+            vc = key_columns(values, low, far, half, cols, vcols)
             g = grad[rows, cols]
             p = prob[head * 2 + half]
             dprob = dot(vc, g, ((1,), (1,)))
             delta = jnp.sum(p * dprob, axis=0, keepdims=True)
             dscore = (p * (dprob - delta) * scale).astype(BF)
             grad_queries[rows, cols] = dot(dscore, kc, ((0,), (0,))).astype(BF)
-            parts.append((dot(dscore, inputs[rows, cols]), dot(p.astype(BF), g)))
+            parts.append((dot(dscore, queries[rows, cols]), dot(p.astype(BF), g)))
         for side, out_cols in enumerate((cols, vcols)):
             a, b = parts[0][side], parts[1][side]
             for half, (mine, other) in enumerate(((a, b), (b, a))):
                 coarse = jnp.concatenate([mine[128:224], other[224:240]], axis=0).astype(BF)
                 local[half * HALF : (half + 1) * HALF, out_cols] = mine[0:128] + dot(fold, coarse)
             remote = (a[LOCAL_KEYS:] + b[LOCAL_KEYS:]).astype(BF)
-            direct[:, out_cols] = remote[0:48]
-            m7[:, out_cols] = remote[48:64]
-            m8a[:, out_cols] = remote[64:80]
-            m8b[:, out_cols] = remote[80:96]
-
-
-def relay_back_kernel(direct, t1, t2, t3, pair, u1, u2, u3):
-    x = jnp.concatenate([direct[16:48, :], t1[...], t2[...], t3[...]], axis=0)
-    n, j = grid_of((8 * BLOCK, 5 * BLOCK))
-    m, i = n >> 4, n & 15
-    pick = (i < 8) & (m >= 2) & (m < 4) & (j == (m - 2) * 8 + i)
-    pick |= (i >= 8) & (i < 12) & (m >= 4) & (j == 16 + (m - 4) * 4 + (i - 8))
-    pick |= (i >= 12) & (i < 14) & (j == 32 + 2 * m + (i - 12))
-    pick |= (i == 14) & ((j == 48 + m) | (j == 64 + m))
-    y = dot(matrix(pick), x).astype(BF)
-    pair[...] = y[0:32]
-    u1[...] = y[32:64]
-    u2[...] = y[64:96]
-    u3[...] = y[96:128]
-
-
-def pair_kernel(direct, pair, v1, v2, v3, own, mate):
-    total = pair[...].astype(F32)
-    for v in (v1, v2, v3):
-        total += v[...].astype(F32)
-    own[...] = total[0:16].astype(BF)
-    mate[0:16, :] = direct[0:16, :]
-    mate[16:32, :] = total[16:32].astype(BF)
-
-
-def finish_kernel(local, own, came, grad_keys, grad_values):
-    x = jnp.concatenate([came[...], own[...]], axis=0)
+            remotes.append(remote)
+            top[:, out_cols] = remote[0:16]
+            fine[:, out_cols] = remote[16:48]
+    core = lax.axis_index("ctx") & 1
+    n, j = grid_of((4 * 32, FAR))
+    k, i = n >> 5, n & 31
+    along_y = (k > 0) & (i < 16) & (j == 32 + 16 * k + i)
+    dc = (i >= 12).astype(jnp.int32)
+    r = i - 12 * dc
+    along_x = (i < 24) & (r < 8) & (k == 1) & (j == 16 + dc * 8 + r)
+    along_x |= (i < 24) & (r >= 8) & (k >= 2) & (j == 32 + (2 * k - 4 + dc) * 4 + r - 8)
+    along_x |= (i >= 24) & (i < 28) & (j == 48 + 4 * k + i - 24)
+    along_x |= (i >= 28) & (i < 30) & (j == 64 + 2 * k + i - 28)
+    along_x |= (i >= 30) & (j == 80 + 2 * k + i - 30)
+    pick = matrix(((core == 0) & along_y) | ((core == 1) & along_x))
+    for at, remote in zip(REMOTE_COLUMNS, remotes):
+        got = dot(pick, remote).astype(BF)
+        for n in range(4):
+            row = n * 128 + at // 256 * 32
+            first[row : row + 32, at % 256 : at % 256 + HEAD_DIM] = got[32 * n : 32 * (n + 1)]
+
+
+def combine_kernel(near, back, coarse, keep, kept, a1, a2, a3):
+    for k, out in enumerate((keep, a1, a2, a3)):
+        for n in range(8):
+            total = near[8 * k + n].astype(F32) + back[8 * k + n].astype(F32)
+            out[n * 128 : (n + 1) * 128, :] = total.astype(BF)
+    kept[...] = coarse[0:128, :]
+    for k, out in ((1, a1), (2, a2), (3, a3)):
+        out[1024:1152, :] = coarse[128 * k : 128 * (k + 1), :]
+
+
+def sum_rows(refs, rows):
+    total = refs[0][rows, :].astype(F32)
+    for r in refs[1:]:
+        total += r[rows, :].astype(F32)
+    return total
+
+
+def middle_kernel(fine, kept, keep, a1, a2, a3, keep2, kept2, u1, u2, u3):
+    for k, out in enumerate((keep2, u1, u2, u3)):
+        out[0:256, :] = sum_rows((keep, a1, a2, a3), slice(k * 256, (k + 1) * 256)).astype(BF)
+    core = lax.axis_index("ctx") & 1
+    n, j = grid_of((4 * 32, 32 + 4 * 32))
+    k, i = n >> 5, n & 31
+    dc, r = i >> 4, i & 15
+    m = 2 * k + dc
+    along_x = (r < 8) & (k == 1) & (j == dc * 8 + r)
+    along_x |= (r >= 8) & (r < 12) & (k >= 2) & (j == 16 + (m - 4) * 4 + r - 8)
+    along_x |= (r >= 12) & (r < 14) & (j == 64 + 2 * m + r - 12)
+    along_x |= (r == 14) & ((j == 96 + m) | (j == 128 + m))
+    row = j & 31
+    along_y = (k == 0) & (r < 12) & (row == dc * 12 + r)
+    along_y |= (k == 1) & (i < 4) & (row == 24 + i)
+    along_y |= (k == 2) & (i < 2) & (row == 28 + i)
+    along_y |= (k == 3) & (i < 2) & (row == 30 + i)
+    pick = matrix(((core == 0) & along_x) | ((core == 1) & along_y & (j >= 32)))
+    for c in range(4):
+        got = [kept[32 * c : 32 * (c + 1), :]]
+        got += [a[1024 + 32 * c : 1056 + 32 * c, :] for a in (a1, a2, a3)]
+        y = dot(pick, jnp.concatenate([fine[:, 256 * c : 256 * (c + 1)]] + got, axis=0)).astype(BF)
+        kept2[32 * c : 32 * (c + 1), :] = y[0:32]
+        for k, u in ((1, u1), (2, u2), (3, u3)):
+            u[256 + 32 * c : 288 + 32 * c, :] = y[32 * k : 32 * (k + 1)]
+
+
+def last_kernel(top, kept, keep, u1, u2, u3, mine, own, mate):
+    mine[...] = sum_rows((keep, u1, u2, u3), slice(0, 128))
+    mate[0:128, :] = sum_rows((keep, u1, u2, u3), slice(128, 256)).astype(BF)
+    core = lax.axis_index("ctx") & 1
+    i, j = grid_of((32, 4 * 32))
+    dc, r = i >> 4, i & 15
+    placed = (j < 32) & (j == i)
+    placed |= (r >= 12) & (r < 14) & (j == 32 + dc * 2 + r - 12)
+    placed |= (r == 14) & ((j == 64 + dc) | (j == 96 + dc))
+    pick = matrix(((core == 0) & (j & 31 == i)) | ((core == 1) & placed))
+    for c in range(4):
+        got = [kept[32 * c : 32 * (c + 1), :]]
+        got += [u[256 + 32 * c : 288 + 32 * c, :] for u in (u1, u2, u3)]
+        y = dot(pick, jnp.concatenate(got, axis=0)).astype(BF)
+        own[:, 256 * c : 256 * (c + 1)] = y[0:16]
+        mate[128 + 32 * c : 144 + 32 * c, :] = top[:, 256 * c : 256 * (c + 1)]
+        mate[144 + 32 * c : 160 + 32 * c, :] = y[16:32]
+
+
+def finish_kernel(local, own, mine, came, grad_keys, grad_values, grad_weight):
+    core = lax.axis_index("ctx") & 1
+    grad_weight[:, pl.ds(pl.multiple_of(core * 256, 256), 256)] = mine[...]
+    grad_weight[:, pl.ds(pl.multiple_of(256 - core * 256, 256), 256)] = came[0:128, :].astype(F32)
+    got = [came[128 + 32 * c : 160 + 32 * c, :] for c in range(4)]
+    x = jnp.concatenate([jnp.concatenate(got, axis=1), own[...]], axis=0)
     t, j = grid_of((ROWS, 3 * BLOCK))
     i = j & 15
     high = j >= BLOCK
@@ -264,20 +332,22 @@
     core = rank & 1
     place = rank >> 1
     copies[0].wait()
-    att = att_held[...]
+    sides = []
+    for holder, out in ((core, near_held), (1 - core, away_held)):
+        at = pl.multiple_of(holder * 256, 256)
+        sides.append((holder, att_held[:, pl.ds(at, 256)], out))
     for k, offset in enumerate(OFFSETS):
         copies[1 + k].wait()
         if k == 7:
             copies[9].wait()
         z = chunk_of(offset)
-        for side, out in enumerate((near_held, away_held)):
-            for pair in range(2):
-                at = pl.multiple_of((2 * pair + (core ^ side)) * 128, 128)
-                term = (dot(held[k, :, pl.ds(at, 128)], att, ((0,), (0,))) * GRAD_SCALE).astype(BF)
-                apart = (2 * z + pair) ^ place
-                kx, ky = apart & 3, apart >> 2
-                out[0, kx * 4 + ky] = term[:, :256]
-                out[1, ky * 4 + kx] = term[:, 256:]
+        for i in range(4):
+            block = held[k, :, i * 128 : (i + 1) * 128]
+            apart = (2 * z + (i >> 1)) ^ place
+            kx, ky = apart & 3, apart >> 2
+            for holder, att, out in sides:
+                slot = jnp.where(holder == 0, ky * 4 + kx, kx * 4 + ky) * 2 + ((i & 1) ^ holder)
+                out[slot] = (dot(block, att, ((0,), (0,))) * GRAD_SCALE).astype(BF)
     stores = [
         pltpu.make_async_copy(away_held, away, sems.at[18]),
         pltpu.make_async_copy(near_held, near, sems.at[19]),
@@ -301,6 +371,18 @@
     return lax.ppermute(x, "ctx", pairs)
 
 
+def crossing(x, k, step):
+    pairs = []
+    for rank in range(32):
+        y, xx, c = rank >> 3, (rank >> 1) & 3, rank & 1
+        if c == step:
+            y ^= k
+        else:
+            xx ^= k
+        pairs.append((rank, (y << 2 | xx) << 1 | c))
+    return lax.ppermute(x, "ctx", pairs)
+
+
 def shift(x, step):
     return lax.ppermute(x, "tp", [(i, (i + step) % 8) for i in range(8)])
 
@@ -314,32 +396,17 @@
     return blocks + [shift(right[:HALF], 1), shift(left[HALF:], -1)]
 
 
-def total_of(*terms):
-    return functools.reduce(lambda a, b: a + b, [t.astype(F32) for t in terms])
-
-
 def together(*xs):
     return lax.optimization_barrier(xs)
 
 
-def send_blocks(held, count, last):
-    moved = [[], []]
-    for k in (2, 1, 3):
-        for side in range(2):
-            step = {"dx" if (side == 0) != last else "dy": k}
-            moved[side].append(ctx_exchange(held[side][k * count : (k + 1) * count], **step))
-    return moved
-
-
 def on_device(queries, keys, values, out_weight, out_grad):
     tile = shaped((ROWS, WIDTH))
-    half = shaped((HALF, WIDTH))
     pack16, pack32 = shaped((16, 2 * WIDTH)), shaped((32, 2 * WIDTH))
 
     r1, l1 = shift(out_grad, 1), shift(out_grad, -1)
-    inputs = jnp.concatenate([queries, keys, values], axis=1)
     low, pack, high = call(
-        pool_kernel, (shaped((224, 2 * WIDTH)), pack32, pack16), inputs, micros=2
+        pool_kernel, (shaped((224, 2 * WIDTH)), pack32, pack16), keys, values, micros=2
     )
     first = ctx_exchange(pack, dc=1)
 
@@ -355,22 +422,28 @@
 
     r3, l3, *column = together(r3, l3, *column)
     r4, l4 = shift(r3[:HALF], 1), shift(l3[HALF:], -1)
-    operands = (inputs, low, first, *row, *column)
+    operands = (queries, keys, values, low, first, *row, *column)
     outs = (tile, shaped((2 * HEADS, KEYS, HALF), F32), shaped((FAR, 2 * WIDTH)), shaped((8, ROWS, WIDTH)))
     attention, prob, far, shares = pl.pallas_call(
         forward_kernel,
         grid=(1,),
         out_shape=outs,
         in_specs=[ANY] + [whole(x) for x in operands],
-        out_specs=tuple(whole(x) for x in outs),
-        scratch_shapes=[pltpu.VMEM((8, WIDTH, WIDTH), BF), pltpu.SemaphoreType.DMA((8,))],
+        out_specs=(whole(outs[0]), ANY, whole(outs[2]), ANY),
+        scratch_shapes=[
+            pltpu.VMEM((8, WIDTH, WIDTH), BF),
+            pltpu.VMEM(outs[1].shape, F32),
+            pltpu.VMEM(outs[3].shape, BF),
+            pltpu.SemaphoreType.DMA((17,)),
+        ],
         compiler_params=LARGE,
-        cost_estimate=cost(0),
+        cost_estimate=cost(8),
     )(out_weight, *operands)
+    shares, r4, l4 = together(shares, r4, l4)
     mixed = lax.psum_scatter(shares.reshape(8 * ROWS, WIDTH), "tp", scatter_dimension=0, tiled=True)
 
     blocks = [out_grad, r1, l1, r2, l2, r3, l3, r4, l4]
-    parts = shaped((2, 16, 128, 256))
+    parts = shaped((32, 128, 256))
     near, away, grad_attention = pl.pallas_call(
         product_kernel,
         grid=(1,),
@@ -381,8 +454,8 @@
             pltpu.VMEM((ROWS, WIDTH), BF),
             pltpu.VMEM((8, ROWS, WIDTH), BF),
             pltpu.VMEM((8, WIDTH, WIDTH), BF),
-            pltpu.VMEM((2, 16, 128, 256), BF),
-            pltpu.VMEM((2, 16, 128, 256), BF),
+            pltpu.VMEM((32, 128, 256), BF),
+            pltpu.VMEM((32, 128, 256), BF),
             pltpu.SemaphoreType.DMA((20,)),
         ],
         compiler_params=LARGE,
@@ -390,28 +463,35 @@
     )(*blocks, attention, out_weight)
 
     back = ctx_exchange(away, dc=1)
-    grad_queries, local, direct, m7, m8a, m8b = call(
+    grad_queries, local, fine, top, coarse = call(
         backward_kernel,
-        (tile, shaped((ROWS, 2 * WIDTH), F32), shaped((48, 2 * WIDTH))) + (pack16,) * 3,
-        inputs, low, far, prob, grad_attention, params=LARGE, micros=0,
-    )
-
-    held = [total_of(near[side], back[side]).astype(BF) for side in range(2)]
-    direct, m7, m8a, m8b, *held = together(direct, m7, m8a, m8b, *held)
-    moved = send_blocks(held, 4, False)
-    column = [ctx_exchange(m7, dy=1), ctx_exchange(m8a, dy=2), ctx_exchange(m8b, dy=3)]
-
-    held = [total_of(held[side][:4], *moved[side]).astype(BF) for side in range(2)]
-    moved = send_blocks(held, 1, True)
-    pair, *sent = call(relay_back_kernel, (pack32,) * 4, direct, *column)
-    came = [ctx_exchange(sent[k - 1], dx=k) for k in (1, 2, 3)]
-
-    own, mate = call(pair_kernel, (pack16, pack32), direct, pair, *came)
-    came = ctx_exchange(mate, dc=1)
-    held = [total_of(held[side][:1], *moved[side]) for side in range(2)]
-    grad_weight = jnp.concatenate([h[0] for h in held], axis=1)
-
-    grad_keys, grad_values = call(finish_kernel, (tile,) * 2, local, own, came)
+        (
+            tile,
+            shaped((ROWS, 2 * WIDTH), F32),
+            shaped((32, 2 * WIDTH)),
+            pack16,
+            shaped((512, 256)),
+        ),
+        queries, keys, values, low, far, prob, grad_attention, params=LARGE, micros=0,
+    )
+
+    small, joint = shaped((128, 256)), shaped((1152, 256))
+    keep, kept, *sent = call(
+        combine_kernel, (shaped((1024, 256)), small) + (joint,) * 3, near, back, coarse
+    )
+    over = [crossing(sent[k - 1], k, 0) for k in (1, 2, 3)]
+    joint = shaped((384, 256))
+    keep, kept, *sent = call(
+        middle_kernel, (shaped((256, 256)), small) + (joint,) * 3, fine, kept, keep, *over
+    )
+    over = [crossing(sent[k - 1], k, 1) for k in (1, 2, 3)]
+    mixed, *over = together(mixed, *over)
+    mine, own, mate = call(
+        last_kernel, (shaped((128, 256), F32), pack16, shaped((256, 256))), top, kept, keep, *over
+    )
+    grad_keys, grad_values, grad_weight = call(
+        finish_kernel, (tile, tile, shaped((128, WIDTH), F32)), local, own, mine, ctx_exchange(mate, dc=1)
+    )
     return mixed, grad_queries, grad_keys, grad_values, grad_weight
 
 

time: 125 us -> 115 us (0.920)
  starting transfers between devices: 53.5 us -> 37.6 us
  waiting for transfers between devices: 23 us -> 29.9 us
  other arithmetic: 3.54 us -> 0.01 us
  Pallas kernels: 25.4 us -> 28 us
    ppermute x27 -> x9, starting transfers between devices: 39.9 us -> 16.1 us  [ctx_exchange(): return lax.ppermute(x, 'ctx', pairs)]
    ppermute x0 -> x6, waiting for transfers between devices: none -> 20.6 us  [crossing(): return lax.ppermute(x, 'ctx', pairs)]
    ppermute x27 -> x9, waiting for transfers between devices: 22.9 us -> 9.28 us  [ctx_exchange(): return lax.ppermute(x, 'ctx', pairs)]
    ppermute x0 -> x6, starting transfers between devices: none -> 7.88 us  [crossing(): return lax.ppermute(x, 'ctx', pairs)]
    convert_element_type x3 -> x0, other arithmetic: 2.74 us -> none  [the longest x1 2.45 us: on_device(): held = [total_of(near[side], back[side]).astype(BF) for side in range(2)]]
    pallas_call x6 -> x7, Pallas kernels: 10.6 us -> 13.3 us  [call(): pl.pallas_call(kernel, grid=(1,), out_shape=outs, in_specs=[whole(a) for...]
    unnamed x48 -> x46, local copies, waits for them, and re-layouts: 3.55 us -> 4.37 us
  transfers between devices with their start and end apart: 36 -> 24, of which waited for: 13 -> 12; matrix products, arithmetic and copies ran while one was open for 5% -> 0% of each run, Pallas kernels for 15% -> 23%
where the time goes in v2:
time: 115 us; the launch traced here: 114 us
  starting transfers between devices  37.6 us (33%)
  waiting for transfers between devices  29.9 us (26%)
  Pallas kernels  28 us (24%)
  between operations  14.3 us (12%)
  local copies, waits for them, and re-layouts  4.39 us (4%)
    ppermute x6, waiting for transfers between devices, crossing(): return lax.ppermute(x, 'ctx', pairs)  20.6 us
    ppermute x9, starting transfers between devices, ctx_exchange(): return lax.ppermute(x, 'ctx', pairs)  16.1 us
    ppermute x8, starting transfers between devices, shift(): return lax.ppermute(x, 'tp', [(i, (i + step) % 8) for i in range(8)])  13.6 us
    pallas_call x7, Pallas kernels, call(): pl.pallas_call(kernel, grid=(1,), out_shape=outs, in_specs=[whole(a) for...  13.3 us
    ppermute x9, waiting for transfers between devices, ctx_exchange(): return lax.ppermute(x, 'ctx', pairs)  9.28 us
    pallas_call x1, Pallas kernels, on_device(): pl.pallas_call(forward_kernel, grid=(1,), out_shape=outs, in_specs=[ANY]...  8.12 us
    ppermute x6, starting transfers between devices, crossing(): return lax.ppermute(x, 'ctx', pairs)  7.88 us
    pallas_call x1, Pallas kernels, on_device(): pl.pallas_call(product_kernel, grid=(1,), out_shape=(parts, parts, tile),...  6.59 us
  transfers between devices with their start and end apart: 24, of which 12 were waited for; matrix products, arithmetic and copies ran while one was open for 0% of the time, Pallas kernels for 23%

profile of v2, /device:TPU:1, one launch (start us, length us, event | category | flops | bytes accessed | tf_op | source)
XLA Modules:
  0.0 114.2 jit_solution(14963613998694788880)
XLA Ops:
  7.2 2.5 %collective-permute-start.1 = (bf16[256,512]{1,0:T(8,128)(2,1)}, bf16[256,512]{1,0:T(8,128)(2,1)S(1)}, u32[]{:S(2)}, u32[]{:S(2)}) collective-permute-start(bf16[256,512]{1,0:T(8,128)(2,1)} %refs_0_.1), channel_id=1, source_target_pairs={{0,1},{1,2},{2,3},{3,4},{4,5},{5,6},{6,7},{7,0},{8,9},{9,10},{10,1... | collective-permute-start | bytes 786440 | tf_op jit(solution)/shard_map/ppermute | solution.py:387
  9.8 4.0 %collective-permute-start.2 = (bf16[256,512]{1,0:T(8,128)(2,1)}, bf16[256,512]{1,0:T(8,128)(2,1)S(1)}, u32[]{:S(2)}, u32[]{:S(2)}) collective-permute-start(bf16[256,512]{1,0:T(8,128)(2,1)} %refs_0_.1), channel_id=1, source_target_pairs={{0,7},{1,0},{2,1},{3,2},{4,3},{5,4},{6,5},{7,6},{8,15},{9,8},{10,9... | collective-permute-start | bytes 786440 | tf_op jit(solution)/shard_map/ppermute | solution.py:387
  15.7 2.2 %shard_map.92 = (bf16[224,1024]{1,0:T(8,128)(2,1)S(1)}, bf16[32,1024]{1,0:T(8,128)(2,1)S(1)}, bf16[16,1024]{1,0:T(8,128)(2,1)S(1)}) custom-call(bf16[256,512]{1,0:T(8,128)(2,1)S(1)} %copy-done, bf16[256,512]{1,0:T(8,128)(2,1)S(1)} %copy-done.1), custom_call_target="tpu_custom_call" | custom-call | bytes 7400000 | tf_op jit(solution)/shard_map/pallas_call | solution.py:46
  20.7 2.7 %collective-permute-start.7 = (bf16[256,512]{1,0:T(8,128)(2,1)S(1)}, bf16[256,512]{1,0:T(8,128)(2,1)S(1)}, u32[]{:S(2)}, u32[]{:S(2)}) collective-permute-start(bf16[256,512]{1,0:T(8,128)(2,1)S(1)} %collective-permute-done.2.refs_2_), channel_id=1, source_target_pairs={{0,7},{1,0},{2,1},{3,2},{4,3},{5,4},{6,5},{7,6},{8,15},{9,8},{10,9... | collective-permute-start | bytes 786440 | tf_op jit(solution)/shard_map/ppermute | solution.py:387
  23.3 2.5 %collective-permute-start.5 = (bf16[32,1024]{1,0:T(8,128)(2,1)S(1)}, bf16[32,1024]{1,0:T(8,128)(2,1)S(1)}, u32[]{:S(2)}, u32[]{:S(2)}) collective-permute-start(bf16[32,1024]{1,0:T(8,128)(2,1)S(1)} %pad_maximum_fusion), channel_id=1, source_target_pairs={{0,48},{8,56},{16,32},{24,40},{32,16},{40,24},{48,0},{56,8},{64,11... | collective-permute-start | bytes 196616 | tf_op jit(solution)/shard_map/ppermute | solution.py:371
  28.0 2.5 %collective-permute-done.4.x2 = bf16[32,1024]{1,0:T(8,128)(2,1)S(1)} collective-permute-done((bf16[32,1024]{1,0:T(8,128)(2,1)S(1)}, bf16[32,1024]{1,0:T(8,128)(2,1)S(1)}, u32[]{:S(2)}, u32[]{:S(2)}) %collective-permute-start.4) | collective-permute-done | bytes 65568 | tf_op jit(solution)/shard_map/ppermute | solution.py:371
  30.8 2.7 %collective-permute-start.9 = (bf16[256,512]{1,0:T(8,128)(2,1)S(1)}, bf16[256,512]{1,0:T(8,128)(2,1)S(1)}, u32[]{:S(2)}, u32[]{:S(2)}) collective-permute-start(bf16[256,512]{1,0:T(8,128)(2,1)S(1)} %collective-permute-done.7.refs_4_), channel_id=1, source_target_pairs={{0,7},{1,0},{2,1},{3,2},{4,3},{5,4},{6,5},{7,6},{8,15},{9,8},{10,9... | collective-permute-start | bytes 786440 | tf_op jit(solution)/shard_map/ppermute | solution.py:387
  34.7 1.9 %collective-permute-start.12 = (bf16[16,1024]{1,0:T(8,128)(2,1)S(1)}, bf16[16,1024]{1,0:T(8,128)(2,1)S(1)}, u32[]{:S(2)}, u32[]{:S(2)}) collective-permute-start(bf16[16,1024]{1,0:T(8,128)(2,1)S(1)} %get-tuple-element.68), channel_id=1, source_target_pairs={{0,192},{8,200},{16,208},{24,216},{32,224},{40,232},{48,240},{56,2... | collective-permute-start | bytes 98312 | tf_op jit(solution)/shard_map/ppermute | solution.py:371
  37.3 1.6 %collective-permute-done.12.s3 = bf16[16,1024]{1,0:T(8,128)(2,1)S(1)} collective-permute-done((bf16[16,1024]{1,0:T(8,128)(2,1)S(1)}, bf16[16,1024]{1,0:T(8,128)(2,1)S(1)}, u32[]{:S(2)}, u32[]{:S(2)}) %collective-permute-start.12) | collective-permute-done | bytes 32800 | tf_op jit(solution)/shard_map/ppermute | solution.py:371
  39.0 1.9 %collective-permute-done.11.s2 = bf16[16,1024]{1,0:T(8,128)(2,1)S(1)} collective-permute-done((bf16[16,1024]{1,0:T(8,128)(2,1)S(1)}, bf16[16,1024]{1,0:T(8,128)(2,1)S(1)}, u32[]{:S(2)}, u32[]{:S(2)}) %collective-permute-start.11) | collective-permute-done | bytes 32800 | tf_op jit(solution)/shard_map/ppermute | solution.py:371
  42.5 8.1 %shard_map.94 = (bf16[256,512]{1,0:T(8,128)(2,1)}, f32[8,336,128]{2,1,0:T(8,128)}, bf16[96,1024]{1,0:T(8,128)(2,1)}, bf16[8,256,512]{2,1,0:T(8,128)(2,1)}) custom-call(bf16[4096,512]{1,0:T(8,128)(2,1)} %refs_10_.1, bf16[256,512]{1,0:T(8,128)(2,1)} %queries.3, bf16[256,512]{1,0:T(8,128)(2,1)} %keys.5, bf16[256,512]{1,0:T(8,128)(2,1)} %values.5, ...), custom_call_target="tpu_custom_call" | custom-call | bytes 29600000 | tf_op jit(solution)/shard_map/pallas_call | solution.py:427
  51.4 6.6 %shard_map.95 = (bf16[32,128,256]{2,1,0:T(8,128)(2,1)}, bf16[32,128,256]{2,1,0:T(8,128)(2,1)}, bf16[256,512]{1,0:T(8,128)(2,1)}) custom-call(bf16[256,512]{1,0:T(8,128)(2,1)} %refs_0_.1, bf16[256,512]{1,0:T(8,128)(2,1)} %copy-done.14, bf16[256,512]{1,0:T(8,128)(2,1)} %copy-done.15, bf16[256,512]{1,0:T(8,128)(2,1)} %copy-done.16, ...), custom_call_target="tpu_custom_call" | custom-call | tf_op jit(solution)/shard_map/pallas_call | solution.py:447
  58.0 5.5 %collective-permute-start.15 = (bf16[32,128,256]{2,1,0:T(8,128)(2,1)}, bf16[32,128,256]{2,1,0:T(8,128)(2,1)}, u32[]{:S(2)}, u32[]{:S(2)}) collective-permute-start(bf16[32,128,256]{2,1,0:T(8,128)(2,1)} %get-tuple-element.84), channel_id=1, source_target_pairs={{0,8},{8,0},{16,24},{24,16},{32,40},{40,32},{48,56},{56,48},{64,72... | collective-permute-start | bytes 6291464 | tf_op jit(solution)/shard_map/ppermute | solution.py:371
  63.5 6.9 %shard_map.96 = (bf16[256,512]{1,0:T(8,128)(2,1)}, f32[256,1024]{1,0:T(8,128)}, bf16[32,1024]{1,0:T(8,128)(2,1)}, bf16[16,1024]{1,0:T(8,128)(2,1)}, bf16[512,256]{1,0:T(8,128)(2,1)}) custom-call(bf16[256,512]{1,0:T(8,128)(2,1)} %queries.3, bf16[256,512]{1,0:T(8,128)(2,1)} %keys.5, bf16[256,512]{1,0:T(8,128)(2,1)} %values.5, bf16[224,1024]{1,0:T(8,128)(2,1)} %copy-done.3, ...), custom_call_target="tpu_custom_call" | custom-call | tf_op jit(solution)/shard_map/pallas_call | solution.py:46
  71.4 2.1 %shard_map.97 = (bf16[1024,256]{1,0:T(8,128)(2,1)S(1)}, bf16[128,256]{1,0:T(8,128)(2,1)S(1)}, bf16[1152,256]{1,0:T(8,128)(2,1)S(1)}, bf16[1152,256]{1,0:T(8,128)(2,1)S(1)}, bf16[1152,256]{1,0:T(8,128)(2,1)S(1)}) custom-call(bf16[32,128,256]{2,1,0:T(8,128)(2,1)S(1)} %copy-done.2, bf16[32,128,256]{2,1,0:T(8,128)(2,1)} %collective-permute-done.15.back, ...), custom_call_target="tpu_custom_call" | custom-call | bytes 1110000 | tf_op jit(solution)/shard_map/pallas_call | solution.py:46
  73.7 2.2 %collective-permute-start.17 = (bf16[1152,256]{1,0:T(8,128)(2,1)S(1)}, bf16[1152,256]{1,0:T(8,128)(2,1)S(1)}, u32[]{:S(2)}, u32[]{:S(2)}) collective-permute-start(bf16[1152,256]{1,0:T(8,128)(2,1)S(1)} %get-tuple-element.89), channel_id=1, source_target_pairs={{0,128},{8,40},{16,144},{24,56},{32,160},{40,8},{48,176},{56,24},{... | collective-permute-start | bytes 1769480 | tf_op jit(solution)/shard_map/ppermute | solution.py:383
  77.5 5.3 %collective-permute-done.16.a1 = bf16[1152,256]{1,0:T(8,128)(2,1)S(1)} collective-permute-done((bf16[1152,256]{1,0:T(8,128)(2,1)S(1)}, bf16[1152,256]{1,0:T(8,128)(2,1)S(1)}, u32[]{:S(2)}, u32[]{:S(2)}) %collective-permute-start.16) | collective-permute-done | bytes 589856 | tf_op jit(solution)/shard_map/ppermute | solution.py:383
  82.8 7.0 %collective-permute-done.17.a2 = bf16[1152,256]{1,0:T(8,128)(2,1)S(1)} collective-permute-done((bf16[1152,256]{1,0:T(8,128)(2,1)S(1)}, bf16[1152,256]{1,0:T(8,128)(2,1)S(1)}, u32[]{:S(2)}, u32[]{:S(2)}) %collective-permute-start.17) | collective-permute-done | bytes 589856 | tf_op jit(solution)/shard_map/ppermute | solution.py:383
  89.8 2.6 %collective-permute-done.18.a3 = bf16[1152,256]{1,0:T(8,128)(2,1)S(1)} collective-permute-done((bf16[1152,256]{1,0:T(8,128)(2,1)S(1)}, bf16[1152,256]{1,0:T(8,128)(2,1)S(1)}, u32[]{:S(2)}, u32[]{:S(2)}) %collective-permute-start.18) | collective-permute-done | bytes 589856 | tf_op jit(solution)/shard_map/ppermute | solution.py:383
  93.2 1.8 %collective-permute-start.20 = (bf16[384,256]{1,0:T(8,128)(2,1)S(1)}, bf16[384,256]{1,0:T(8,128)(2,1)S(1)}, u32[]{:S(2)}, u32[]{:S(2)}) collective-permute-start(bf16[384,256]{1,0:T(8,128)(2,1)S(1)} %get-tuple-element.92), channel_id=1, source_target_pairs={{0,32},{8,136},{16,48},{24,152},{32,0},{40,168},{48,16},{56,184},{... | collective-permute-start | bytes 589832 | tf_op jit(solution)/shard_map/ppermute | solution.py:383
  95.1 1.9 %collective-permute-start.21 = (bf16[384,256]{1,0:T(8,128)(2,1)S(1)}, bf16[384,256]{1,0:T(8,128)(2,1)S(1)}, u32[]{:S(2)}, u32[]{:S(2)}) collective-permute-start(bf16[384,256]{1,0:T(8,128)(2,1)S(1)} %get-tuple-element.93), channel_id=1, source_target_pairs={{0,48},{8,200},{16,32},{24,216},{32,16},{40,232},{48,0},{56,248},{... | collective-permute-start | bytes 589832 | tf_op jit(solution)/shard_map/ppermute | solution.py:383
  98.0 2.6 %collective-permute-done.20.u2 = bf16[384,256]{1,0:T(8,128)(2,1)S(1)} collective-permute-done((bf16[384,256]{1,0:T(8,128)(2,1)S(1)}, bf16[384,256]{1,0:T(8,128)(2,1)S(1)}, u32[]{:S(2)}, u32[]{:S(2)}) %collective-permute-start.20) | collective-permute-done | bytes 196640 | tf_op jit(solution)/shard_map/ppermute | solution.py:383
  100.6 2.1 %collective-permute-done.21.u3 = bf16[384,256]{1,0:T(8,128)(2,1)S(1)} collective-permute-done((bf16[384,256]{1,0:T(8,128)(2,1)S(1)}, bf16[384,256]{1,0:T(8,128)(2,1)S(1)}, u32[]{:S(2)}, u32[]{:S(2)}) %collective-permute-start.21) | collective-permute-done | bytes 196640 | tf_op jit(solution)/shard_map/ppermute | solution.py:383
  102.8 2.5 %collective-permute-start.22 = (bf16[256,256]{1,0:T(8,128)(2,1)S(1)}, bf16[256,256]{1,0:T(8,128)(2,1)S(1)}, u32[]{:S(2)}, u32[]{:S(2)}) collective-permute-start(bf16[256,256]{1,0:T(8,128)(2,1)S(1)} %get-tuple-element.105), channel_id=1, source_target_pairs={{0,8},{8,0},{16,24},{24,16},{32,40},{40,32},{48,56},{56,48},{64,72... | collective-permute-start | bytes 393224 | tf_op jit(solution)/shard_map/ppermute | solution.py:371
  (84 shorter events, 18.1 us)
Async XLA Ops:
  7.2 95.5 %reduce-scatter.2.cloned.1.call-start = ((), (), s32[]{:S(2)}) async-start(), calls=%async_computation.1 | async-start | bytes 2359296 | tf_op jit(solution)/shard_map/reduce_scatter | solution.py:443
  7.2 13.3 %collective-permute-start.1 = (bf16[256,512]{1,0:T(8,128)(2,1)}, bf16[256,512]{1,0:T(8,128)(2,1)S(1)}, u32[]{:S(2)}, u32[]{:S(2)}) collective-permute-start(bf16[256,512]{1,0:T(8,128)(2,1)} %refs_0_.1), channel_id=1, source_target_pairs={{0,1},{1,2},{2,3},{3,4},{4,5},{5,6},{6,7},{7,0},{8,9},{9,10},{10,1... | collective-permute-start | bytes 786440 | tf_op jit(solution)/shard_map/ppermute | solution.py:387
  9.8 10.8 %collective-permute-start.2 = (bf16[256,512]{1,0:T(8,128)(2,1)}, bf16[256,512]{1,0:T(8,128)(2,1)S(1)}, u32[]{:S(2)}, u32[]{:S(2)}) collective-permute-start(bf16[256,512]{1,0:T(8,128)(2,1)} %refs_0_.1), channel_id=1, source_target_pairs={{0,7},{1,0},{2,1},{3,2},{4,3},{5,4},{6,5},{7,6},{8,15},{9,8},{10,9... | collective-permute-start | bytes 786440 | tf_op jit(solution)/shard_map/ppermute | solution.py:387
  18.7 1.9 %collective-permute-start = (bf16[32,1024]{1,0:T(8,128)(2,1)S(1)}, bf16[32,1024]{1,0:T(8,128)(2,1)S(1)}, u32[]{:S(2)}, u32[]{:S(2)}) collective-permute-start(bf16[32,1024]{1,0:T(8,128)(2,1)S(1)} %get-tuple-element.58), channel_id=1, source_target_pairs={{0,8},{8,0},{16,24},{24,16},{32,40},{40,32},{48,56},{56,48},{64,72... | collective-permute-start | bytes 196616 | tf_op jit(solution)/shard_map/ppermute | solution.py:371
  20.6 10.0 %collective-permute-start.6 = (bf16[256,512]{1,0:T(8,128)(2,1)S(1)}, bf16[256,512]{1,0:T(8,128)(2,1)S(1)}, u32[]{:S(2)}, u32[]{:S(2)}) collective-permute-start(bf16[256,512]{1,0:T(8,128)(2,1)S(1)} %collective-permute-done.1.refs_1_), channel_id=1, source_target_pairs={{0,1},{1,2},{2,3},{3,4},{4,5},{5,6},{6,7},{7,0},{8,9},{9,10},{10,1... | collective-permute-start | bytes 786440 | tf_op jit(solution)/shard_map/ppermute | solution.py:387
  20.7 10.0 %collective-permute-start.7 = (bf16[256,512]{1,0:T(8,128)(2,1)S(1)}, bf16[256,512]{1,0:T(8,128)(2,1)S(1)}, u32[]{:S(2)}, u32[]{:S(2)}) collective-permute-start(bf16[256,512]{1,0:T(8,128)(2,1)S(1)} %collective-permute-done.2.refs_2_), channel_id=1, source_target_pairs={{0,7},{1,0},{2,1},{3,2},{4,3},{5,4},{6,5},{7,6},{8,15},{9,8},{10,9... | collective-permute-start | bytes 786440 | tf_op jit(solution)/shard_map/ppermute | solution.py:387
  23.3 4.6 %collective-permute-start.5 = (bf16[32,1024]{1,0:T(8,128)(2,1)S(1)}, bf16[32,1024]{1,0:T(8,128)(2,1)S(1)}, u32[]{:S(2)}, u32[]{:S(2)}) collective-permute-start(bf16[32,1024]{1,0:T(8,128)(2,1)S(1)} %pad_maximum_fusion), channel_id=1, source_target_pairs={{0,48},{8,56},{16,32},{24,40},{32,16},{40,24},{48,0},{56,8},{64,11... | collective-permute-start | bytes 196616 | tf_op jit(solution)/shard_map/ppermute | solution.py:371
  25.8 4.6 %collective-permute-start.4 = (bf16[32,1024]{1,0:T(8,128)(2,1)S(1)}, bf16[32,1024]{1,0:T(8,128)(2,1)S(1)}, u32[]{:S(2)}, u32[]{:S(2)}) collective-permute-start(bf16[32,1024]{1,0:T(8,128)(2,1)S(1)} %pad_maximum_fusion), channel_id=1, source_target_pairs={{0,32},{8,40},{16,48},{24,56},{32,0},{40,8},{48,16},{56,24},{64,96... | collective-permute-start | bytes 196616 | tf_op jit(solution)/shard_map/ppermute | solution.py:371
  26.3 4.1 %collective-permute-start.3 = (bf16[32,1024]{1,0:T(8,128)(2,1)S(1)}, bf16[32,1024]{1,0:T(8,128)(2,1)S(1)}, u32[]{:S(2)}, u32[]{:S(2)}) collective-permute-start(bf16[32,1024]{1,0:T(8,128)(2,1)S(1)} %pad_maximum_fusion), channel_id=1, source_target_pairs={{0,16},{8,24},{16,0},{24,8},{32,48},{40,56},{48,32},{56,40},{64,80... | collective-permute-start | bytes 196616 | tf_op jit(solution)/shard_map/ppermute | solution.py:371
  30.7 10.2 %collective-permute-start.8 = (bf16[256,512]{1,0:T(8,128)(2,1)S(1)}, bf16[256,512]{1,0:T(8,128)(2,1)S(1)}, u32[]{:S(2)}, u32[]{:S(2)}) collective-permute-start(bf16[256,512]{1,0:T(8,128)(2,1)S(1)} %collective-permute-done.6.refs_3_), channel_id=1, source_target_pairs={{0,1},{1,2},{2,3},{3,4},{4,5},{5,6},{6,7},{7,0},{8,9},{9,10},{10,1... | collective-permute-start | bytes 786440 | tf_op jit(solution)/shard_map/ppermute | solution.py:387
  30.8 10.1 %collective-permute-start.9 = (bf16[256,512]{1,0:T(8,128)(2,1)S(1)}, bf16[256,512]{1,0:T(8,128)(2,1)S(1)}, u32[]{:S(2)}, u32[]{:S(2)}) collective-permute-start(bf16[256,512]{1,0:T(8,128)(2,1)S(1)} %collective-permute-done.7.refs_4_), channel_id=1, source_target_pairs={{0,7},{1,0},{2,1},{3,2},{4,3},{5,4},{6,5},{7,6},{8,15},{9,8},{10,9... | collective-permute-start | bytes 786440 | tf_op jit(solution)/shard_map/ppermute | solution.py:387
  33.4 3.9 %collective-permute-start.10 = (bf16[16,1024]{1,0:T(8,128)(2,1)S(1)}, bf16[16,1024]{1,0:T(8,128)(2,1)S(1)}, u32[]{:S(2)}, u32[]{:S(2)}) collective-permute-start(bf16[16,1024]{1,0:T(8,128)(2,1)S(1)} %get-tuple-element.67), channel_id=1, source_target_pairs={{0,64},{8,72},{16,80},{24,88},{32,96},{40,104},{48,112},{56,120},{... | collective-permute-start | bytes 98312 | tf_op jit(solution)/shard_map/ppermute | solution.py:371
  34.7 4.3 %collective-permute-start.12 = (bf16[16,1024]{1,0:T(8,128)(2,1)S(1)}, bf16[16,1024]{1,0:T(8,128)(2,1)S(1)}, u32[]{:S(2)}, u32[]{:S(2)}) collective-permute-start(bf16[16,1024]{1,0:T(8,128)(2,1)S(1)} %get-tuple-element.68), channel_id=1, source_target_pairs={{0,192},{8,200},{16,208},{24,216},{32,224},{40,232},{48,240},{56,2... | collective-permute-start | bytes 98312 | tf_op jit(solution)/shard_map/ppermute | solution.py:371
  36.6 4.3 %collective-permute-start.11 = (bf16[16,1024]{1,0:T(8,128)(2,1)S(1)}, bf16[16,1024]{1,0:T(8,128)(2,1)S(1)}, u32[]{:S(2)}, u32[]{:S(2)}) collective-permute-start(bf16[16,1024]{1,0:T(8,128)(2,1)S(1)} %get-tuple-element.68), channel_id=1, source_target_pairs={{0,128},{8,136},{16,144},{24,152},{32,160},{40,168},{48,176},{56,1... | collective-permute-start | bytes 98312 | tf_op jit(solution)/shard_map/ppermute | solution.py:371
  40.9 9.8 %collective-permute-start.14 = (bf16[128,512]{1,0:T(8,128)(2,1)S(1)}, bf16[128,512]{1,0:T(8,128)(2,1)S(1)}, u32[]{:S(2)}, u32[]{:S(2)}) collective-permute-start(bf16[128,512]{1,0:T(8,128)(2,1)S(1)} %slice.11), channel_id=1, source_target_pairs={{0,7},{1,0},{2,1},{3,2},{4,3},{5,4},{6,5},{7,6},{8,15},{9,8},{10,9... | collective-permute-start | bytes 393224 | tf_op jit(solution)/shard_map/ppermute | solution.py:387
  41.0 9.7 %collective-permute-start.13 = (bf16[128,512]{1,0:T(8,128)(2,1)S(1)}, bf16[128,512]{1,0:T(8,128)(2,1)S(1)}, u32[]{:S(2)}, u32[]{:S(2)}) collective-permute-start(bf16[128,512]{1,0:T(8,128)(2,1)S(1)} %slice.10), channel_id=1, source_target_pairs={{0,1},{1,2},{2,3},{3,4},{4,5},{5,6},{6,7},{7,0},{8,9},{9,10},{10,1... | collective-permute-start | bytes 393224 | tf_op jit(solution)/shard_map/ppermute | solution.py:387
  58.0 12.4 %collective-permute-start.15 = (bf16[32,128,256]{2,1,0:T(8,128)(2,1)}, bf16[32,128,256]{2,1,0:T(8,128)(2,1)}, u32[]{:S(2)}, u32[]{:S(2)}) collective-permute-start(bf16[32,128,256]{2,1,0:T(8,128)(2,1)} %get-tuple-element.84), channel_id=1, source_target_pairs={{0,8},{8,0},{16,24},{24,16},{32,40},{40,32},{48,56},{56,48},{64,72... | collective-permute-start | bytes 6291464 | tf_op jit(solution)/shard_map/ppermute | solution.py:371
  73.6 9.2 %collective-permute-start.16 = (bf16[1152,256]{1,0:T(8,128)(2,1)S(1)}, bf16[1152,256]{1,0:T(8,128)(2,1)S(1)}, u32[]{:S(2)}, u32[]{:S(2)}) collective-permute-start(bf16[1152,256]{1,0:T(8,128)(2,1)S(1)} %get-tuple-element.88), channel_id=1, source_target_pairs={{0,64},{8,24},{16,80},{24,8},{32,96},{40,56},{48,112},{56,40},{64,... | collective-permute-start | bytes 1769480 | tf_op jit(solution)/shard_map/ppermute | solution.py:383
  73.7 16.1 %collective-permute-start.17 = (bf16[1152,256]{1,0:T(8,128)(2,1)S(1)}, bf16[1152,256]{1,0:T(8,128)(2,1)S(1)}, u32[]{:S(2)}, u32[]{:S(2)}) collective-permute-start(bf16[1152,256]{1,0:T(8,128)(2,1)S(1)} %get-tuple-element.89), channel_id=1, source_target_pairs={{0,128},{8,40},{16,144},{24,56},{32,160},{40,8},{48,176},{56,24},{... | collective-permute-start | bytes 1769480 | tf_op jit(solution)/shard_map/ppermute | solution.py:383
  75.9 16.6 %collective-permute-start.18 = (bf16[1152,256]{1,0:T(8,128)(2,1)S(1)}, bf16[1152,256]{1,0:T(8,128)(2,1)S(1)}, u32[]{:S(2)}, u32[]{:S(2)}) collective-permute-start(bf16[1152,256]{1,0:T(8,128)(2,1)S(1)} %get-tuple-element.90), channel_id=1, source_target_pairs={{0,192},{8,56},{16,208},{24,40},{32,224},{40,24},{48,240},{56,8},{... | collective-permute-start | bytes 1769480 | tf_op jit(solution)/shard_map/ppermute | solution.py:383
  93.1 4.9 %collective-permute-start.19 = (bf16[384,256]{1,0:T(8,128)(2,1)S(1)}, bf16[384,256]{1,0:T(8,128)(2,1)S(1)}, u32[]{:S(2)}, u32[]{:S(2)}) collective-permute-start(bf16[384,256]{1,0:T(8,128)(2,1)S(1)} %get-tuple-element.91), channel_id=1, source_target_pairs={{0,16},{8,72},{16,0},{24,88},{32,48},{40,104},{48,32},{56,120},{64... | collective-permute-start | bytes 589832 | tf_op jit(solution)/shard_map/ppermute | solution.py:383
  93.2 7.3 %collective-permute-start.20 = (bf16[384,256]{1,0:T(8,128)(2,1)S(1)}, bf16[384,256]{1,0:T(8,128)(2,1)S(1)}, u32[]{:S(2)}, u32[]{:S(2)}) collective-permute-start(bf16[384,256]{1,0:T(8,128)(2,1)S(1)} %get-tuple-element.92), channel_id=1, source_target_pairs={{0,32},{8,136},{16,48},{24,152},{32,0},{40,168},{48,16},{56,184},{... | collective-permute-start | bytes 589832 | tf_op jit(solution)/shard_map/ppermute | solution.py:383
  95.1 7.6 %collective-permute-start.21 = (bf16[384,256]{1,0:T(8,128)(2,1)S(1)}, bf16[384,256]{1,0:T(8,128)(2,1)S(1)}, u32[]{:S(2)}, u32[]{:S(2)}) collective-permute-start(bf16[384,256]{1,0:T(8,128)(2,1)S(1)} %get-tuple-element.93), channel_id=1, source_target_pairs={{0,48},{8,200},{16,32},{24,216},{32,16},{40,232},{48,0},{56,248},{... | collective-permute-start | bytes 589832 | tf_op jit(solution)/shard_map/ppermute | solution.py:383
  102.8 3.5 %collective-permute-start.22 = (bf16[256,256]{1,0:T(8,128)(2,1)S(1)}, bf16[256,256]{1,0:T(8,128)(2,1)S(1)}, u32[]{:S(2)}, u32[]{:S(2)}) collective-permute-start(bf16[256,256]{1,0:T(8,128)(2,1)S(1)} %get-tuple-element.105), channel_id=1, source_target_pairs={{0,8},{8,0},{16,24},{24,16},{32,40},{40,32},{48,56},{56,48},{64,72... | collective-permute-start | bytes 393224 | tf_op jit(solution)/shard_map/ppermute | solution.py:371
  (23 other events, 291.2 us)
Sparse Core Ops, SparseCore 0:
  50.9 39.5 reduce-scatter.1

commit v3 on v2

--- a/solution.py
+++ b/solution.py
@@ -59,34 +59,32 @@
 
 
 def pool_kernel(keys, values, low, pack, high):
-    for side, src in enumerate((keys, values)):
-        cols = slice(side * WIDTH, (side + 1) * WIDTH)
-        layer = src[...]
-        at = 0
-        rows = ROWS
-        while rows > BLOCK:
-            i, j = grid_of((rows // 2, rows))
-            layer = dot(matrix(j >> 1 == i, 0.5), layer).astype(BF)
-            rows //= 2
-            if rows > BLOCK:
-                low[at : at + rows, cols] = layer
-                at += rows
-        pack[0:BLOCK, cols] = layer
-        i, j = grid_of((BLOCK, BLOCK))
-        halve = matrix(j >> 1 == i, 0.5)
-        total = jnp.zeros((BLOCK, WIDTH), F32)
-        at, rows = 0, BLOCK
-        while rows > 1:
-            layer = dot(halve, layer).astype(BF)
-            rows //= 2
-            total += dot(matrix((i - at == j) & (j < rows)), layer)
+    layer = jnp.concatenate([keys[...], values[...]], axis=1)
+    at = 0
+    rows = ROWS
+    while rows > BLOCK:
+        i, j = grid_of((rows // 2, rows))
+        layer = dot(matrix(j >> 1 == i, 0.5), layer).astype(BF)
+        rows //= 2
+        if rows > BLOCK:
+            low[at : at + rows, :] = layer
             at += rows
-        top = total.astype(BF)
-        pack[BLOCK : 2 * BLOCK, cols] = top
-        high[:, cols] = top
-
-
-def relay_kernel(own, first, x1, x2, x3, out7, out8):
+    pack[0:BLOCK, :] = layer
+    i, j = grid_of((BLOCK, BLOCK))
+    halve = matrix(j >> 1 == i, 0.5)
+    total = jnp.zeros((BLOCK, 2 * WIDTH), F32)
+    at, rows = 0, BLOCK
+    while rows > 1:
+        layer = dot(halve, layer).astype(BF)
+        rows //= 2
+        total += dot(matrix((i - at == j) & (j < rows)), layer)
+        at += rows
+    top = total.astype(BF)
+    pack[BLOCK : 2 * BLOCK, :] = top
+    high[...] = top
+
+
+def relay_kernel(own, first, x1, x3, x2, out7, out8):
     x = jnp.concatenate([own[...], first[BLOCK:, :], x1[...], x2[...], x3[...]], axis=0)
     i, j = grid_of((BLOCK, 8 * BLOCK))
     out7[...] = dot(matrix(j == (i >> 1) * BLOCK + 12 + (i & 1)), x).astype(BF)
@@ -117,7 +115,7 @@
 
 
 def forward_kernel(
-    weight, queries, keys, values, low, r1, x1, x2, x3, s1, s2, s3,
+    weight, queries, keys, values, low, r1, x1, x3, x2, s1, s3, s2,
     attention, prob_out, far, shares_out, held, prob, shares, sems
 ):
     copies = []
@@ -234,7 +232,7 @@
     return total
 
 
-def middle_kernel(fine, kept, keep, a1, a2, a3, keep2, kept2, u1, u2, u3):
+def middle_kernel(fine, kept, keep, a2, a1, a3, keep2, kept2, u1, u2, u3):
     for k, out in enumerate((keep2, u1, u2, u3)):
         out[0:256, :] = sum_rows((keep, a1, a2, a3), slice(k * 256, (k + 1) * 256)).astype(BF)
     core = lax.axis_index("ctx") & 1
@@ -261,7 +259,7 @@
             u[256 + 32 * c : 288 + 32 * c, :] = y[32 * k : 32 * (k + 1)]
 
 
-def last_kernel(top, kept, keep, u1, u2, u3, mine, own, mate):
+def last_kernel(top, kept, keep, u2, u1, u3, mine, own, mate):
     mine[...] = sum_rows((keep, u1, u2, u3), slice(0, 128))
     mate[0:128, :] = sum_rows((keep, u1, u2, u3), slice(128, 256)).astype(BF)
     core = lax.axis_index("ctx") & 1
@@ -413,12 +411,12 @@
     both = jnp.concatenate([high, first[BLOCK:]], axis=0)
     r1, l1, both = together(r1, l1, both)
     r2, l2 = shift(r1, 1), shift(l1, -1)
-    row = [ctx_exchange(both, dx=k) for k in (1, 2, 3)]
+    row = [ctx_exchange(both, dx=k) for k in (1, 3, 2)]
 
     out7, out8 = call(relay_kernel, (pack16,) * 2, high, first, *row)
     r2, l2, out7, out8 = together(r2, l2, out7, out8)
     r3, l3 = shift(r2, 1), shift(l2, -1)
-    column = [ctx_exchange(out7, dy=1), ctx_exchange(out8, dy=2), ctx_exchange(out8, dy=3)]
+    column = [ctx_exchange(out7, dy=1), ctx_exchange(out8, dy=3), ctx_exchange(out8, dy=2)]
 
     r3, l3, *column = together(r3, l3, *column)
     r4, l4 = shift(r3[:HALF], 1), shift(l3[HALF:], -1)
@@ -479,12 +477,12 @@
     keep, kept, *sent = call(
         combine_kernel, (shaped((1024, 256)), small) + (joint,) * 3, near, back, coarse
     )
-    over = [crossing(sent[k - 1], k, 0) for k in (1, 2, 3)]
+    over = [crossing(sent[k - 1], k, 0) for k in (2, 1, 3)]
     joint = shaped((384, 256))
     keep, kept, *sent = call(
         middle_kernel, (shaped((256, 256)), small) + (joint,) * 3, fine, kept, keep, *over
     )
-    over = [crossing(sent[k - 1], k, 1) for k in (1, 2, 3)]
+    over = [crossing(sent[k - 1], k, 1) for k in (2, 1, 3)]
     mixed, *over = together(mixed, *over)
     mine, own, mate = call(
         last_kernel, (shaped((128, 256), F32), pack16, shaped((256, 256))), top, kept, keep, *over

time: 115 us -> 112 us (0.974)
    ppermute x6, waiting for transfers between devices: 20.6 us -> 18.8 us  [crossing(): return lax.ppermute(x, 'ctx', pairs)]
    ppermute x6, starting transfers between devices: 7.88 us -> 6.68 us  [crossing(): return lax.ppermute(x, 'ctx', pairs)]
where the time goes in v3:
time: 112 us
  starting transfers between devices  37 us (33%)
  waiting for transfers between devices  29 us (26%)
  Pallas kernels  27 us (24%)
  between operations  14.3 us (13%)
  local copies, waits for them, and re-layouts  4.38 us (4%)
    ppermute x6, waiting for transfers between devices, crossing(): return lax.ppermute(x, 'ctx', pairs)  18.8 us
    ppermute x9, starting transfers between devices, ctx_exchange(): return lax.ppermute(x, 'ctx', pairs)  16.7 us
    ppermute x8, starting transfers between devices, shift(): return lax.ppermute(x, 'tp', [(i, (i + step) % 8) for i in range(8)])  13.6 us
    pallas_call x7, Pallas kernels, call(): pl.pallas_call(kernel, grid=(1,), out_shape=outs, in_specs=[whole(a) for...  12.2 us
    ppermute x9, waiting for transfers between devices, ctx_exchange(): return lax.ppermute(x, 'ctx', pairs)  9.82 us
    pallas_call x1, Pallas kernels, on_device(): pl.pallas_call(forward_kernel, grid=(1,), out_shape=outs, in_specs=[ANY]...  8.13 us
    ppermute x6, starting transfers between devices, crossing(): return lax.ppermute(x, 'ctx', pairs)  6.68 us
    pallas_call x1, Pallas kernels, on_device(): pl.pallas_call(product_kernel, grid=(1,), out_shape=(parts, parts, tile),...  6.61 us
  transfers between devices with their start and end apart: 24, of which 12 were waited for; matrix products, arithmetic and copies ran while one was open for 0% of the time, Pallas kernels for 23%

profile of v3, /device:TPU:1, one launch (start us, length us, event | category | flops | bytes accessed | tf_op | source)
XLA Modules:
  0.0 111.7 jit_solution(6484568975534812650)
XLA Ops:
  7.2 2.5 %collective-permute-start.1 = (bf16[256,512]{1,0:T(8,128)(2,1)}, bf16[256,512]{1,0:T(8,128)(2,1)S(1)}, u32[]{:S(2)}, u32[]{:S(2)}) collective-permute-start(bf16[256,512]{1,0:T(8,128)(2,1)} %refs_0_.1), channel_id=1, source_target_pairs={{0,1},{1,2},{2,3},{3,4},{4,5},{5,6},{6,7},{7,0},{8,9},{9,10},{10,1... | collective-permute-start | bytes 786440 | tf_op jit(solution)/shard_map/ppermute | solution.py:385
  9.8 4.0 %collective-permute-start.2 = (bf16[256,512]{1,0:T(8,128)(2,1)}, bf16[256,512]{1,0:T(8,128)(2,1)S(1)}, u32[]{:S(2)}, u32[]{:S(2)}) collective-permute-start(bf16[256,512]{1,0:T(8,128)(2,1)} %refs_0_.1), channel_id=1, source_target_pairs={{0,7},{1,0},{2,1},{3,2},{4,3},{5,4},{6,5},{7,6},{8,15},{9,8},{10,9... | collective-permute-start | bytes 786440 | tf_op jit(solution)/shard_map/ppermute | solution.py:385
  15.7 1.2 %shard_map.92 = (bf16[224,1024]{1,0:T(8,128)(2,1)S(1)}, bf16[32,1024]{1,0:T(8,128)(2,1)S(1)}, bf16[16,1024]{1,0:T(8,128)(2,1)S(1)}) custom-call(bf16[256,512]{1,0:T(8,128)(2,1)S(1)} %copy-done, bf16[256,512]{1,0:T(8,128)(2,1)S(1)} %copy-done.1), custom_call_target="tpu_custom_call" | custom-call | bytes 7400000 | tf_op jit(solution)/shard_map/pallas_call | solution.py:46
  20.0 2.7 %collective-permute-start.7 = (bf16[256,512]{1,0:T(8,128)(2,1)S(1)}, bf16[256,512]{1,0:T(8,128)(2,1)S(1)}, u32[]{:S(2)}, u32[]{:S(2)}) collective-permute-start(bf16[256,512]{1,0:T(8,128)(2,1)S(1)} %collective-permute-done.2.refs_2_), channel_id=1, source_target_pairs={{0,7},{1,0},{2,1},{3,2},{4,3},{5,4},{6,5},{7,6},{8,15},{9,8},{10,9... | collective-permute-start | bytes 786440 | tf_op jit(solution)/shard_map/ppermute | solution.py:385
  22.7 2.7 %collective-permute-start.5 = (bf16[32,1024]{1,0:T(8,128)(2,1)S(1)}, bf16[32,1024]{1,0:T(8,128)(2,1)S(1)}, u32[]{:S(2)}, u32[]{:S(2)}) collective-permute-start(bf16[32,1024]{1,0:T(8,128)(2,1)S(1)} %pad_maximum_fusion), channel_id=1, source_target_pairs={{0,32},{8,40},{16,48},{24,56},{32,0},{40,8},{48,16},{56,24},{64,96... | collective-permute-start | bytes 196616 | tf_op jit(solution)/shard_map/ppermute | solution.py:369
  27.3 2.9 %collective-permute-done.4.x3 = bf16[32,1024]{1,0:T(8,128)(2,1)S(1)} collective-permute-done((bf16[32,1024]{1,0:T(8,128)(2,1)S(1)}, bf16[32,1024]{1,0:T(8,128)(2,1)S(1)}, u32[]{:S(2)}, u32[]{:S(2)}) %collective-permute-start.4) | collective-permute-done | bytes 65568 | tf_op jit(solution)/shard_map/ppermute | solution.py:369
  30.6 2.7 %collective-permute-start.9 = (bf16[256,512]{1,0:T(8,128)(2,1)S(1)}, bf16[256,512]{1,0:T(8,128)(2,1)S(1)}, u32[]{:S(2)}, u32[]{:S(2)}) collective-permute-start(bf16[256,512]{1,0:T(8,128)(2,1)S(1)} %collective-permute-done.7.refs_4_), channel_id=1, source_target_pairs={{0,7},{1,0},{2,1},{3,2},{4,3},{5,4},{6,5},{7,6},{8,15},{9,8},{10,9... | collective-permute-start | bytes 786440 | tf_op jit(solution)/shard_map/ppermute | solution.py:385
  33.2 1.3 %collective-permute-start.10 = (bf16[16,1024]{1,0:T(8,128)(2,1)S(1)}, bf16[16,1024]{1,0:T(8,128)(2,1)S(1)}, u32[]{:S(2)}, u32[]{:S(2)}) collective-permute-start(bf16[16,1024]{1,0:T(8,128)(2,1)S(1)} %get-tuple-element.67), channel_id=1, source_target_pairs={{0,64},{8,72},{16,80},{24,88},{32,96},{40,104},{48,112},{56,120},{... | collective-permute-start | bytes 98312 | tf_op jit(solution)/shard_map/ppermute | solution.py:369
  34.5 2.6 %collective-permute-start.12 = (bf16[16,1024]{1,0:T(8,128)(2,1)S(1)}, bf16[16,1024]{1,0:T(8,128)(2,1)S(1)}, u32[]{:S(2)}, u32[]{:S(2)}) collective-permute-start(bf16[16,1024]{1,0:T(8,128)(2,1)S(1)} %get-tuple-element.68), channel_id=1, source_target_pairs={{0,128},{8,136},{16,144},{24,152},{32,160},{40,168},{48,176},{56,1... | collective-permute-start | bytes 98312 | tf_op jit(solution)/shard_map/ppermute | solution.py:369
  37.2 1.6 %collective-permute-done.12.s2 = bf16[16,1024]{1,0:T(8,128)(2,1)S(1)} collective-permute-done((bf16[16,1024]{1,0:T(8,128)(2,1)S(1)}, bf16[16,1024]{1,0:T(8,128)(2,1)S(1)}, u32[]{:S(2)}, u32[]{:S(2)}) %collective-permute-start.12) | collective-permute-done | bytes 32800 | tf_op jit(solution)/shard_map/ppermute | solution.py:369
  38.8 2.3 %collective-permute-done.11.s3 = bf16[16,1024]{1,0:T(8,128)(2,1)S(1)} collective-permute-done((bf16[16,1024]{1,0:T(8,128)(2,1)S(1)}, bf16[16,1024]{1,0:T(8,128)(2,1)S(1)}, u32[]{:S(2)}, u32[]{:S(2)}) %collective-permute-start.11) | collective-permute-done | bytes 32800 | tf_op jit(solution)/shard_map/ppermute | solution.py:369
  42.8 8.1 %shard_map.94 = (bf16[256,512]{1,0:T(8,128)(2,1)}, f32[8,336,128]{2,1,0:T(8,128)}, bf16[96,1024]{1,0:T(8,128)(2,1)}, bf16[8,256,512]{2,1,0:T(8,128)(2,1)}) custom-call(bf16[4096,512]{1,0:T(8,128)(2,1)} %refs_10_.1, bf16[256,512]{1,0:T(8,128)(2,1)} %queries.3, bf16[256,512]{1,0:T(8,128)(2,1)} %keys.5, bf16[256,512]{1,0:T(8,128)(2,1)} %values.5, ...), custom_call_target="tpu_custom_call" | custom-call | bytes 29600000 | tf_op jit(solution)/shard_map/pallas_call | solution.py:425
  51.7 6.6 %shard_map.95 = (bf16[32,128,256]{2,1,0:T(8,128)(2,1)}, bf16[32,128,256]{2,1,0:T(8,128)(2,1)}, bf16[256,512]{1,0:T(8,128)(2,1)}) custom-call(bf16[256,512]{1,0:T(8,128)(2,1)} %refs_0_.1, bf16[256,512]{1,0:T(8,128)(2,1)} %copy-done.14, bf16[256,512]{1,0:T(8,128)(2,1)} %copy-done.15, bf16[256,512]{1,0:T(8,128)(2,1)} %copy-done.16, ...), custom_call_target="tpu_custom_call" | custom-call | tf_op jit(solution)/shard_map/pallas_call | solution.py:445
  58.3 5.6 %collective-permute-start.15 = (bf16[32,128,256]{2,1,0:T(8,128)(2,1)}, bf16[32,128,256]{2,1,0:T(8,128)(2,1)}, u32[]{:S(2)}, u32[]{:S(2)}) collective-permute-start(bf16[32,128,256]{2,1,0:T(8,128)(2,1)} %get-tuple-element.84), channel_id=1, source_target_pairs={{0,8},{8,0},{16,24},{24,16},{32,40},{40,32},{48,56},{56,48},{64,72... | collective-permute-start | bytes 6291464 | tf_op jit(solution)/shard_map/ppermute | solution.py:369
  63.9 6.9 %shard_map.96 = (bf16[256,512]{1,0:T(8,128)(2,1)}, f32[256,1024]{1,0:T(8,128)}, bf16[32,1024]{1,0:T(8,128)(2,1)}, bf16[16,1024]{1,0:T(8,128)(2,1)}, bf16[512,256]{1,0:T(8,128)(2,1)}) custom-call(bf16[256,512]{1,0:T(8,128)(2,1)} %queries.3, bf16[256,512]{1,0:T(8,128)(2,1)} %keys.5, bf16[256,512]{1,0:T(8,128)(2,1)} %values.5, bf16[224,1024]{1,0:T(8,128)(2,1)} %copy-done.3, ...), custom_call_target="tpu_custom_call" | custom-call | tf_op jit(solution)/shard_map/pallas_call | solution.py:46
  71.8 2.1 %shard_map.97 = (bf16[1024,256]{1,0:T(8,128)(2,1)S(1)}, bf16[128,256]{1,0:T(8,128)(2,1)S(1)}, bf16[1152,256]{1,0:T(8,128)(2,1)S(1)}, bf16[1152,256]{1,0:T(8,128)(2,1)S(1)}, bf16[1152,256]{1,0:T(8,128)(2,1)S(1)}) custom-call(bf16[32,128,256]{2,1,0:T(8,128)(2,1)S(1)} %copy-done.2, bf16[32,128,256]{2,1,0:T(8,128)(2,1)} %collective-permute-done.15.back, ...), custom_call_target="tpu_custom_call" | custom-call | bytes 1110000 | tf_op jit(solution)/shard_map/pallas_call | solution.py:46
  73.9 1.3 %collective-permute-start.16 = (bf16[1152,256]{1,0:T(8,128)(2,1)S(1)}, bf16[1152,256]{1,0:T(8,128)(2,1)S(1)}, u32[]{:S(2)}, u32[]{:S(2)}) collective-permute-start(bf16[1152,256]{1,0:T(8,128)(2,1)S(1)} %get-tuple-element.88), channel_id=1, source_target_pairs={{0,128},{8,40},{16,144},{24,56},{32,160},{40,8},{48,176},{56,24},{... | collective-permute-start | bytes 1769480 | tf_op jit(solution)/shard_map/ppermute | solution.py:381
  75.2 1.3 %collective-permute-start.17 = (bf16[1152,256]{1,0:T(8,128)(2,1)S(1)}, bf16[1152,256]{1,0:T(8,128)(2,1)S(1)}, u32[]{:S(2)}, u32[]{:S(2)}) collective-permute-start(bf16[1152,256]{1,0:T(8,128)(2,1)S(1)} %get-tuple-element.89), channel_id=1, source_target_pairs={{0,64},{8,24},{16,80},{24,8},{32,96},{40,56},{48,112},{56,40},{64,... | collective-permute-start | bytes 1769480 | tf_op jit(solution)/shard_map/ppermute | solution.py:381
  77.3 7.3 %collective-permute-done.16.a2 = bf16[1152,256]{1,0:T(8,128)(2,1)S(1)} collective-permute-done((bf16[1152,256]{1,0:T(8,128)(2,1)S(1)}, bf16[1152,256]{1,0:T(8,128)(2,1)S(1)}, u32[]{:S(2)}, u32[]{:S(2)}) %collective-permute-start.16) | collective-permute-done | bytes 589856 | tf_op jit(solution)/shard_map/ppermute | solution.py:381
  84.6 5.9 %collective-permute-done.17.a1 = bf16[1152,256]{1,0:T(8,128)(2,1)S(1)} collective-permute-done((bf16[1152,256]{1,0:T(8,128)(2,1)S(1)}, bf16[1152,256]{1,0:T(8,128)(2,1)S(1)}, u32[]{:S(2)}, u32[]{:S(2)}) %collective-permute-start.17) | collective-permute-done | bytes 589856 | tf_op jit(solution)/shard_map/ppermute | solution.py:381
  92.2 2.6 %collective-permute-start.21 = (bf16[384,256]{1,0:T(8,128)(2,1)S(1)}, bf16[384,256]{1,0:T(8,128)(2,1)S(1)}, u32[]{:S(2)}, u32[]{:S(2)}) collective-permute-start(bf16[384,256]{1,0:T(8,128)(2,1)S(1)} %get-tuple-element.93), channel_id=1, source_target_pairs={{0,48},{8,200},{16,32},{24,216},{32,16},{40,232},{48,0},{56,248},{... | collective-permute-start | bytes 589832 | tf_op jit(solution)/shard_map/ppermute | solution.py:381
  94.8 3.1 %collective-permute-done.19.u2 = bf16[384,256]{1,0:T(8,128)(2,1)S(1)} collective-permute-done((bf16[384,256]{1,0:T(8,128)(2,1)S(1)}, bf16[384,256]{1,0:T(8,128)(2,1)S(1)}, u32[]{:S(2)}, u32[]{:S(2)}) %collective-permute-start.19) | collective-permute-done | bytes 196640 | tf_op jit(solution)/shard_map/ppermute | solution.py:381
  97.9 2.1 %collective-permute-done.21.u3 = bf16[384,256]{1,0:T(8,128)(2,1)S(1)} collective-permute-done((bf16[384,256]{1,0:T(8,128)(2,1)S(1)}, bf16[384,256]{1,0:T(8,128)(2,1)S(1)}, u32[]{:S(2)}, u32[]{:S(2)}) %collective-permute-start.21) | collective-permute-done | bytes 196640 | tf_op jit(solution)/shard_map/ppermute | solution.py:381
  100.2 2.6 %collective-permute-start.22 = (bf16[256,256]{1,0:T(8,128)(2,1)S(1)}, bf16[256,256]{1,0:T(8,128)(2,1)S(1)}, u32[]{:S(2)}, u32[]{:S(2)}) collective-permute-start(bf16[256,256]{1,0:T(8,128)(2,1)S(1)} %get-tuple-element.105), channel_id=1, source_target_pairs={{0,8},{8,0},{16,24},{24,16},{32,40},{40,32},{48,56},{56,48},{64,72... | collective-permute-start | bytes 393224 | tf_op jit(solution)/shard_map/ppermute | solution.py:369
  (84 shorter events, 15.1 us)
Async XLA Ops:
  7.2 92.8 %reduce-scatter.2.cloned.1.call-start = ((), (), s32[]{:S(2)}) async-start(), calls=%async_computation.1 | async-start | bytes 2359296 | tf_op jit(solution)/shard_map/reduce_scatter | solution.py:441
  7.2 12.7 %collective-permute-start.1 = (bf16[256,512]{1,0:T(8,128)(2,1)}, bf16[256,512]{1,0:T(8,128)(2,1)S(1)}, u32[]{:S(2)}, u32[]{:S(2)}) collective-permute-start(bf16[256,512]{1,0:T(8,128)(2,1)} %refs_0_.1), channel_id=1, source_target_pairs={{0,1},{1,2},{2,3},{3,4},{4,5},{5,6},{6,7},{7,0},{8,9},{9,10},{10,1... | collective-permute-start | bytes 786440 | tf_op jit(solution)/shard_map/ppermute | solution.py:385
  9.8 10.2 %collective-permute-start.2 = (bf16[256,512]{1,0:T(8,128)(2,1)}, bf16[256,512]{1,0:T(8,128)(2,1)S(1)}, u32[]{:S(2)}, u32[]{:S(2)}) collective-permute-start(bf16[256,512]{1,0:T(8,128)(2,1)} %refs_0_.1), channel_id=1, source_target_pairs={{0,7},{1,0},{2,1},{3,2},{4,3},{5,4},{6,5},{7,6},{8,15},{9,8},{10,9... | collective-permute-start | bytes 786440 | tf_op jit(solution)/shard_map/ppermute | solution.py:385
  17.7 1.9 %collective-permute-start = (bf16[32,1024]{1,0:T(8,128)(2,1)S(1)}, bf16[32,1024]{1,0:T(8,128)(2,1)S(1)}, u32[]{:S(2)}, u32[]{:S(2)}) collective-permute-start(bf16[32,1024]{1,0:T(8,128)(2,1)S(1)} %get-tuple-element.58), channel_id=1, source_target_pairs={{0,8},{8,0},{16,24},{24,16},{32,40},{40,32},{48,56},{56,48},{64,72... | collective-permute-start | bytes 196616 | tf_op jit(solution)/shard_map/ppermute | solution.py:369
  19.9 10.5 %collective-permute-start.6 = (bf16[256,512]{1,0:T(8,128)(2,1)S(1)}, bf16[256,512]{1,0:T(8,128)(2,1)S(1)}, u32[]{:S(2)}, u32[]{:S(2)}) collective-permute-start(bf16[256,512]{1,0:T(8,128)(2,1)S(1)} %collective-permute-done.1.refs_1_), channel_id=1, source_target_pairs={{0,1},{1,2},{2,3},{3,4},{4,5},{5,6},{6,7},{7,0},{8,9},{9,10},{10,1... | collective-permute-start | bytes 786440 | tf_op jit(solution)/shard_map/ppermute | solution.py:385
  20.0 10.4 %collective-permute-start.7 = (bf16[256,512]{1,0:T(8,128)(2,1)S(1)}, bf16[256,512]{1,0:T(8,128)(2,1)S(1)}, u32[]{:S(2)}, u32[]{:S(2)}) collective-permute-start(bf16[256,512]{1,0:T(8,128)(2,1)S(1)} %collective-permute-done.2.refs_2_), channel_id=1, source_target_pairs={{0,7},{1,0},{2,1},{3,2},{4,3},{5,4},{6,5},{7,6},{8,15},{9,8},{10,9... | collective-permute-start | bytes 786440 | tf_op jit(solution)/shard_map/ppermute | solution.py:385
  22.7 4.6 %collective-permute-start.5 = (bf16[32,1024]{1,0:T(8,128)(2,1)S(1)}, bf16[32,1024]{1,0:T(8,128)(2,1)S(1)}, u32[]{:S(2)}, u32[]{:S(2)}) collective-permute-start(bf16[32,1024]{1,0:T(8,128)(2,1)S(1)} %pad_maximum_fusion), channel_id=1, source_target_pairs={{0,32},{8,40},{16,48},{24,56},{32,0},{40,8},{48,16},{56,24},{64,96... | collective-permute-start | bytes 196616 | tf_op jit(solution)/shard_map/ppermute | solution.py:369
  25.4 4.8 %collective-permute-start.4 = (bf16[32,1024]{1,0:T(8,128)(2,1)S(1)}, bf16[32,1024]{1,0:T(8,128)(2,1)S(1)}, u32[]{:S(2)}, u32[]{:S(2)}) collective-permute-start(bf16[32,1024]{1,0:T(8,128)(2,1)S(1)} %pad_maximum_fusion), channel_id=1, source_target_pairs={{0,48},{8,56},{16,32},{24,40},{32,16},{40,24},{48,0},{56,8},{64,11... | collective-permute-start | bytes 196616 | tf_op jit(solution)/shard_map/ppermute | solution.py:369
  26.3 4.0 %collective-permute-start.3 = (bf16[32,1024]{1,0:T(8,128)(2,1)S(1)}, bf16[32,1024]{1,0:T(8,128)(2,1)S(1)}, u32[]{:S(2)}, u32[]{:S(2)}) collective-permute-start(bf16[32,1024]{1,0:T(8,128)(2,1)S(1)} %pad_maximum_fusion), channel_id=1, source_target_pairs={{0,16},{8,24},{16,0},{24,8},{32,48},{40,56},{48,32},{56,40},{64,80... | collective-permute-start | bytes 196616 | tf_op jit(solution)/shard_map/ppermute | solution.py:369
  30.5 10.7 %collective-permute-start.8 = (bf16[256,512]{1,0:T(8,128)(2,1)S(1)}, bf16[256,512]{1,0:T(8,128)(2,1)S(1)}, u32[]{:S(2)}, u32[]{:S(2)}) collective-permute-start(bf16[256,512]{1,0:T(8,128)(2,1)S(1)} %collective-permute-done.6.refs_3_), channel_id=1, source_target_pairs={{0,1},{1,2},{2,3},{3,4},{4,5},{5,6},{6,7},{7,0},{8,9},{9,10},{10,1... | collective-permute-start | bytes 786440 | tf_op jit(solution)/shard_map/ppermute | solution.py:385
  30.6 10.6 %collective-permute-start.9 = (bf16[256,512]{1,0:T(8,128)(2,1)S(1)}, bf16[256,512]{1,0:T(8,128)(2,1)S(1)}, u32[]{:S(2)}, u32[]{:S(2)}) collective-permute-start(bf16[256,512]{1,0:T(8,128)(2,1)S(1)} %collective-permute-done.7.refs_4_), channel_id=1, source_target_pairs={{0,7},{1,0},{2,1},{3,2},{4,3},{5,4},{6,5},{7,6},{8,15},{9,8},{10,9... | collective-permute-start | bytes 786440 | tf_op jit(solution)/shard_map/ppermute | solution.py:385
  33.2 3.9 %collective-permute-start.10 = (bf16[16,1024]{1,0:T(8,128)(2,1)S(1)}, bf16[16,1024]{1,0:T(8,128)(2,1)S(1)}, u32[]{:S(2)}, u32[]{:S(2)}) collective-permute-start(bf16[16,1024]{1,0:T(8,128)(2,1)S(1)} %get-tuple-element.67), channel_id=1, source_target_pairs={{0,64},{8,72},{16,80},{24,88},{32,96},{40,104},{48,112},{56,120},{... | collective-permute-start | bytes 98312 | tf_op jit(solution)/shard_map/ppermute | solution.py:369
  34.5 4.3 %collective-permute-start.12 = (bf16[16,1024]{1,0:T(8,128)(2,1)S(1)}, bf16[16,1024]{1,0:T(8,128)(2,1)S(1)}, u32[]{:S(2)}, u32[]{:S(2)}) collective-permute-start(bf16[16,1024]{1,0:T(8,128)(2,1)S(1)} %get-tuple-element.68), channel_id=1, source_target_pairs={{0,128},{8,136},{16,144},{24,152},{32,160},{40,168},{48,176},{56,1... | collective-permute-start | bytes 98312 | tf_op jit(solution)/shard_map/ppermute | solution.py:369
  37.2 4.0 %collective-permute-start.11 = (bf16[16,1024]{1,0:T(8,128)(2,1)S(1)}, bf16[16,1024]{1,0:T(8,128)(2,1)S(1)}, u32[]{:S(2)}, u32[]{:S(2)}) collective-permute-start(bf16[16,1024]{1,0:T(8,128)(2,1)S(1)} %get-tuple-element.68), channel_id=1, source_target_pairs={{0,192},{8,200},{16,208},{24,216},{32,224},{40,232},{48,240},{56,2... | collective-permute-start | bytes 98312 | tf_op jit(solution)/shard_map/ppermute | solution.py:369
  41.2 9.8 %collective-permute-start.14 = (bf16[128,512]{1,0:T(8,128)(2,1)S(1)}, bf16[128,512]{1,0:T(8,128)(2,1)S(1)}, u32[]{:S(2)}, u32[]{:S(2)}) collective-permute-start(bf16[128,512]{1,0:T(8,128)(2,1)S(1)} %slice.11), channel_id=1, source_target_pairs={{0,7},{1,0},{2,1},{3,2},{4,3},{5,4},{6,5},{7,6},{8,15},{9,8},{10,9... | collective-permute-start | bytes 393224 | tf_op jit(solution)/shard_map/ppermute | solution.py:385
  42.0 9.0 %collective-permute-start.13 = (bf16[128,512]{1,0:T(8,128)(2,1)S(1)}, bf16[128,512]{1,0:T(8,128)(2,1)S(1)}, u32[]{:S(2)}, u32[]{:S(2)}) collective-permute-start(bf16[128,512]{1,0:T(8,128)(2,1)S(1)} %slice.10), channel_id=1, source_target_pairs={{0,1},{1,2},{2,3},{3,4},{4,5},{5,6},{6,7},{7,0},{8,9},{9,10},{10,1... | collective-permute-start | bytes 393224 | tf_op jit(solution)/shard_map/ppermute | solution.py:385
  58.3 12.5 %collective-permute-start.15 = (bf16[32,128,256]{2,1,0:T(8,128)(2,1)}, bf16[32,128,256]{2,1,0:T(8,128)(2,1)}, u32[]{:S(2)}, u32[]{:S(2)}) collective-permute-start(bf16[32,128,256]{2,1,0:T(8,128)(2,1)} %get-tuple-element.84), channel_id=1, source_target_pairs={{0,8},{8,0},{16,24},{24,16},{32,40},{40,32},{48,56},{56,48},{64,72... | collective-permute-start | bytes 6291464 | tf_op jit(solution)/shard_map/ppermute | solution.py:369
  73.9 10.7 %collective-permute-start.16 = (bf16[1152,256]{1,0:T(8,128)(2,1)S(1)}, bf16[1152,256]{1,0:T(8,128)(2,1)S(1)}, u32[]{:S(2)}, u32[]{:S(2)}) collective-permute-start(bf16[1152,256]{1,0:T(8,128)(2,1)S(1)} %get-tuple-element.88), channel_id=1, source_target_pairs={{0,128},{8,40},{16,144},{24,56},{32,160},{40,8},{48,176},{56,24},{... | collective-permute-start | bytes 1769480 | tf_op jit(solution)/shard_map/ppermute | solution.py:381
  75.2 15.3 %collective-permute-start.17 = (bf16[1152,256]{1,0:T(8,128)(2,1)S(1)}, bf16[1152,256]{1,0:T(8,128)(2,1)S(1)}, u32[]{:S(2)}, u32[]{:S(2)}) collective-permute-start(bf16[1152,256]{1,0:T(8,128)(2,1)S(1)} %get-tuple-element.89), channel_id=1, source_target_pairs={{0,64},{8,24},{16,80},{24,8},{32,96},{40,56},{48,112},{56,40},{64,... | collective-permute-start | bytes 1769480 | tf_op jit(solution)/shard_map/ppermute | solution.py:381
  76.5 14.4 %collective-permute-start.18 = (bf16[1152,256]{1,0:T(8,128)(2,1)S(1)}, bf16[1152,256]{1,0:T(8,128)(2,1)S(1)}, u32[]{:S(2)}, u32[]{:S(2)}) collective-permute-start(bf16[1152,256]{1,0:T(8,128)(2,1)S(1)} %get-tuple-element.90), channel_id=1, source_target_pairs={{0,192},{8,56},{16,208},{24,40},{32,224},{40,24},{48,240},{56,8},{... | collective-permute-start | bytes 1769480 | tf_op jit(solution)/shard_map/ppermute | solution.py:381
  91.5 6.4 %collective-permute-start.19 = (bf16[384,256]{1,0:T(8,128)(2,1)S(1)}, bf16[384,256]{1,0:T(8,128)(2,1)S(1)}, u32[]{:S(2)}, u32[]{:S(2)}) collective-permute-start(bf16[384,256]{1,0:T(8,128)(2,1)S(1)} %get-tuple-element.91), channel_id=1, source_target_pairs={{0,32},{8,136},{16,48},{24,152},{32,0},{40,168},{48,16},{56,184},{... | collective-permute-start | bytes 589832 | tf_op jit(solution)/shard_map/ppermute | solution.py:381
  91.7 6.3 %collective-permute-start.20 = (bf16[384,256]{1,0:T(8,128)(2,1)S(1)}, bf16[384,256]{1,0:T(8,128)(2,1)S(1)}, u32[]{:S(2)}, u32[]{:S(2)}) collective-permute-start(bf16[384,256]{1,0:T(8,128)(2,1)S(1)} %get-tuple-element.92), channel_id=1, source_target_pairs={{0,16},{8,72},{16,0},{24,88},{32,48},{40,104},{48,32},{56,120},{64... | collective-permute-start | bytes 589832 | tf_op jit(solution)/shard_map/ppermute | solution.py:381
  92.2 7.8 %collective-permute-start.21 = (bf16[384,256]{1,0:T(8,128)(2,1)S(1)}, bf16[384,256]{1,0:T(8,128)(2,1)S(1)}, u32[]{:S(2)}, u32[]{:S(2)}) collective-permute-start(bf16[384,256]{1,0:T(8,128)(2,1)S(1)} %get-tuple-element.93), channel_id=1, source_target_pairs={{0,48},{8,200},{16,32},{24,216},{32,16},{40,232},{48,0},{56,248},{... | collective-permute-start | bytes 589832 | tf_op jit(solution)/shard_map/ppermute | solution.py:381
  100.2 3.6 %collective-permute-start.22 = (bf16[256,256]{1,0:T(8,128)(2,1)S(1)}, bf16[256,256]{1,0:T(8,128)(2,1)S(1)}, u32[]{:S(2)}, u32[]{:S(2)}) collective-permute-start(bf16[256,256]{1,0:T(8,128)(2,1)S(1)} %get-tuple-element.105), channel_id=1, source_target_pairs={{0,8},{8,0},{16,24},{24,16},{32,40},{40,32},{48,56},{56,48},{64,72... | collective-permute-start | bytes 393224 | tf_op jit(solution)/shard_map/ppermute | solution.py:369
  (23 other events, 289.8 us)
Sparse Core Ops, SparseCore 0:
  51.2 39.3 reduce-scatter.1

commit v4 on v3

--- a/solution.py
+++ b/solution.py
@@ -215,14 +215,20 @@
             first[row : row + 32, at % 256 : at % 256 + HEAD_DIM] = got[32 * n : 32 * (n + 1)]
 
 
-def combine_kernel(near, back, coarse, keep, kept, a1, a2, a3):
+def combine_kernel(near, back, coarse, keep, kept, a1, a2, a3, sems):
+    copies = [pltpu.make_async_copy(coarse.at[0:128, :], kept, sems.at[0])]
+    for k, out in ((1, a1), (2, a2), (3, a3)):
+        copies.append(
+            pltpu.make_async_copy(coarse.at[128 * k : 128 * (k + 1), :], out.at[1024:1152, :], sems.at[k])
+        )
+    for c in copies:
+        c.start()
     for k, out in enumerate((keep, a1, a2, a3)):
         for n in range(8):
             total = near[8 * k + n].astype(F32) + back[8 * k + n].astype(F32)
             out[n * 128 : (n + 1) * 128, :] = total.astype(BF)
-    kept[...] = coarse[0:128, :]
-    for k, out in ((1, a1), (2, a2), (3, a3)):
-        out[1024:1152, :] = coarse[128 * k : 128 * (k + 1), :]
+    for c in copies:
+        c.wait()
 
 
 def sum_rows(refs, rows):
@@ -474,9 +480,17 @@
     )
 
     small, joint = shaped((128, 256)), shaped((1152, 256))
-    keep, kept, *sent = call(
-        combine_kernel, (shaped((1024, 256)), small) + (joint,) * 3, near, back, coarse
-    )
+    outs = (shaped((1024, 256)), small) + (joint,) * 3
+    keep, kept, *sent = pl.pallas_call(
+        combine_kernel,
+        grid=(1,),
+        out_shape=outs,
+        in_specs=[whole(near), whole(back), ANY],
+        out_specs=tuple(whole(x) for x in outs),
+        scratch_shapes=[pltpu.SemaphoreType.DMA((4,))],
+        compiler_params=SMALL,
+        cost_estimate=cost(0.3),
+    )(near, back, coarse)
     over = [crossing(sent[k - 1], k, 0) for k in (2, 1, 3)]
     joint = shaped((384, 256))
     keep, kept, *sent = call(

time: 112 us -> 112 us (level)
    pallas_call x0 -> x1, Pallas kernels: none -> 2.46 us  [on_device(): pl.pallas_call(combine_kernel, grid=(1,), out_shape=outs, in_specs=[whole...]
    pallas_call x7 -> x6, Pallas kernels: 12.2 us -> 10.1 us  [call(): pl.pallas_call(kernel, grid=(1,), out_shape=outs, in_specs=[whole(a) for...]
where the time goes in v4:
time: 112 us
  starting transfers between devices  36.9 us (33%)
  waiting for transfers between devices  29.1 us (26%)
  Pallas kernels  27.3 us (24%)
  between operations  14.3 us (13%)
  local copies, waits for them, and re-layouts  4.38 us (4%)
    ppermute x6, waiting for transfers between devices, crossing(): return lax.ppermute(x, 'ctx', pairs)  18.9 us
    ppermute x9, starting transfers between devices, ctx_exchange(): return lax.ppermute(x, 'ctx', pairs)  16.6 us
    ppermute x8, starting transfers between devices, shift(): return lax.ppermute(x, 'tp', [(i, (i + step) % 8) for i in range(8)])  13.6 us
    pallas_call x6, Pallas kernels, call(): pl.pallas_call(kernel, grid=(1,), out_shape=outs, in_specs=[whole(a) for...  10.1 us
    ppermute x9, waiting for transfers between devices, ctx_exchange(): return lax.ppermute(x, 'ctx', pairs)  9.82 us
    pallas_call x1, Pallas kernels, on_device(): pl.pallas_call(forward_kernel, grid=(1,), out_shape=outs, in_specs=[ANY]...  8.13 us
    ppermute x6, starting transfers between devices, crossing(): return lax.ppermute(x, 'ctx', pairs)  6.67 us
    pallas_call x1, Pallas kernels, on_device(): pl.pallas_call(product_kernel, grid=(1,), out_shape=(parts, parts, tile),...  6.61 us
  transfers between devices with their start and end apart: 24, of which 12 were waited for; matrix products, arithmetic and copies ran while one was open for 0% of the time, Pallas kernels for 23%

profile of v4, /device:TPU:1, one launch (start us, length us, event | category | flops | bytes accessed | tf_op | source)
XLA Modules:
  0.0 112.0 jit_solution(14255891532362392468)
XLA Ops:
  7.2 2.5 %collective-permute-start.1 = (bf16[256,512]{1,0:T(8,128)(2,1)}, bf16[256,512]{1,0:T(8,128)(2,1)S(1)}, u32[]{:S(2)}, u32[]{:S(2)}) collective-permute-start(bf16[256,512]{1,0:T(8,128)(2,1)} %refs_0_.1), channel_id=1, source_target_pairs={{0,1},{1,2},{2,3},{3,4},{4,5},{5,6},{6,7},{7,0},{8,9},{9,10},{10,1... | collective-permute-start | bytes 786440 | tf_op jit(solution)/shard_map/ppermute | solution.py:391
  9.8 4.0 %collective-permute-start.2 = (bf16[256,512]{1,0:T(8,128)(2,1)}, bf16[256,512]{1,0:T(8,128)(2,1)S(1)}, u32[]{:S(2)}, u32[]{:S(2)}) collective-permute-start(bf16[256,512]{1,0:T(8,128)(2,1)} %refs_0_.1), channel_id=1, source_target_pairs={{0,7},{1,0},{2,1},{3,2},{4,3},{5,4},{6,5},{7,6},{8,15},{9,8},{10,9... | collective-permute-start | bytes 786440 | tf_op jit(solution)/shard_map/ppermute | solution.py:391
  15.7 1.2 %shard_map.92 = (bf16[224,1024]{1,0:T(8,128)(2,1)S(1)}, bf16[32,1024]{1,0:T(8,128)(2,1)S(1)}, bf16[16,1024]{1,0:T(8,128)(2,1)S(1)}) custom-call(bf16[256,512]{1,0:T(8,128)(2,1)S(1)} %copy-done, bf16[256,512]{1,0:T(8,128)(2,1)S(1)} %copy-done.1), custom_call_target="tpu_custom_call" | custom-call | bytes 7400000 | tf_op jit(solution)/shard_map/pallas_call | solution.py:46
  20.0 2.7 %collective-permute-start.7 = (bf16[256,512]{1,0:T(8,128)(2,1)S(1)}, bf16[256,512]{1,0:T(8,128)(2,1)S(1)}, u32[]{:S(2)}, u32[]{:S(2)}) collective-permute-start(bf16[256,512]{1,0:T(8,128)(2,1)S(1)} %collective-permute-done.2.refs_2_), channel_id=1, source_target_pairs={{0,7},{1,0},{2,1},{3,2},{4,3},{5,4},{6,5},{7,6},{8,15},{9,8},{10,9... | collective-permute-start | bytes 786440 | tf_op jit(solution)/shard_map/ppermute | solution.py:391
  22.7 2.7 %collective-permute-start.5 = (bf16[32,1024]{1,0:T(8,128)(2,1)S(1)}, bf16[32,1024]{1,0:T(8,128)(2,1)S(1)}, u32[]{:S(2)}, u32[]{:S(2)}) collective-permute-start(bf16[32,1024]{1,0:T(8,128)(2,1)S(1)} %pad_maximum_fusion), channel_id=1, source_target_pairs={{0,32},{8,40},{16,48},{24,56},{32,0},{40,8},{48,16},{56,24},{64,96... | collective-permute-start | bytes 196616 | tf_op jit(solution)/shard_map/ppermute | solution.py:375
  27.3 2.9 %collective-permute-done.4.x3 = bf16[32,1024]{1,0:T(8,128)(2,1)S(1)} collective-permute-done((bf16[32,1024]{1,0:T(8,128)(2,1)S(1)}, bf16[32,1024]{1,0:T(8,128)(2,1)S(1)}, u32[]{:S(2)}, u32[]{:S(2)}) %collective-permute-start.4) | collective-permute-done | bytes 65568 | tf_op jit(solution)/shard_map/ppermute | solution.py:375
  30.6 2.7 %collective-permute-start.9 = (bf16[256,512]{1,0:T(8,128)(2,1)S(1)}, bf16[256,512]{1,0:T(8,128)(2,1)S(1)}, u32[]{:S(2)}, u32[]{:S(2)}) collective-permute-start(bf16[256,512]{1,0:T(8,128)(2,1)S(1)} %collective-permute-done.7.refs_4_), channel_id=1, source_target_pairs={{0,7},{1,0},{2,1},{3,2},{4,3},{5,4},{6,5},{7,6},{8,15},{9,8},{10,9... | collective-permute-start | bytes 786440 | tf_op jit(solution)/shard_map/ppermute | solution.py:391
  33.2 1.3 %collective-permute-start.10 = (bf16[16,1024]{1,0:T(8,128)(2,1)S(1)}, bf16[16,1024]{1,0:T(8,128)(2,1)S(1)}, u32[]{:S(2)}, u32[]{:S(2)}) collective-permute-start(bf16[16,1024]{1,0:T(8,128)(2,1)S(1)} %get-tuple-element.67), channel_id=1, source_target_pairs={{0,64},{8,72},{16,80},{24,88},{32,96},{40,104},{48,112},{56,120},{... | collective-permute-start | bytes 98312 | tf_op jit(solution)/shard_map/ppermute | solution.py:375
  34.5 2.6 %collective-permute-start.12 = (bf16[16,1024]{1,0:T(8,128)(2,1)S(1)}, bf16[16,1024]{1,0:T(8,128)(2,1)S(1)}, u32[]{:S(2)}, u32[]{:S(2)}) collective-permute-start(bf16[16,1024]{1,0:T(8,128)(2,1)S(1)} %get-tuple-element.68), channel_id=1, source_target_pairs={{0,128},{8,136},{16,144},{24,152},{32,160},{40,168},{48,176},{56,1... | collective-permute-start | bytes 98312 | tf_op jit(solution)/shard_map/ppermute | solution.py:375
  37.2 1.6 %collective-permute-done.12.s2 = bf16[16,1024]{1,0:T(8,128)(2,1)S(1)} collective-permute-done((bf16[16,1024]{1,0:T(8,128)(2,1)S(1)}, bf16[16,1024]{1,0:T(8,128)(2,1)S(1)}, u32[]{:S(2)}, u32[]{:S(2)}) %collective-permute-start.12) | collective-permute-done | bytes 32800 | tf_op jit(solution)/shard_map/ppermute | solution.py:375
  38.8 2.3 %collective-permute-done.11.s3 = bf16[16,1024]{1,0:T(8,128)(2,1)S(1)} collective-permute-done((bf16[16,1024]{1,0:T(8,128)(2,1)S(1)}, bf16[16,1024]{1,0:T(8,128)(2,1)S(1)}, u32[]{:S(2)}, u32[]{:S(2)}) %collective-permute-start.11) | collective-permute-done | bytes 32800 | tf_op jit(solution)/shard_map/ppermute | solution.py:375
  42.8 8.1 %shard_map.94 = (bf16[256,512]{1,0:T(8,128)(2,1)}, f32[8,336,128]{2,1,0:T(8,128)}, bf16[96,1024]{1,0:T(8,128)(2,1)}, bf16[8,256,512]{2,1,0:T(8,128)(2,1)}) custom-call(bf16[4096,512]{1,0:T(8,128)(2,1)} %refs_10_.1, bf16[256,512]{1,0:T(8,128)(2,1)} %queries.3, bf16[256,512]{1,0:T(8,128)(2,1)} %keys.5, bf16[256,512]{1,0:T(8,128)(2,1)} %values.5, ...), custom_call_target="tpu_custom_call" | custom-call | bytes 29600000 | tf_op jit(solution)/shard_map/pallas_call | solution.py:431
  51.7 6.6 %shard_map.95 = (bf16[32,128,256]{2,1,0:T(8,128)(2,1)}, bf16[32,128,256]{2,1,0:T(8,128)(2,1)}, bf16[256,512]{1,0:T(8,128)(2,1)}) custom-call(bf16[256,512]{1,0:T(8,128)(2,1)} %refs_0_.1, bf16[256,512]{1,0:T(8,128)(2,1)} %copy-done.14, bf16[256,512]{1,0:T(8,128)(2,1)} %copy-done.15, bf16[256,512]{1,0:T(8,128)(2,1)} %copy-done.16, ...), custom_call_target="tpu_custom_call" | custom-call | tf_op jit(solution)/shard_map/pallas_call | solution.py:451
  58.3 5.6 %collective-permute-start.15 = (bf16[32,128,256]{2,1,0:T(8,128)(2,1)}, bf16[32,128,256]{2,1,0:T(8,128)(2,1)}, u32[]{:S(2)}, u32[]{:S(2)}) collective-permute-start(bf16[32,128,256]{2,1,0:T(8,128)(2,1)} %get-tuple-element.84), channel_id=1, source_target_pairs={{0,8},{8,0},{16,24},{24,16},{32,40},{40,32},{48,56},{56,48},{64,72... | collective-permute-start | bytes 6291464 | tf_op jit(solution)/shard_map/ppermute | solution.py:375
  63.9 6.9 %shard_map.96 = (bf16[256,512]{1,0:T(8,128)(2,1)}, f32[256,1024]{1,0:T(8,128)}, bf16[32,1024]{1,0:T(8,128)(2,1)}, bf16[16,1024]{1,0:T(8,128)(2,1)}, bf16[512,256]{1,0:T(8,128)(2,1)}) custom-call(bf16[256,512]{1,0:T(8,128)(2,1)} %queries.3, bf16[256,512]{1,0:T(8,128)(2,1)} %keys.5, bf16[256,512]{1,0:T(8,128)(2,1)} %values.5, bf16[224,1024]{1,0:T(8,128)(2,1)} %copy-done.3, ...), custom_call_target="tpu_custom_call" | custom-call | tf_op jit(solution)/shard_map/pallas_call | solution.py:46
  71.8 2.5 %shard_map.97 = (bf16[1024,256]{1,0:T(8,128)(2,1)S(1)}, bf16[128,256]{1,0:T(8,128)(2,1)S(1)}, bf16[1152,256]{1,0:T(8,128)(2,1)S(1)}, bf16[1152,256]{1,0:T(8,128)(2,1)S(1)}, bf16[1152,256]{1,0:T(8,128)(2,1)S(1)}) custom-call(bf16[32,128,256]{2,1,0:T(8,128)(2,1)S(1)} %copy-done.2, bf16[32,128,256]{2,1,0:T(8,128)(2,1)} %collective-permute-done.15.back, ...), custom_call_target="tpu_custom_call" | custom-call | bytes 1110000 | tf_op jit(solution)/shard_map/pallas_call | solution.py:484
  74.3 1.3 %collective-permute-start.16 = (bf16[1152,256]{1,0:T(8,128)(2,1)S(1)}, bf16[1152,256]{1,0:T(8,128)(2,1)S(1)}, u32[]{:S(2)}, u32[]{:S(2)}) collective-permute-start(bf16[1152,256]{1,0:T(8,128)(2,1)S(1)} %get-tuple-element.88), channel_id=1, source_target_pairs={{0,128},{8,40},{16,144},{24,56},{32,160},{40,8},{48,176},{56,24},{... | collective-permute-start | bytes 1769480 | tf_op jit(solution)/shard_map/ppermute | solution.py:387
  75.6 1.3 %collective-permute-start.17 = (bf16[1152,256]{1,0:T(8,128)(2,1)S(1)}, bf16[1152,256]{1,0:T(8,128)(2,1)S(1)}, u32[]{:S(2)}, u32[]{:S(2)}) collective-permute-start(bf16[1152,256]{1,0:T(8,128)(2,1)S(1)} %get-tuple-element.89), channel_id=1, source_target_pairs={{0,64},{8,24},{16,80},{24,8},{32,96},{40,56},{48,112},{56,40},{64,... | collective-permute-start | bytes 1769480 | tf_op jit(solution)/shard_map/ppermute | solution.py:387
  77.6 7.3 %collective-permute-done.16.a2 = bf16[1152,256]{1,0:T(8,128)(2,1)S(1)} collective-permute-done((bf16[1152,256]{1,0:T(8,128)(2,1)S(1)}, bf16[1152,256]{1,0:T(8,128)(2,1)S(1)}, u32[]{:S(2)}, u32[]{:S(2)}) %collective-permute-start.16) | collective-permute-done | bytes 589856 | tf_op jit(solution)/shard_map/ppermute | solution.py:387
  84.9 5.9 %collective-permute-done.17.a1 = bf16[1152,256]{1,0:T(8,128)(2,1)S(1)} collective-permute-done((bf16[1152,256]{1,0:T(8,128)(2,1)S(1)}, bf16[1152,256]{1,0:T(8,128)(2,1)S(1)}, u32[]{:S(2)}, u32[]{:S(2)}) %collective-permute-start.17) | collective-permute-done | bytes 589856 | tf_op jit(solution)/shard_map/ppermute | solution.py:387
  92.5 2.8 %collective-permute-start.21 = (bf16[384,256]{1,0:T(8,128)(2,1)S(1)}, bf16[384,256]{1,0:T(8,128)(2,1)S(1)}, u32[]{:S(2)}, u32[]{:S(2)}) collective-permute-start(bf16[384,256]{1,0:T(8,128)(2,1)S(1)} %get-tuple-element.93), channel_id=1, source_target_pairs={{0,48},{8,200},{16,32},{24,216},{32,16},{40,232},{48,0},{56,248},{... | collective-permute-start | bytes 589832 | tf_op jit(solution)/shard_map/ppermute | solution.py:387
  95.3 3.1 %collective-permute-done.19.u2 = bf16[384,256]{1,0:T(8,128)(2,1)S(1)} collective-permute-done((bf16[384,256]{1,0:T(8,128)(2,1)S(1)}, bf16[384,256]{1,0:T(8,128)(2,1)S(1)}, u32[]{:S(2)}, u32[]{:S(2)}) %collective-permute-start.19) | collective-permute-done | bytes 196640 | tf_op jit(solution)/shard_map/ppermute | solution.py:387
  98.4 2.1 %collective-permute-done.21.u3 = bf16[384,256]{1,0:T(8,128)(2,1)S(1)} collective-permute-done((bf16[384,256]{1,0:T(8,128)(2,1)S(1)}, bf16[384,256]{1,0:T(8,128)(2,1)S(1)}, u32[]{:S(2)}, u32[]{:S(2)}) %collective-permute-start.21) | collective-permute-done | bytes 196640 | tf_op jit(solution)/shard_map/ppermute | solution.py:387
  100.6 2.5 %collective-permute-start.22 = (bf16[256,256]{1,0:T(8,128)(2,1)S(1)}, bf16[256,256]{1,0:T(8,128)(2,1)S(1)}, u32[]{:S(2)}, u32[]{:S(2)}) collective-permute-start(bf16[256,256]{1,0:T(8,128)(2,1)S(1)} %get-tuple-element.105), channel_id=1, source_target_pairs={{0,8},{8,0},{16,24},{24,16},{32,40},{40,32},{48,56},{56,48},{64,72... | collective-permute-start | bytes 393224 | tf_op jit(solution)/shard_map/ppermute | solution.py:375
  (84 shorter events, 15.1 us)
Async XLA Ops:
  7.2 93.3 %reduce-scatter.2.cloned.1.call-start = ((), (), s32[]{:S(2)}) async-start(), calls=%async_computation.1 | async-start | bytes 2359296 | tf_op jit(solution)/shard_map/reduce_scatter | solution.py:447
  7.2 12.7 %collective-permute-start.1 = (bf16[256,512]{1,0:T(8,128)(2,1)}, bf16[256,512]{1,0:T(8,128)(2,1)S(1)}, u32[]{:S(2)}, u32[]{:S(2)}) collective-permute-start(bf16[256,512]{1,0:T(8,128)(2,1)} %refs_0_.1), channel_id=1, source_target_pairs={{0,1},{1,2},{2,3},{3,4},{4,5},{5,6},{6,7},{7,0},{8,9},{9,10},{10,1... | collective-permute-start | bytes 786440 | tf_op jit(solution)/shard_map/ppermute | solution.py:391
  9.8 10.2 %collective-permute-start.2 = (bf16[256,512]{1,0:T(8,128)(2,1)}, bf16[256,512]{1,0:T(8,128)(2,1)S(1)}, u32[]{:S(2)}, u32[]{:S(2)}) collective-permute-start(bf16[256,512]{1,0:T(8,128)(2,1)} %refs_0_.1), channel_id=1, source_target_pairs={{0,7},{1,0},{2,1},{3,2},{4,3},{5,4},{6,5},{7,6},{8,15},{9,8},{10,9... | collective-permute-start | bytes 786440 | tf_op jit(solution)/shard_map/ppermute | solution.py:391
  17.7 1.9 %collective-permute-start = (bf16[32,1024]{1,0:T(8,128)(2,1)S(1)}, bf16[32,1024]{1,0:T(8,128)(2,1)S(1)}, u32[]{:S(2)}, u32[]{:S(2)}) collective-permute-start(bf16[32,1024]{1,0:T(8,128)(2,1)S(1)} %get-tuple-element.58), channel_id=1, source_target_pairs={{0,8},{8,0},{16,24},{24,16},{32,40},{40,32},{48,56},{56,48},{64,72... | collective-permute-start | bytes 196616 | tf_op jit(solution)/shard_map/ppermute | solution.py:375
  19.9 10.5 %collective-permute-start.6 = (bf16[256,512]{1,0:T(8,128)(2,1)S(1)}, bf16[256,512]{1,0:T(8,128)(2,1)S(1)}, u32[]{:S(2)}, u32[]{:S(2)}) collective-permute-start(bf16[256,512]{1,0:T(8,128)(2,1)S(1)} %collective-permute-done.1.refs_1_), channel_id=1, source_target_pairs={{0,1},{1,2},{2,3},{3,4},{4,5},{5,6},{6,7},{7,0},{8,9},{9,10},{10,1... | collective-permute-start | bytes 786440 | tf_op jit(solution)/shard_map/ppermute | solution.py:391
  20.0 10.4 %collective-permute-start.7 = (bf16[256,512]{1,0:T(8,128)(2,1)S(1)}, bf16[256,512]{1,0:T(8,128)(2,1)S(1)}, u32[]{:S(2)}, u32[]{:S(2)}) collective-permute-start(bf16[256,512]{1,0:T(8,128)(2,1)S(1)} %collective-permute-done.2.refs_2_), channel_id=1, source_target_pairs={{0,7},{1,0},{2,1},{3,2},{4,3},{5,4},{6,5},{7,6},{8,15},{9,8},{10,9... | collective-permute-start | bytes 786440 | tf_op jit(solution)/shard_map/ppermute | solution.py:391
  22.7 4.6 %collective-permute-start.5 = (bf16[32,1024]{1,0:T(8,128)(2,1)S(1)}, bf16[32,1024]{1,0:T(8,128)(2,1)S(1)}, u32[]{:S(2)}, u32[]{:S(2)}) collective-permute-start(bf16[32,1024]{1,0:T(8,128)(2,1)S(1)} %pad_maximum_fusion), channel_id=1, source_target_pairs={{0,32},{8,40},{16,48},{24,56},{32,0},{40,8},{48,16},{56,24},{64,96... | collective-permute-start | bytes 196616 | tf_op jit(solution)/shard_map/ppermute | solution.py:375
  25.4 4.8 %collective-permute-start.4 = (bf16[32,1024]{1,0:T(8,128)(2,1)S(1)}, bf16[32,1024]{1,0:T(8,128)(2,1)S(1)}, u32[]{:S(2)}, u32[]{:S(2)}) collective-permute-start(bf16[32,1024]{1,0:T(8,128)(2,1)S(1)} %pad_maximum_fusion), channel_id=1, source_target_pairs={{0,48},{8,56},{16,32},{24,40},{32,16},{40,24},{48,0},{56,8},{64,11... | collective-permute-start | bytes 196616 | tf_op jit(solution)/shard_map/ppermute | solution.py:375
  26.3 4.0 %collective-permute-start.3 = (bf16[32,1024]{1,0:T(8,128)(2,1)S(1)}, bf16[32,1024]{1,0:T(8,128)(2,1)S(1)}, u32[]{:S(2)}, u32[]{:S(2)}) collective-permute-start(bf16[32,1024]{1,0:T(8,128)(2,1)S(1)} %pad_maximum_fusion), channel_id=1, source_target_pairs={{0,16},{8,24},{16,0},{24,8},{32,48},{40,56},{48,32},{56,40},{64,80... | collective-permute-start | bytes 196616 | tf_op jit(solution)/shard_map/ppermute | solution.py:375
  30.5 10.7 %collective-permute-start.8 = (bf16[256,512]{1,0:T(8,128)(2,1)S(1)}, bf16[256,512]{1,0:T(8,128)(2,1)S(1)}, u32[]{:S(2)}, u32[]{:S(2)}) collective-permute-start(bf16[256,512]{1,0:T(8,128)(2,1)S(1)} %collective-permute-done.6.refs_3_), channel_id=1, source_target_pairs={{0,1},{1,2},{2,3},{3,4},{4,5},{5,6},{6,7},{7,0},{8,9},{9,10},{10,1... | collective-permute-start | bytes 786440 | tf_op jit(solution)/shard_map/ppermute | solution.py:391
  30.6 10.6 %collective-permute-start.9 = (bf16[256,512]{1,0:T(8,128)(2,1)S(1)}, bf16[256,512]{1,0:T(8,128)(2,1)S(1)}, u32[]{:S(2)}, u32[]{:S(2)}) collective-permute-start(bf16[256,512]{1,0:T(8,128)(2,1)S(1)} %collective-permute-done.7.refs_4_), channel_id=1, source_target_pairs={{0,7},{1,0},{2,1},{3,2},{4,3},{5,4},{6,5},{7,6},{8,15},{9,8},{10,9... | collective-permute-start | bytes 786440 | tf_op jit(solution)/shard_map/ppermute | solution.py:391
  33.2 3.9 %collective-permute-start.10 = (bf16[16,1024]{1,0:T(8,128)(2,1)S(1)}, bf16[16,1024]{1,0:T(8,128)(2,1)S(1)}, u32[]{:S(2)}, u32[]{:S(2)}) collective-permute-start(bf16[16,1024]{1,0:T(8,128)(2,1)S(1)} %get-tuple-element.67), channel_id=1, source_target_pairs={{0,64},{8,72},{16,80},{24,88},{32,96},{40,104},{48,112},{56,120},{... | collective-permute-start | bytes 98312 | tf_op jit(solution)/shard_map/ppermute | solution.py:375
  34.5 4.3 %collective-permute-start.12 = (bf16[16,1024]{1,0:T(8,128)(2,1)S(1)}, bf16[16,1024]{1,0:T(8,128)(2,1)S(1)}, u32[]{:S(2)}, u32[]{:S(2)}) collective-permute-start(bf16[16,1024]{1,0:T(8,128)(2,1)S(1)} %get-tuple-element.68), channel_id=1, source_target_pairs={{0,128},{8,136},{16,144},{24,152},{32,160},{40,168},{48,176},{56,1... | collective-permute-start | bytes 98312 | tf_op jit(solution)/shard_map/ppermute | solution.py:375
  37.2 4.0 %collective-permute-start.11 = (bf16[16,1024]{1,0:T(8,128)(2,1)S(1)}, bf16[16,1024]{1,0:T(8,128)(2,1)S(1)}, u32[]{:S(2)}, u32[]{:S(2)}) collective-permute-start(bf16[16,1024]{1,0:T(8,128)(2,1)S(1)} %get-tuple-element.68), channel_id=1, source_target_pairs={{0,192},{8,200},{16,208},{24,216},{32,224},{40,232},{48,240},{56,2... | collective-permute-start | bytes 98312 | tf_op jit(solution)/shard_map/ppermute | solution.py:375
  41.2 9.8 %collective-permute-start.14 = (bf16[128,512]{1,0:T(8,128)(2,1)S(1)}, bf16[128,512]{1,0:T(8,128)(2,1)S(1)}, u32[]{:S(2)}, u32[]{:S(2)}) collective-permute-start(bf16[128,512]{1,0:T(8,128)(2,1)S(1)} %slice.11), channel_id=1, source_target_pairs={{0,7},{1,0},{2,1},{3,2},{4,3},{5,4},{6,5},{7,6},{8,15},{9,8},{10,9... | collective-permute-start | bytes 393224 | tf_op jit(solution)/shard_map/ppermute | solution.py:391
  42.0 9.0 %collective-permute-start.13 = (bf16[128,512]{1,0:T(8,128)(2,1)S(1)}, bf16[128,512]{1,0:T(8,128)(2,1)S(1)}, u32[]{:S(2)}, u32[]{:S(2)}) collective-permute-start(bf16[128,512]{1,0:T(8,128)(2,1)S(1)} %slice.10), channel_id=1, source_target_pairs={{0,1},{1,2},{2,3},{3,4},{4,5},{5,6},{6,7},{7,0},{8,9},{9,10},{10,1... | collective-permute-start | bytes 393224 | tf_op jit(solution)/shard_map/ppermute | solution.py:391
  58.3 12.5 %collective-permute-start.15 = (bf16[32,128,256]{2,1,0:T(8,128)(2,1)}, bf16[32,128,256]{2,1,0:T(8,128)(2,1)}, u32[]{:S(2)}, u32[]{:S(2)}) collective-permute-start(bf16[32,128,256]{2,1,0:T(8,128)(2,1)} %get-tuple-element.84), channel_id=1, source_target_pairs={{0,8},{8,0},{16,24},{24,16},{32,40},{40,32},{48,56},{56,48},{64,72... | collective-permute-start | bytes 6291464 | tf_op jit(solution)/shard_map/ppermute | solution.py:375
  74.3 10.7 %collective-permute-start.16 = (bf16[1152,256]{1,0:T(8,128)(2,1)S(1)}, bf16[1152,256]{1,0:T(8,128)(2,1)S(1)}, u32[]{:S(2)}, u32[]{:S(2)}) collective-permute-start(bf16[1152,256]{1,0:T(8,128)(2,1)S(1)} %get-tuple-element.88), channel_id=1, source_target_pairs={{0,128},{8,40},{16,144},{24,56},{32,160},{40,8},{48,176},{56,24},{... | collective-permute-start | bytes 1769480 | tf_op jit(solution)/shard_map/ppermute | solution.py:387
  75.6 15.3 %collective-permute-start.17 = (bf16[1152,256]{1,0:T(8,128)(2,1)S(1)}, bf16[1152,256]{1,0:T(8,128)(2,1)S(1)}, u32[]{:S(2)}, u32[]{:S(2)}) collective-permute-start(bf16[1152,256]{1,0:T(8,128)(2,1)S(1)} %get-tuple-element.89), channel_id=1, source_target_pairs={{0,64},{8,24},{16,80},{24,8},{32,96},{40,56},{48,112},{56,40},{64,... | collective-permute-start | bytes 1769480 | tf_op jit(solution)/shard_map/ppermute | solution.py:387
  76.8 14.5 %collective-permute-start.18 = (bf16[1152,256]{1,0:T(8,128)(2,1)S(1)}, bf16[1152,256]{1,0:T(8,128)(2,1)S(1)}, u32[]{:S(2)}, u32[]{:S(2)}) collective-permute-start(bf16[1152,256]{1,0:T(8,128)(2,1)S(1)} %get-tuple-element.90), channel_id=1, source_target_pairs={{0,192},{8,56},{16,208},{24,40},{32,224},{40,24},{48,240},{56,8},{... | collective-permute-start | bytes 1769480 | tf_op jit(solution)/shard_map/ppermute | solution.py:387
  91.9 6.4 %collective-permute-start.19 = (bf16[384,256]{1,0:T(8,128)(2,1)S(1)}, bf16[384,256]{1,0:T(8,128)(2,1)S(1)}, u32[]{:S(2)}, u32[]{:S(2)}) collective-permute-start(bf16[384,256]{1,0:T(8,128)(2,1)S(1)} %get-tuple-element.91), channel_id=1, source_target_pairs={{0,32},{8,136},{16,48},{24,152},{32,0},{40,168},{48,16},{56,184},{... | collective-permute-start | bytes 589832 | tf_op jit(solution)/shard_map/ppermute | solution.py:387
  92.0 6.3 %collective-permute-start.20 = (bf16[384,256]{1,0:T(8,128)(2,1)S(1)}, bf16[384,256]{1,0:T(8,128)(2,1)S(1)}, u32[]{:S(2)}, u32[]{:S(2)}) collective-permute-start(bf16[384,256]{1,0:T(8,128)(2,1)S(1)} %get-tuple-element.92), channel_id=1, source_target_pairs={{0,16},{8,72},{16,0},{24,88},{32,48},{40,104},{48,32},{56,120},{64... | collective-permute-start | bytes 589832 | tf_op jit(solution)/shard_map/ppermute | solution.py:387
  92.5 7.9 %collective-permute-start.21 = (bf16[384,256]{1,0:T(8,128)(2,1)S(1)}, bf16[384,256]{1,0:T(8,128)(2,1)S(1)}, u32[]{:S(2)}, u32[]{:S(2)}) collective-permute-start(bf16[384,256]{1,0:T(8,128)(2,1)S(1)} %get-tuple-element.93), channel_id=1, source_target_pairs={{0,48},{8,200},{16,32},{24,216},{32,16},{40,232},{48,0},{56,248},{... | collective-permute-start | bytes 589832 | tf_op jit(solution)/shard_map/ppermute | solution.py:387
  100.6 3.5 %collective-permute-start.22 = (bf16[256,256]{1,0:T(8,128)(2,1)S(1)}, bf16[256,256]{1,0:T(8,128)(2,1)S(1)}, u32[]{:S(2)}, u32[]{:S(2)}) collective-permute-start(bf16[256,256]{1,0:T(8,128)(2,1)S(1)} %get-tuple-element.105), channel_id=1, source_target_pairs={{0,8},{8,0},{16,24},{24,16},{32,40},{40,32},{48,56},{56,48},{64,72... | collective-permute-start | bytes 393224 | tf_op jit(solution)/shard_map/ppermute | solution.py:375
  (23 other events, 290.3 us)
Sparse Core Ops, SparseCore 0:
  51.2 39.3 reduce-scatter.1
